TPU v7x, 32 devices: a whole 2x2x4 slice. The times are simulated.
32 devices in a mesh: dev: 32 (over z, y, x, core).
Axes of the slice: x: 2, y: 2, z: 4, core: 2. Of those that a mesh axis runs over, the one named last changes fastest.
Arguments:
- cells_in: bfloat16 [12288, 1024], P('dev'), may hold values from -6 to 6
- lengths: int32 [64], replicated, may hold values from 1 to 383, as said below
- sets_weights: float32 [12582912], P('dev')
- rows_weights: float32 [49152], P('dev')
- norm_gains: float32 [2176], P('dev'), may hold values from 0.5 to 1.5
- sets_first: float32 [12582912], P('dev')
- rows_first: float32 [49152], P('dev')
- gains_first: float32 [2176], P('dev')
- sets_second: float32 [12582912], P('dev')
- rows_second: float32 [49152], P('dev')
- gains_second: float32 [2176], P('dev')
- out_grad: bfloat16 [11520, 1024], P('dev'), may hold values from -6 to 6
Outputs:
- rows_out: bfloat16 [11520, 1024], P('dev')
- cells_grad: float32 [12288, 1024], P('dev')
- sets_grad: float32 [12582912], P('dev')
- rows_grad: float32 [49152], P('dev')
- gains_grad: float32 [2176], P('dev')
- sets_new: float32 [12582912], P('dev')
- rows_new: float32 [49152], P('dev')
- gains_new: float32 [2176], P('dev')
- sets_first_new: float32 [12582912], P('dev')
- rows_first_new: float32 [49152], P('dev')
- gains_first_new: float32 [2176], P('dev')
- sets_second_new: float32 [12582912], P('dev')
- rows_second_new: float32 [49152], P('dev')
- gains_second_new: float32 [2176], P('dev')
- sets_low: bfloat16 [12582912], P('dev')
- rows_low: bfloat16 [49152], P('dev')
- gains_low: bfloat16 [2176], P('dev')
Inputs may be any that keep to these rules, and one draw needn't show every extreme that they name: Each device's 2 lengths sum to a multiple of 32 that is at most 384, and some device's to exactly 384; all lengths together sum to 11520.
All inputs are finite; a program needn't handle non-finite values.
Results may differ from a plain program's by a relative error of at most 0.024.
Values may be sent and summed in bfloat16 or wider, within the bound.
No kernel may reach another device: no remote copies, remote signals or barrier semaphores. Data moves between devices by JAX's collectives and lax.ppermute only.
A program may use at most 320 MiB of HBM per device.

v0:
```python
import jax
import jax.numpy as jnp
from jax import lax
from jax.sharding import PartitionSpec as P

ATTRS = 16
HEADS = 8
SETS_DEV = 2
STEP = 5
ROWS_EVEN = 360


norm_eps = 1e-05
beta_one = 0.5
beta_two = 0.5
adam_eps = 1e-08
decay_rate = 0.1
gain_rate = 0.5


def forward_mul(left, right):
    return jnp.dot(left, right, preferred_element_type=jnp.float32)


def outer(left, right):
    return lax.dot_general(
        left, right, (((0,), (0,)), ((), ())), preferred_element_type=jnp.float32
    )


def backmul(upstream, weight):
    return lax.dot_general(
        upstream, weight, (((1,), (1,)), ((), ())), preferred_element_type=jnp.float32
    )


def norm_gain(inputs, gain_vec):
    center = inputs - jnp.mean(inputs, axis=-1, keepdims=True)
    spread = jnp.mean(center * center, axis=-1, keepdims=True)
    return center * lax.rsqrt(spread + norm_eps) * gain_vec


def norm_back(inputs, gain_vec, upstream):
    unused, pull = jax.vjp(norm_gain, inputs, gain_vec)
    return pull(upstream)


def exact_gelu(inputs):
    return jax.nn.gelu(inputs, approximate=False)


def split_block(flat, feature):
    cut_one = 3 * feature * feature
    cut_two = cut_one + feature * feature
    cut_three = cut_two + 4 * feature * feature
    return (
        flat[:cut_one].reshape(feature, 3 * feature),
        flat[cut_one:cut_two].reshape(feature, feature),
        flat[cut_two:cut_three].reshape(feature, 4 * feature),
        flat[cut_three:].reshape(4 * feature, feature),
    )


def split_gains(flat, model_width, feature):
    return (
        flat[:model_width],
        flat[model_width : 2 * model_width],
        flat[2 * model_width : 2 * model_width + feature],
        flat[2 * model_width + feature :],
    )


def unpack(full_sets, full_rows, full_gains, model_width, feature):
    gain_list = [
        piece.astype(jnp.float32) for piece in split_gains(full_gains, model_width, feature)
    ]
    return (split_block(full_sets, model_width), split_block(full_rows, feature), gain_list)


def block_rates(position, feature, out_fan):
    cut_one = 3 * feature * feature
    cut_two = cut_one + feature * feature
    cut_three = cut_two + 4 * feature * feature
    fans = (feature, out_fan, feature, 4 * feature)
    rates = [0.5 * fan ** (-0.5) for fan in fans]
    return jnp.where(
        position < cut_one,
        rates[0],
        jnp.where(
            position < cut_two, rates[1], jnp.where(position < cut_three, rates[2], rates[3])
        ),
    ).astype(jnp.float32)


def adam_update(weight, gradient, first, second, rates, decay):
    first_new = beta_one * first + (1.0 - beta_one) * gradient
    second_new = beta_two * second + (1.0 - beta_two) * gradient * gradient
    corrected = first_new / (1.0 - beta_one**STEP)
    scaled = second_new / (1.0 - beta_two**STEP)
    weight_new = weight - rates * (corrected / (jnp.sqrt(scaled) + adam_eps) + decay * weight)
    return (weight_new, first_new, second_new)


def query_block(slots):
    pieces = max(1, slots // 512)
    while slots % pieces:
        pieces -= 1
    return slots // pieces


def mlp_forward(inputs, gain_vec, w_up, w_down):
    normed = norm_gain(inputs, gain_vec).astype(jnp.bfloat16)
    hidden = exact_gelu(forward_mul(normed, w_up)).astype(jnp.bfloat16)
    return inputs + forward_mul(hidden, w_down)


def mlp_backward(inputs, gain_vec, w_up, w_down, upstream):
    normed = norm_gain(inputs, gain_vec).astype(jnp.bfloat16)
    before = forward_mul(normed, w_up)
    active, pull = jax.vjp(exact_gelu, before)
    hidden = active.astype(jnp.bfloat16)
    grad_low = upstream.astype(jnp.bfloat16)
    grad_hidden = backmul(grad_low, w_down)
    grad_before = pull(grad_hidden)[0].astype(jnp.bfloat16)
    grad_inputs, grad_gain = norm_back(inputs, gain_vec, backmul(grad_before, w_up))
    return (upstream + grad_inputs, grad_gain, outer(normed, grad_before), outer(hidden, grad_low))


def sets_forward(inputs, gain_vec, w_qkv, w_out, labels):
    slots, feature = inputs.shape
    head_size = feature // HEADS
    scaling = head_size ** (-0.5)
    normed = norm_gain(inputs, gain_vec).astype(jnp.bfloat16)
    joined = forward_mul(normed, w_qkv).astype(jnp.bfloat16).reshape(slots, 3, HEADS, head_size)
    queries, key_rows, values = (joined[:, 0], joined[:, 1], joined[:, 2])
    block = query_block(slots)
    related = labels[0:block, None] == labels[None, :]
    scores = (
        jnp.einsum("qhd,khd->hqk", queries, key_rows, preferred_element_type=jnp.float32) * scaling
    )
    scores = jnp.where(related[None], scores, -jnp.inf)
    peak = jnp.max(scores, axis=-1, keepdims=True)
    weights = jnp.exp(scores - peak)
    summed = jnp.sum(weights, axis=-1, keepdims=True)
    chance = (weights / summed).astype(jnp.bfloat16)
    pieces = jnp.einsum("hqk,khd->qhd", chance, values, preferred_element_type=jnp.float32).astype(
        jnp.bfloat16
    )
    log_sums = peak + jnp.log(summed)
    blended = pieces.reshape(slots, feature)
    return (inputs + forward_mul(blended, w_out), (joined, blended, log_sums))


def sets_backward(inputs, gain_vec, w_qkv, w_out, labels, kept_parts, upstream):
    joined, blended, log_total = kept_parts
    slots, feature = inputs.shape
    head_size = feature // HEADS
    scaling = head_size ** (-0.5)
    queries, key_rows, values = (joined[:, 0], joined[:, 1], joined[:, 2])
    grad_low = upstream.astype(jnp.bfloat16)
    grad_blended = backmul(grad_low, w_out).astype(jnp.bfloat16).reshape(slots, HEADS, head_size)
    grad_out = outer(blended, grad_low)
    block = query_block(slots)
    related = labels[0:block, None] == labels[None, :]
    scores = (
        jnp.einsum("qhd,khd->hqk", queries, key_rows, preferred_element_type=jnp.float32) * scaling
    )
    scores = jnp.where(related[None], scores, -jnp.inf)
    chance = jnp.exp(scores - log_total)
    grad_chance = jnp.einsum(
        "qhd,khd->hqk", grad_blended, values, preferred_element_type=jnp.float32
    )
    row_dot = jnp.sum(chance * grad_chance, axis=-1, keepdims=True)
    grad_scores = (chance * (grad_chance - row_dot)).astype(jnp.bfloat16)
    query_grads = (
        jnp.einsum("hqk,khd->qhd", grad_scores, key_rows, preferred_element_type=jnp.float32)
        * scaling
    )
    grad_keys = (
        jnp.einsum("hqk,qhd->khd", grad_scores, queries, preferred_element_type=jnp.float32)
        * scaling
    )
    grad_values = jnp.einsum(
        "hqk,qhd->khd",
        chance.astype(jnp.bfloat16),
        grad_blended,
        preferred_element_type=jnp.float32,
    )
    grad_joined = jnp.stack([query_grads, grad_keys, grad_values], axis=1)
    grad_joined = grad_joined.reshape(slots, 3 * feature).astype(jnp.bfloat16)
    normed = norm_gain(inputs, gain_vec).astype(jnp.bfloat16)
    grad_inputs, grad_gain = norm_back(inputs, gain_vec, backmul(grad_joined, w_qkv))
    return (upstream + grad_inputs, grad_gain, outer(normed, grad_joined), grad_out)


def rows_attention(cells, gain_vec, w_qkv):
    row_count, attributes, feature = cells.shape
    head_size = feature // HEADS
    normed = norm_gain(cells, gain_vec).astype(jnp.bfloat16).reshape(-1, feature)
    joined = (
        forward_mul(normed, w_qkv)
        .astype(jnp.bfloat16)
        .reshape(row_count, attributes, 3, HEADS, head_size)
    )
    queries, key_rows, values = (joined[:, :, 0], joined[:, :, 1], joined[:, :, 2])
    scores = jnp.einsum(
        "rahd,rbhd->rhab", queries, key_rows, preferred_element_type=jnp.float32
    ) * head_size ** (-0.5)
    chance = jax.nn.softmax(scores, axis=-1)
    blended = (
        jnp.einsum(
            "rhab,rbhd->rahd",
            chance.astype(jnp.bfloat16),
            values,
            preferred_element_type=jnp.float32,
        )
        .astype(jnp.bfloat16)
        .reshape(-1, feature)
    )
    return (normed, joined, chance, blended)


def rows_backward(cells, gain_vec, w_qkv, w_out, upstream):
    row_count, attributes, feature = cells.shape
    head_size = feature // HEADS
    scaling = head_size ** (-0.5)
    normed, joined, chance, blended = rows_attention(cells, gain_vec, w_qkv)
    queries, key_rows, values = (joined[:, :, 0], joined[:, :, 1], joined[:, :, 2])
    grad_low = upstream.astype(jnp.bfloat16)
    grad_out = outer(blended, grad_low)
    grad_blended = (
        backmul(grad_low, w_out)
        .astype(jnp.bfloat16)
        .reshape(row_count, attributes, HEADS, head_size)
    )
    grad_chance = jnp.einsum(
        "rahd,rbhd->rhab", grad_blended, values, preferred_element_type=jnp.float32
    )
    row_dot = jnp.sum(chance * grad_chance, axis=-1, keepdims=True)
    grad_scores = (chance * (grad_chance - row_dot)).astype(jnp.bfloat16)
    grad_queries = (
        jnp.einsum("rhab,rbhd->rahd", grad_scores, key_rows, preferred_element_type=jnp.float32)
        * scaling
    )
    grad_keys = (
        jnp.einsum("rhab,rahd->rbhd", grad_scores, queries, preferred_element_type=jnp.float32)
        * scaling
    )
    grad_values = jnp.einsum(
        "rhab,rahd->rbhd",
        chance.astype(jnp.bfloat16),
        grad_blended,
        preferred_element_type=jnp.float32,
    )
    grad_joined = (
        jnp.stack([grad_queries, grad_keys, grad_values], axis=2)
        .reshape(-1, 3 * feature)
        .astype(jnp.bfloat16)
    )
    grad_cells, grad_gain = norm_back(
        cells.reshape(-1, feature), gain_vec, backmul(grad_joined, w_qkv)
    )
    return (upstream + grad_cells, grad_gain, outer(normed, grad_joined), grad_out)


def local(
    cells_in,
    lengths,
    sets_weights,
    rows_weights,
    norm_gains,
    sets_first,
    rows_first,
    gains_first,
    sets_second,
    rows_second,
    gains_second,
    out_grad,
):
    devices = lax.axis_size("dev")
    device = lax.axis_index("dev")
    slots, model_width = cells_in.shape
    feature = model_width // ATTRS
    per_peer = slots // devices
    full_sets, full_rows, full_gains = (
        lax.all_gather(sets_weights.astype(jnp.bfloat16), "dev", axis=0, tiled=True),
        lax.all_gather(rows_weights.astype(jnp.bfloat16), "dev", axis=0, tiled=True),
        lax.all_gather(norm_gains.astype(jnp.bfloat16), "dev", axis=0, tiled=True),
    )
    set_mats, row_mats, gain_list = unpack(full_sets, full_rows, full_gains, model_width, feature)
    wq1, wo1, wu1, wd1 = set_mats
    wq2, wo2, wu2, wd2 = row_mats
    gain_one, gain_two, gain_three, gain_four = gain_list
    length_table = lengths.reshape(devices, SETS_DEV)
    own_lengths = lax.dynamic_index_in_dim(length_table, device, 0, keepdims=False)
    ends_own = jnp.cumsum(own_lengths)
    positions = jnp.arange(slots, dtype=jnp.int32)
    labels = jnp.sum((positions[:, None] >= ends_own[None, :]).astype(jnp.int32), axis=1)
    counts = jnp.sum(length_table, axis=1) // devices
    ends_at = jnp.cumsum(counts)
    starts = ends_at - counts
    position = jnp.arange(ROWS_EVEN, dtype=jnp.int32)
    source = jnp.sum((ends_at[None, :] <= position[:, None]).astype(jnp.int32), axis=1)
    pick_index = source * per_peer + position - jnp.take(starts, source)
    flat_slot = jnp.arange(devices * per_peer, dtype=jnp.int32)
    slot_owner = flat_slot // per_peer
    slot_row = flat_slot % per_peer
    is_live = slot_row < jnp.take(counts, slot_owner)
    back_index = jnp.minimum(jnp.take(starts, slot_owner) + slot_row, ROWS_EVEN - 1)
    start_cells = cells_in.astype(jnp.float32)
    after_attn, kept_parts = sets_forward(start_cells, gain_one, wq1, wo1, labels)
    leaving = mlp_forward(after_attn, gain_two, wu1, wd1)
    outgoing = leaving.reshape(per_peer, devices, model_width).transpose(1, 0, 2)
    arrived = lax.all_to_all(
        outgoing.astype(jnp.bfloat16), "dev", split_axis=0, concat_axis=0, tiled=True
    ).astype(outgoing.dtype)
    rows_in = jnp.take(arrived.reshape(devices * per_peer, model_width), pick_index, axis=0)
    cells = rows_in.reshape(ROWS_EVEN, ATTRS, feature)
    blended_rows = rows_attention(cells, gain_three, wq2)[3]
    after_rows = rows_in.reshape(-1, feature) + forward_mul(blended_rows, wo2)
    final = mlp_forward(after_rows, gain_four, wu2, wd2)
    rows_out = final.reshape(ROWS_EVEN, model_width).astype(jnp.bfloat16)
    full_sets, full_rows, full_gains = (
        lax.all_gather(sets_weights.astype(jnp.bfloat16), "dev", axis=0, tiled=True),
        lax.all_gather(rows_weights.astype(jnp.bfloat16), "dev", axis=0, tiled=True),
        lax.all_gather(norm_gains.astype(jnp.bfloat16), "dev", axis=0, tiled=True),
    )
    set_mats, row_mats, gain_list = unpack(full_sets, full_rows, full_gains, model_width, feature)
    wq1, wo1, wu1, wd1 = set_mats
    wq2, wo2, wu2, wd2 = row_mats
    gain_one, gain_two, gain_three, gain_four = gain_list
    upstream = out_grad.astype(jnp.float32).reshape(-1, feature)
    grad_after, grad_four, grad_up2, grad_down2 = mlp_backward(
        after_rows, gain_four, wu2, wd2, upstream
    )
    grad_cells, grad_three, grad_qkv2, grad_out2 = rows_backward(
        cells, gain_three, wq2, wo2, grad_after
    )
    grad_mid = grad_cells.reshape(ROWS_EVEN, model_width)
    spread_back = jnp.where(is_live[:, None], jnp.take(grad_mid, back_index, axis=0), 0.0)
    returned = lax.all_to_all(
        spread_back.reshape(devices, per_peer, model_width).astype(jnp.bfloat16),
        "dev",
        split_axis=0,
        concat_axis=0,
        tiled=True,
    ).astype(jnp.float32)
    grad_leaving = returned.transpose(1, 0, 2).reshape(slots, model_width)
    grad_attn, grad_two, grad_up1, grad_down1 = mlp_backward(
        after_attn, gain_two, wu1, wd1, grad_leaving
    )
    cells_grad, grad_one, grad_qkv1, grad_out1 = sets_backward(
        start_cells, gain_one, wq1, wo1, labels, kept_parts, grad_attn
    )
    sets_full = jnp.concatenate(
        [grad_qkv1.reshape(-1), grad_out1.reshape(-1), grad_up1.reshape(-1), grad_down1.reshape(-1)]
    )
    rows_full = jnp.concatenate(
        [grad_qkv2.reshape(-1), grad_out2.reshape(-1), grad_up2.reshape(-1), grad_down2.reshape(-1)]
    )
    gains_full = jnp.concatenate([grad_one, grad_two, grad_three, grad_four])
    sets_grad, rows_grad, gains_grad = (
        lax.psum_scatter(sets_full, "dev", scatter_dimension=0, tiled=True),
        lax.psum_scatter(rows_full, "dev", scatter_dimension=0, tiled=True),
        lax.psum_scatter(gains_full, "dev", scatter_dimension=0, tiled=True),
    )
    set_index = device * sets_grad.shape[0] + jnp.arange(sets_grad.shape[0], dtype=jnp.int32)
    row_index = device * rows_grad.shape[0] + jnp.arange(rows_grad.shape[0], dtype=jnp.int32)
    set_rates = block_rates(set_index, model_width, max(1, 3 * model_width // slots))
    row_rates = block_rates(row_index, feature, max(1, feature // 8))
    sets_new, sets_first_new, sets_second_new = adam_update(
        sets_weights, sets_grad, sets_first, sets_second, set_rates, decay_rate
    )
    rows_new, rows_first_new, rows_second_new = adam_update(
        rows_weights, rows_grad, rows_first, rows_second, row_rates, decay_rate
    )
    gains_new, gains_first_new, gains_second_new = adam_update(
        norm_gains, gains_grad, gains_first, gains_second, gain_rate, 0.0
    )
    return (
        rows_out,
        cells_grad,
        sets_grad,
        rows_grad,
        gains_grad,
        sets_new,
        rows_new,
        gains_new,
        sets_first_new,
        rows_first_new,
        gains_first_new,
        sets_second_new,
        rows_second_new,
        gains_second_new,
        sets_new.astype(jnp.bfloat16),
        rows_new.astype(jnp.bfloat16),
        gains_new.astype(jnp.bfloat16),
    )


def solution(mesh):
    return jax.shard_map(
        local,
        mesh=mesh,
        in_specs=(
            P("dev", None),
            P(),
            P("dev"),
            P("dev"),
            P("dev"),
            P("dev"),
            P("dev"),
            P("dev"),
            P("dev"),
            P("dev"),
            P("dev"),
            P("dev", None),
        ),
        out_specs=(
            P("dev", None),
            P("dev", None),
            P("dev"),
            P("dev"),
            P("dev"),
            P("dev"),
            P("dev"),
            P("dev"),
            P("dev"),
            P("dev"),
            P("dev"),
            P("dev"),
            P("dev"),
            P("dev"),
            P("dev"),
            P("dev"),
            P("dev"),
        ),
        check_vma=False,
    )
```

profile of v0, /device:TPU:0, one launch (start us, length us, event | category | flops | bytes accessed | tf_op | source)
XLA Modules:
  0.0 1599.2 jit_solution(258575864726062695)
XLA Ops:
  11.9 20.3 %select_compare_fusion = pred[384]{0:T(512)(128)(4,1)S(1)} fusion(s32[]{:T(128)} %bitcast.78, s32[]{:T(128)} %bitcast.77, s32[]{:T(128)} %bitcast.76, s32[]{:T(128)} %bitcast.75, s32[]{:T(128)} %bitcast.74, s32[]{:T(128)} %bitcast.73, s32[]{:T(128)} %bitcast.72, s32[]{:T(128)} %bitcast.71, s32[]{:T(128)} %bitcast.70, s32[]{:T(128)} %bitcast.69, ...), kind=kLoop, calls=%fused_computation.232 | loop fusion | flops 31488 | bytes 512 | tf_op jit(solution)/shard_map/lt | solution.py:308
  34.2 20.8 %compare_and_fusion.1 = (pred[384]{0:T(512)(128)(4,1)S(1)}, s32[384]{0:T(512)}) fusion(s32[]{:T(128)} %bitcast.32, s32[]{:T(128)} %bitcast.31, s32[]{:T(128)} %bitcast.30, s32[]{:T(128)} %bitcast.29, s32[]{:T(128)} %bitcast.28, s32[]{:T(128)} %bitcast.27, s32[]{:T(128)} %bitcast.26, s32[]{:T(128)} %bitcast.25, s32[]{:T(128)} %bitcast.24, s32[]{:T(128)} %bitcast.23, ...), kind=kLoop, calls=%fused_computation.246 | loop fusion | flops 34176 | bytes 2048 | tf_op jit(solution)/shard_map/jit(_take)/and | solution.py:340
  55.9 43.1 %all-reduce = bf16[2176]{0:T(1024)(128)(2,1)S(1)} all-reduce(bf16[2176]{0:T(1024)(128)(2,1)S(1)} %dynamic-update-slice), channel_id=1, replica_groups=mesh['dev'=32] {'dev'}, use_global_device_ids=true, to_apply=%add | all-reduce | flops 2176 | bytes 8704
  104.7 66.1 %all-gather.3.cloned.1.call-done = bf16[12582912]{0:T(1024)(128)(2,1)} async-done(((bf16[393216]{0:T(1024)(128)(2,1)}), bf16[12582912]{0:T(1024)(128)(2,1)}) %all-gather.3.cloned.1.call-update) | async-done | bytes 25165840 | tf_op jit(solution)/shard_map/all_gather | solution.py:286
  174.6 6.5 slice.350
  181.1 10.3 slice.157
  191.4 11.3 fusion.112
  202.7 13.4 slice.167
  231.8 13.5 slice.165
  245.4 20.1 %multiply_convert_fusion = (bf16[384,4096]{1,0:T(8,128)(2,1)S(1)}, f32[384,4096]{1,0:T(8,128)}, f32[384,4096]{1,0:T(8,128)}) fusion(bf16[1024,4096]{1,0:T(8,128)(2,1)} %slice.165, f32[384,1024]{1,0:T(8,128)S(1)} %get-tuple-element.169, f32[1024]{0:T(1024)S(1)} %get-tuple-element.100, f32[384]{0:T(512)S(1)} %fusion.87, f32[384]{0:T(512)S(1)} %broadcast_multiply_fusion.3), kind=kOutput, calls=%fused_computation.18 | convolution fusion | flops 3325034496 | bytes 25697280 | tf_op jit(solution)/shard_map/dot_general | solution.py:22
  265.4 7.1 add_convert_fusion.2
  276.9 15.7 compare_and_fusion.2
  293.3 42.3 %all-gather = bf16[32,1,1536]{2,1,0:T(2,128)(2,1)S(1)} all-gather(bf16[1,1,1536]{2,1,0:T(2,128)(2,1)S(1)} %reshape.862), channel_id=1, replica_groups=mesh['dev'=32] {'dev'}, dimensions={0}, use_global_device_ids=true | all-gather | bytes 101376 | tf_op jit(solution)/shard_map/all_gather | solution.py:287
  354.2 15.5 reshape.636
  369.7 10.4 fusion.113
  384.4 9.2 fusion.18
  393.6 19.0 %copy.211 = f32[360,8,16,16]{0,3,2,1:T(8,128)} copy(f32[360,8,16,16]{2,3,1,0:T(8,128)} %fusion.18) | data formatting | bytes 5898240 | tf_op jit(solution)/shard_map/rahd,rbhd->rhab/dot_general | solution.py:206
  419.1 17.6 %copy.212 = bf16[360,8,16,16]{3,2,1,0:T(8,128)(2,1)} copy(bf16[360,8,16,16]{0,3,2,1:T(8,128)(2,1)S(1)} %fusion.100) | data formatting | bytes 2949120 | tf_op jit(solution)/shard_map/convert_element_type | solution.py:213
  436.6 9.9 convert_bitcast_fusion
  446.6 6.3 copy.213
  452.9 6.6 reshape.637
  461.2 14.9 multiply_convert_fusion.1
  484.5 6.5 reshape.640
  491.0 12.0 fusion.24
  502.9 13.6 fusion.15
  516.5 19.4 %copy.218 = f32[360,8,16,16]{0,3,2,1:T(8,128)} copy(f32[360,8,16,16]{2,3,1,0:T(8,128)} %fusion.15) | data formatting | bytes 5898240 | tf_op jit(solution)/shard_map/rahd,rbhd->rhab/dot_general | solution.py:236
  535.9 6.8 multiply_convert_fusion.3
  542.8 18.0 %copy.219 = bf16[360,8,16,16]{3,2,1,0:T(8,128)(2,1)} copy(bf16[360,8,16,16]{0,3,2,1:T(8,128)(2,1)} %multiply_convert_fusion.3) | data formatting | bytes 2949120 | tf_op jit(solution)/shard_map/convert_element_type | solution.py:240
  560.8 11.8 multiply_bitcast_fusion
  572.6 11.6 multiply_bitcast_fusion.1
  590.2 9.9 copy.225
  600.2 9.7 copy.223
  609.9 9.7 copy.224
  623.1 15.6 copy.226
  638.7 16.7 %convert_element_type.211 = bf16[5760,192]{0,1:T(8,128)(2,1)} reshape(bf16[360,16,3,8,8]{1,0,4,3,2:T(8,128)(2,1)} %copy.226) | data formatting | bytes 4423680 | tf_op jit(solution)/shard_map/convert_element_type | solution.py:258
  681.0 19.4 %all-to-all-done.1 = bf16[32,12,1024]{2,1,0:T(8,128)(2,1)} async-done(((bf16[32,12,1024]{2,1,0:T(8,128)(2,1)}), bf16[32,12,1024]{2,1,0:T(8,128)(2,1)}, u32[]{:S(2)}, u32[]{:S(2)}) %all-to-all-start.1) | async-done | bytes 786464 | tf_op jit(solution)/shard_map/all_to_all | solution.py:341
  702.1 13.3 add_convert_fusion
  715.4 7.7 multiply_reduce_fusion.3
  743.0 8.7 convolution_bitcast_fusion.1
  751.7 8.1 convolution_bitcast_fusion
  764.6 6.8 convolution_bitcast_fusion.2
  771.4 12.0 copy.255
  783.4 15.1 copy.257
  798.6 14.3 copy.258
  812.9 43.5 %pad_maximum_fusion = f32[12582912]{0:T(1024)} fusion(f32[4194304]{0:T(1024)} %bitcast.271, f32[4194304]{0:T(1024)} %bitcast.270, f32[1048576]{0:T(1024)} %bitcast.275, f32[3145728]{0:T(1024)S(1)} %bitcast.274), kind=kLoop, calls=%fused_computation.4 | loop fusion | flops 37748736 | bytes 100663296 | tf_op jit(solution)/shard_map/concatenate | solution.py:355
  873.3 40.1 %all-reduce.3 = f32[2176]{0:T(1024)S(1)} all-reduce(f32[2176]{0:T(1024)S(1)} %concatenate.11), channel_id=4, replica_groups=mesh['dev'=32] {'dev'}, use_global_device_ids=true, to_apply=%region_35.37.clone | all-reduce | flops 2176 | bytes 17408
  917.4 666.5 %all-reduce.7.cloned.1.call-done = (f32[12582912]{0:T(1024)}, f32[49152]{0:T(1024)}) async-done(((f32[12582912]{0:T(1024)}, f32[49152]{0:T(1024)}), (f32[12582912]{0:T(1024)}, f32[49152]{0:T(1024)})) %all-reduce.7.cloned.1.call-update) | async-done | bytes 50528272
  1583.9 6.8 fusion.105
  (324 shorter events, 160.0 us)
Async XLA Ops:
  7.2 96.7 %copy-start.3 = (bf16[384,1024]{1,0:T(8,128)(2,1)S(1)}, bf16[384,1024]{1,0:T(8,128)(2,1)}, u32[]{:S(2)}) copy-start(bf16[384,1024]{1,0:T(8,128)(2,1)} %param.14) | copy-start | bytes 2359300
  7.2 163.5 %all-gather.3.cloned.1.call-start = ((), (), s32[]{:S(2)}) async-start(), calls=%async_computation.2 | async-start | bytes 25952256 | tf_op jit(solution)/shard_map/all_gather | solution.py:286
  104.1 112.0 %copy-start.56 = (f32[384]{0:T(512)}, f32[384]{0:T(512)S(1)}, u32[]{:S(2)}) copy-start(f32[384]{0:T(512)S(1)} %broadcast_multiply_fusion.4) | copy-start | bytes 4612
  104.5 70.2 %copy-start.64 = (f32[384]{0:T(512)}, f32[384]{0:T(512)S(1)}, u32[]{:S(2)}) copy-start(f32[384]{0:T(512)S(1)} %fusion.48) | copy-start | bytes 4612
  104.5 111.6 %copy-start.58 = (f32[384]{0:T(512)}, f32[384]{0:T(512)S(1)}, u32[]{:S(2)}) copy-start(f32[384]{0:T(512)S(1)} %fusion.86) | copy-start | bytes 4612
  104.5 111.6 %copy-start.48 = (f32[1024]{0:T(1024)}, f32[1024]{0:T(1024)S(1)}, u32[]{:S(2)}) copy-start(f32[1024]{0:T(1024)S(1)} %get-tuple-element.101) | copy-start | bytes 12292
  104.5 140.8 %copy-start.42 = (f32[1024]{0:T(1024)}, f32[1024]{0:T(1024)S(1)}, u32[]{:S(2)}) copy-start(f32[1024]{0:T(1024)S(1)} %get-tuple-element.100) | copy-start | bytes 12292
  231.5 34.0 %copy-start.6 = (f32[384,1024]{1,0:T(8,128)}, f32[384,1024]{1,0:T(8,128)S(1)}, u32[]{:S(2)}) copy-start(f32[384,1024]{1,0:T(8,128)S(1)} %get-tuple-element.169) | copy-start | bytes 4718596
  231.5 13.9 copy-start.51
  231.8 13.5 copy-start.66
  231.8 13.5 copy-start.54
  265.4 7.1 copy-start.30
  272.6 64.3 %copy-start.41 = (bf16[360,1024]{1,0:T(8,128)(2,1)S(1)}, bf16[360,1024]{1,0:T(8,128)(2,1)}, u32[]{:S(2)}) copy-start(bf16[360,1024]{1,0:T(8,128)(2,1)} %param.25) | copy-start | bytes 2211844
  274.0 67.5 %all-to-all-start = ((bf16[32,12,1024]{2,1,0:T(8,128)(2,1)}), bf16[32,12,1024]{2,1,0:T(8,128)(2,1)S(1)}, u32[]{:S(2)}, u32[]{:S(2)}) async-start(bf16[32,12,1024]{2,1,0:T(8,128)(2,1)} %bitcast.267), calls=%async_computation | async-start | bytes 2097152 | tf_op jit(solution)/shard_map/all_to_all | solution.py:314
  276.8 63.4 %copy-start.75 = (s32[384]{0:T(512)S(1)}, s32[384]{0:T(512)}, u32[]{:S(2)}) copy-start(s32[384]{0:T(512)} %get-tuple-element.73) | copy-start | bytes 4612
  336.6 15.4 copy-start.44
  336.8 139.4 %copy-start.46 = (bf16[256,64]{1,0:T(8,128)(2,1)}, bf16[256,64]{1,0:T(8,128)(2,1)S(1)}, u32[]{:S(2)}) copy-start(bf16[256,64]{1,0:T(8,128)(2,1)S(1)} %slice.180) | copy-start | bytes 98308
  340.9 11.1 copy-start.62
  461.2 14.9 copy-start.14
  572.6 14.3 copy-start.53
  638.7 16.7 %copy-start.45 = (bf16[64,192]{1,0:T(8,128)(2,1)S(1)}, bf16[64,192]{1,0:T(8,128)(2,1)}, u32[]{:S(2)}) copy-start(bf16[64,192]{1,0:T(8,128)(2,1)} %copy-done.44) | copy-start | bytes 73732
  638.7 16.7 %copy-start.63 = (f32[64]{0:T(128)S(1)}, f32[64]{0:T(128)}, u32[]{:S(2)}) copy-start(f32[64]{0:T(128)} %copy-done.62) | copy-start | bytes 772
  670.6 6.1 copy-start.26
  670.6 6.1 copy-start.28
  670.6 29.7 %all-to-all-start.1 = ((bf16[32,12,1024]{2,1,0:T(8,128)(2,1)}), bf16[32,12,1024]{2,1,0:T(8,128)(2,1)}, u32[]{:S(2)}, u32[]{:S(2)}) async-start(bf16[32,12,1024]{2,1,0:T(8,128)(2,1)} %select_convert_fusion), calls=%async_computation.1 | async-start | bytes 2097152 | tf_op jit(solution)/shard_map/all_to_all | solution.py:341
  674.2 909.8 %all-reduce.7.cloned.1.call-start = ((), (), s32[]{:S(2)}) async-start(), calls=%async_computation.3 | async-start | bytes 101056512
  702.0 49.7 %copy-start.18 = (bf16[12,32,1024]{2,1,0:T(8,128)(2,1)}, bf16[12,32,1024]{2,1,0:T(8,128)(2,1)S(1)}, u32[]{:S(2)}) copy-start(bf16[12,32,1024]{2,1,0:T(8,128)(2,1)S(1)} %copy.228) | copy-start | bytes 2359300
  702.0 13.4 copy-start.7
  702.0 13.4 copy-start.43
  702.0 13.4 copy-start.52
  702.1 13.4 copy-start.55
  715.4 7.7 copy-start.34
  715.4 7.7 copy-start.67
  732.3 7.2 slice-start
  743.0 8.7 copy-start.31
  751.7 8.1 copy-start.10
  783.4 29.4 %slice-start.2 = ((s8[12582912]{0:T(1024)(128)(4,1)}), s8[4194304]{0:T(1024)(128)(4,1)S(1)}, s32[]{:S(2)}) async-start(s8[12582912]{0:T(1024)(128)(4,1)} %bitcast.272), calls=%async_computation.6 | async-start | bytes 8388608
  783.4 29.4 %slice-start.3 = ((s8[12582912]{0:T(1024)(128)(4,1)}), s8[4194304]{0:T(1024)(128)(4,1)S(1)}, s32[]{:S(2)}) async-start(s8[12582912]{0:T(1024)(128)(4,1)} %bitcast.272), calls=%async_computation.7 | async-start | bytes 8388608
  798.6 14.3 slice-start.4
  865.2 7.9 copy-start.76
  865.2 48.2 %copy-start.79 = (f32[68]{0:T(128)S(1)}, f32[68]{0:T(128)}, u32[]{:S(2)}) copy-start(f32[68]{0:T(128)} %param.18) | copy-start | bytes 820
  865.2 48.2 %copy-start.80 = (f32[68]{0:T(128)S(1)}, f32[68]{0:T(128)}, u32[]{:S(2)}) copy-start(f32[68]{0:T(128)} %param.21) | copy-start | bytes 820
  865.2 48.2 %copy-start.81 = (f32[68]{0:T(128)S(1)}, f32[68]{0:T(128)}, u32[]{:S(2)}) copy-start(f32[68]{0:T(128)} %param.24) | copy-start | bytes 820
  865.3 48.8 %copy-start.19 = (bf16[12,32,1024]{2,1,0:T(8,128)(2,1)S(1)}, bf16[12,32,1024]{2,1,0:T(8,128)(2,1)}, u32[]{:S(2)}) copy-start(bf16[12,32,1024]{2,1,0:T(8,128)(2,1)} %copy-done.18) | copy-start | bytes 2359300
  871.2 42.8 %copy-start.12 = (f32[384,1024]{1,0:T(8,128)S(1)}, f32[384,1024]{1,0:T(8,128)}, u32[]{:S(2)}) copy-start(f32[384,1024]{1,0:T(8,128)} %copy-done.11) | copy-start | bytes 4718596
  1583.9 6.8 copy-start.61
  1583.9 6.8 copy-start.73
  1583.9 6.8 copy-start.74
  (44 other events, 114.2 us)
Sparse Core Ops, SparseCore 0:
  11.5 159.1 all-gather.2
  856.5 727.3 all-reduce.6
where the time goes:
time: 1610 us; the launch traced here: 1600 us
  waiting for transfers between devices  752 us (47%)
  local copies, waits for them, and re-layouts  340 us (21%)
  matrix products  210 us (13%)
  other arithmetic  150 us (9%)
  blocking collectives  126 us (8%)
    unnamed x3, waiting for transfers between devices  667 us
    unnamed x2, blocking collectives  83.3 us
    all_gather x1, waiting for transfers between devices, local(): lax.all_gather(sets_weights.astype(jnp.bfloat16), 'dev', axis=0, tiled=True)  66.1 us
    unnamed x185, local copies, waits for them, and re-layouts  61.6 us
    dot_general x8, matrix products, forward_mul(): return jnp.dot(left, right, preferred_element_type=jnp.float32)  56.5 us
    concatenate x1, other arithmetic, local(): jnp.concatenate([grad_qkv1.reshape(-1), grad_out1.reshape(-1), grad_up1.r...  43.5 us
    all_gather x1, blocking collectives, local(): lax.all_gather(rows_weights.astype(jnp.bfloat16), 'dev', axis=0, tiled=True)  42.3 us
    dot_general x8, matrix products, backmul(): lax.dot_general(upstream, weight, (((1,), (1,)), ((), ())), preferred_ele...  37 us
  transfers between devices with their start and end apart: 4, of which 3 were waited for; matrix products, arithmetic and copies ran while one was open for 6% of the time, Pallas kernels for 0%

commit v1 on v0

v1 whole, which is shorter than its diff:
```python
import functools

import jax
import jax.numpy as jnp
from jax import lax
from jax.experimental import pallas as pl
from jax.experimental.pallas import tpu as pltpu
from jax.sharding import PartitionSpec as P

ATTRS = 16
HEADS = 8
SETS_DEV = 2
STEP = 5
LANES = 128

norm_eps = 1e-05
beta_one = 0.5
beta_two = 0.5
adam_eps = 1e-08
decay_rate = 0.1
gain_rate = 0.5

def mm(left, right, dims):
    return lax.dot_general(left, right, (dims, ((), ())), preferred_element_type=jnp.float32)


def gelu_pair(v):
    size = jnp.abs(v) * 0.7071067811865476
    t = 1.0 / (1.0 + 0.3275911 * size)
    bell = jnp.exp(-0.5 * v * v)
    poly = t * (0.254829592 + t * (-0.284496736 + t * (1.421413741 + t * (-1.453152027 + t * 1.061405429))))
    tail = 0.5 * poly * bell
    phi = jnp.where(v < 0.0, tail, 1.0 - tail)
    return v * phi, phi + v * (bell * 0.3989422804014327)


def rows_kernel(
    pick_ref, arrived_ref, og_ref, wq_ref, wqt_ref, wo_ref, wot_ref, wu_ref, wut_ref, wd_ref, wdt_ref, g3_ref, g4_ref,
    out_ref, back_ref, dwq_ref, dwo_ref, dwu_ref, dwd_ref, dg3_ref, dg4_ref,
    joined, prob, dscore, outs, douts, dj, back_acc,
):
    f32, bf = jnp.float32, jnp.bfloat16
    step = pl.program_id(0)
    last = pl.num_programs(0) - 1
    slots = arrived_ref.shape[0]
    scaling = HEADS ** (-0.5)
    feat = 64

    @pl.when(step == 0)
    def _():
        for ref in (dwq_ref, dwo_ref, dwu_ref, dwd_ref, dg3_ref, dg4_ref, back_acc):
            ref[...] = jnp.zeros_like(ref)

    source = lax.broadcasted_iota(jnp.int32, (slots, LANES), 0)
    hot = (source == pick_ref[0]).astype(f32).astype(bf)
    x_t = mm(arrived_ref[...], hot, ((0,), (0,)))

    def to_lanes(tall):
        return jnp.concatenate([tall[a * feat : (a + 1) * feat] for a in range(ATTRS)], axis=1)

    def to_tall(wide):
        return jnp.concatenate([wide[:, a * LANES : (a + 1) * LANES] for a in range(ATTRS)], axis=0)

    def norm(v):
        center = v - jnp.mean(v, axis=0, keepdims=True)
        root = lax.rsqrt(jnp.mean(center * center, axis=0, keepdims=True) + norm_eps)
        return center * root, root

    def norm_back(hat, root, gain, upstream):
        dhat = upstream * gain
        return root * (
            dhat - jnp.mean(dhat, axis=0, keepdims=True) - hat * jnp.mean(dhat * hat, axis=0, keepdims=True)
        )

    def fold(v):
        total = v[:, :LANES]
        for a in range(1, ATTRS):
            total = total + v[:, a * LANES : (a + 1) * LANES]
        return total

    x = to_lanes(x_t)
    g3, g4 = g3_ref[...], g4_ref[...]
    hat3, root3 = norm(x)
    a3 = (hat3 * g3).astype(bf)
    j_t = mm(wqt_ref[...], a3, ((1,), (0,))).astype(bf).astype(f32)
    for a in range(ATTRS):
        joined[a] = j_t[:, a * LANES : (a + 1) * LANES]

    def attend(a, carry):
        q = [joined[a, d * 8 : d * 8 + 8] * scaling for d in range(8)]
        scores = []
        for b in range(ATTRS):
            s = q[0] * joined[b, 64:72]
            for d in range(1, 8):
                s = s + q[d] * joined[b, 64 + d * 8 : 72 + d * 8]
            scores.append(s)
        peak = functools.reduce(jnp.maximum, scores)
        weights = [jnp.exp(s - peak) for s in scores]
        inverse = 1.0 / functools.reduce(jnp.add, weights)
        o = [None] * 8
        for b in range(ATTRS):
            p = weights[b] * inverse
            prob[a, b] = p
            p = p.astype(bf).astype(f32)
            for d in range(8):
                term = p * joined[b, 128 + d * 8 : 136 + d * 8]
                o[d] = term if b == 0 else o[d] + term
        for d in range(8):
            outs[a, d * 8 : d * 8 + 8] = o[d]
        return carry

    lax.fori_loop(0, ATTRS, attend, 0)
    o = jnp.concatenate([outs[a] for a in range(ATTRS)], axis=1).astype(bf)
    h3 = x + mm(wot_ref[...], o, ((1,), (0,)))
    hat4, root4 = norm(h3)
    a4 = (hat4 * g4).astype(bf)
    pre = mm(wut_ref[...], a4, ((1,), (0,)))
    active, slope = gelu_pair(pre)
    u = active.astype(bf)
    y = h3 + mm(wdt_ref[...], u, ((1,), (0,)))
    out_ref[...] = to_tall(y).T.astype(bf)

    grad = to_lanes(og_ref[...].astype(f32).T)
    gz = grad.astype(bf)
    dwd_ref[...] += mm(u, gz, ((1,), (1,)))
    dpre = (slope * mm(wd_ref[...], gz, ((1,), (0,)))).astype(bf)
    dwu_ref[...] += mm(a4, dpre, ((1,), (1,)))
    da4 = mm(wu_ref[...], dpre, ((1,), (0,)))
    dg4_ref[...] += fold(da4 * hat4)
    dh3 = grad + norm_back(hat4, root4, g4, da4)

    gz = dh3.astype(bf)
    dwo_ref[...] += mm(o, gz, ((1,), (1,)))
    do = mm(wo_ref[...], gz, ((1,), (0,))).astype(bf).astype(f32)
    for a in range(ATTRS):
        douts[a] = do[:, a * LANES : (a + 1) * LANES]

    def spread(a, carry):
        up = [douts[a, d * 8 : d * 8 + 8] for d in range(8)]
        dot = None
        slopes = []
        for b in range(ATTRS):
            s = up[0] * joined[b, 128:136]
            for d in range(1, 8):
                s = s + up[d] * joined[b, 128 + d * 8 : 136 + d * 8]
            slopes.append(s)
            term = prob[a, b] * s
            dot = term if b == 0 else dot + term
        dq = [None] * 8
        for b in range(ATTRS):
            ds = (prob[a, b] * (slopes[b] - dot)).astype(bf).astype(f32) * scaling
            dscore[a, b] = ds
            for d in range(8):
                term = ds * joined[b, 64 + d * 8 : 72 + d * 8]
                dq[d] = term if b == 0 else dq[d] + term
        for d in range(8):
            dj[a, d * 8 : d * 8 + 8] = dq[d]
        return carry

    lax.fori_loop(0, ATTRS, spread, 0)

    def collect(b, carry):
        dk, dv = [None] * 8, [None] * 8
        for a in range(ATTRS):
            ds = dscore[a, b]
            p = prob[a, b].astype(bf).astype(f32)
            for d in range(8):
                one = ds * joined[a, d * 8 : d * 8 + 8]
                two = p * douts[a, d * 8 : d * 8 + 8]
                dk[d] = one if a == 0 else dk[d] + one
                dv[d] = two if a == 0 else dv[d] + two
        for d in range(8):
            dj[b, 64 + d * 8 : 72 + d * 8] = dk[d]
            dj[b, 128 + d * 8 : 136 + d * 8] = dv[d]
        return carry

    lax.fori_loop(0, ATTRS, collect, 0)
    djl = jnp.concatenate([dj[a] for a in range(ATTRS)], axis=1).astype(bf)
    dwq_ref[...] += mm(a3, djl, ((1,), (1,)))
    da3 = mm(wq_ref[...], djl, ((1,), (0,)))
    dg3_ref[...] += fold(da3 * hat3)
    dhc = to_tall(dh3 + norm_back(hat3, root3, g3, da3)).astype(bf)
    back_acc[...] += mm(hot, dhc, ((1,), (1,)))

    @pl.when(step == last)
    def _():
        back_ref[...] = back_acc[...].astype(bf)


def rows_layer(pick, arrived, og, wq, wo, wu, wd, g3, g4):
    f32, bf = jnp.float32, jnp.bfloat16
    total, width = og.shape
    slots = arrived.shape[0]
    steps = total // LANES
    feat = 64
    wqp = wq.reshape(feat, 3, HEADS, 8).transpose(0, 1, 3, 2).reshape(feat, 3 * feat)
    wop = wo.reshape(HEADS, 8, feat).transpose(1, 0, 2).reshape(feat, feat)
    whole = lambda *shape: pl.BlockSpec(shape, lambda t: (0,) * len(shape))
    outs = pl.pallas_call(
        rows_kernel,
        grid=(steps,),
        in_specs=[
            pl.BlockSpec((1, 1, LANES), lambda t: (t, 0, 0)),
            whole(slots, width),
            pl.BlockSpec((LANES, width), lambda t: (t, 0)),
            whole(feat, 192), whole(192, feat), whole(feat, feat), whole(feat, feat),
            whole(feat, 256), whole(256, feat), whole(256, feat), whole(feat, 256),
            whole(feat, 1), whole(feat, 1),
        ],
        out_specs=[
            pl.BlockSpec((LANES, width), lambda t: (t, 0)),
            whole(slots, width),
            whole(feat, 192), whole(feat, feat), whole(feat, 256), whole(256, feat),
            whole(feat, LANES), whole(feat, LANES),
        ],
        out_shape=[
            jax.ShapeDtypeStruct((total, width), bf),
            jax.ShapeDtypeStruct((slots, width), bf),
            jax.ShapeDtypeStruct((feat, 192), f32),
            jax.ShapeDtypeStruct((feat, feat), f32),
            jax.ShapeDtypeStruct((feat, 256), f32),
            jax.ShapeDtypeStruct((256, feat), f32),
            jax.ShapeDtypeStruct((feat, LANES), f32),
            jax.ShapeDtypeStruct((feat, LANES), f32),
        ],
        scratch_shapes=[
            pltpu.VMEM((ATTRS, 192, LANES), f32),
            pltpu.VMEM((ATTRS, ATTRS, 8, LANES), f32),
            pltpu.VMEM((ATTRS, ATTRS, 8, LANES), f32),
            pltpu.VMEM((ATTRS, 64, LANES), f32),
            pltpu.VMEM((ATTRS, 64, LANES), f32),
            pltpu.VMEM((ATTRS, 192, LANES), f32),
            pltpu.VMEM((slots, width), f32),
        ],
        compiler_params=pltpu.CompilerParams(vmem_limit_bytes=56 * 2**20),
    )(
        pick.reshape(steps, 1, LANES), arrived, og,
        wqp, wqp.T, wop, wop.T, wu, wu.T, wd, wd.T, g3.reshape(feat, 1), g4.reshape(feat, 1),
    )
    rows_out, back, dwqp, dwop, dwu, dwd, dg3, dg4 = outs
    dwq = dwqp.reshape(feat, 3, 8, HEADS).transpose(0, 1, 3, 2).reshape(feat, 3 * feat)
    dwo = dwop.reshape(8, HEADS, feat).transpose(1, 0, 2).reshape(feat, feat)
    return rows_out, back, dwq, dwo, dwu, dwd, jnp.sum(dg3, axis=1), jnp.sum(dg4, axis=1)


def fwd_mul(left, right):
    return mm(left, right, ((1,), (0,)))


def outer(left, right):
    return mm(left, right, ((0,), (0,)))


def backmul(upstream, weight):
    return mm(upstream, weight, ((1,), (1,)))


def norm_parts(inputs):
    center = inputs - jnp.mean(inputs, axis=-1, keepdims=True)
    root = lax.rsqrt(jnp.mean(center * center, axis=-1, keepdims=True) + norm_eps)
    return center * root, root


def norm_pull(hat, root, gain, upstream):
    dhat = upstream * gain
    inner = jnp.mean(dhat * hat, axis=-1, keepdims=True)
    grad = root * (dhat - jnp.mean(dhat, axis=-1, keepdims=True) - hat * inner)
    return grad, jnp.sum(upstream * hat, axis=0)


def running(values):
    number = jnp.arange(values.shape[0], dtype=jnp.int32)
    return jnp.sum(jnp.where(number[None, :] <= number[:, None], values[None, :], 0), axis=1)


def block_rates(position, feature, out_fan):
    cut_one = 3 * feature * feature
    cut_two = cut_one + feature * feature
    cut_three = cut_two + 4 * feature * feature
    fans = (feature, out_fan, feature, 4 * feature)
    rates = [0.5 * fan ** (-0.5) for fan in fans]
    return jnp.where(
        position < cut_one,
        rates[0],
        jnp.where(position < cut_two, rates[1], jnp.where(position < cut_three, rates[2], rates[3])),
    ).astype(jnp.float32)


def adam_update(weight, gradient, first, second, rates, decay):
    first_new = beta_one * first + (1.0 - beta_one) * gradient
    second_new = beta_two * second + (1.0 - beta_two) * gradient * gradient
    corrected = first_new / (1.0 - beta_one**STEP)
    scaled = second_new / (1.0 - beta_two**STEP)
    weight_new = weight - rates * (corrected / (jnp.sqrt(scaled) + adam_eps) + decay * weight)
    return (weight_new, first_new, second_new)


def local(
    cells_in, lengths, sets_weights, rows_weights, norm_gains, sets_first, rows_first, gains_first,
    sets_second, rows_second, gains_second, out_grad,
):
    f32, bf = jnp.float32, jnp.bfloat16
    devices = lax.axis_size("dev")
    device = lax.axis_index("dev")
    slots, width = cells_in.shape
    feat = width // ATTRS
    per_peer = slots // devices
    rows_even = out_grad.shape[0]
    rows_pad = -(-rows_even // LANES) * LANES
    head = width // HEADS
    scaling = head ** (-0.5)

    n_rows, n_gains = rows_weights.shape[0], norm_gains.shape[0]
    small = jnp.concatenate([rows_weights, norm_gains]).astype(bf)
    small = jnp.pad(small, (0, -small.shape[0] % 1024)).reshape(-1, 1024)
    small = lax.all_gather(small, "dev", axis=0, tiled=False).reshape(devices, -1)
    full_rows = small[:, :n_rows].reshape(-1)
    full_gains = small[:, n_rows : n_rows + n_gains].reshape(-1).astype(f32)
    flat = lax.all_gather(sets_weights.astype(bf).reshape(-1, width), "dev", axis=0, tiled=True)
    wq1 = flat[: 3 * width].reshape(width, 3 * width)
    wo1 = flat[3 * width : 4 * width]
    wu1 = flat[4 * width : 8 * width].reshape(width, 4 * width)
    wd1 = flat[8 * width :]
    square = feat * feat
    wq2 = full_rows[: 3 * square].reshape(feat, 3 * feat)
    wo2 = full_rows[3 * square : 4 * square].reshape(feat, feat)
    wu2 = full_rows[4 * square : 8 * square].reshape(feat, 4 * feat)
    wd2 = full_rows[8 * square :].reshape(4 * feat, feat)
    g1, g2 = full_gains[:width], full_gains[width : 2 * width]
    g3, g4 = full_gains[2 * width : 2 * width + feat], full_gains[2 * width + feat :]

    table = lengths.reshape(devices, SETS_DEV)
    own = lax.dynamic_index_in_dim(table, device, 0, keepdims=False)
    positions = jnp.arange(slots, dtype=jnp.int32)
    labels = jnp.sum((positions[:, None] >= running(own)[None, :]).astype(jnp.int32), axis=1)
    counts = jnp.sum(table, axis=1) // devices
    ends = running(counts)
    spot = jnp.arange(rows_pad, dtype=jnp.int32)
    past = (ends[None, :] <= spot[:, None]).astype(jnp.int32)
    source = jnp.sum(past, axis=1)
    start = jnp.sum(past * counts[None, :], axis=1)
    pick = jnp.where(spot < rows_even, source * per_peer + spot - start, -1)

    h0 = cells_in.astype(f32)
    hat1, root1 = norm_parts(h0)
    a1 = (hat1 * g1).astype(bf)
    joined = fwd_mul(a1, wq1).astype(bf).reshape(slots, 3, HEADS, head)
    queries, key_rows, values = joined[:, 0], joined[:, 1], joined[:, 2]
    related = labels[:, None] == labels[None, :]
    scores = jnp.einsum("qhd,khd->hqk", queries, key_rows, preferred_element_type=f32) * scaling
    scores = jnp.where(related[None], scores, -jnp.inf)
    weights = jnp.exp(scores - jnp.max(scores, axis=-1, keepdims=True))
    chance = weights / jnp.sum(weights, axis=-1, keepdims=True)
    chance_low = chance.astype(bf)
    o1 = jnp.einsum("hqk,khd->qhd", chance_low, values, preferred_element_type=f32).astype(bf).reshape(slots, width)
    h1 = h0 + fwd_mul(o1, wo1)
    hat2, root2 = norm_parts(h1)
    a2 = (hat2 * g2).astype(bf)
    active, slope = gelu_pair(fwd_mul(a2, wu1))
    u1 = active.astype(bf)
    h2 = h1 + fwd_mul(u1, wd1)

    outgoing = h2.astype(bf).reshape(per_peer, devices, width).transpose(1, 0, 2)
    arrived = lax.all_to_all(outgoing, "dev", split_axis=0, concat_axis=0, tiled=True)
    og = jnp.pad(out_grad, ((0, rows_pad - rows_even), (0, 0)))
    rows_out, back, dq2, do2, du2, dd2, dg3, dg4 = rows_layer(
        pick, arrived.reshape(slots, width), og, wq2, wo2, wu2, wd2, g3, g4
    )
    rows_out = rows_out[:rows_even]
    rows_flat = jnp.concatenate([dq2.reshape(-1), do2.reshape(-1), du2.reshape(-1), dd2.reshape(-1)])
    extra = rows_flat.reshape(devices, n_rows).astype(bf)
    extra = jnp.pad(extra, ((0, 0), (0, -n_rows % width))).reshape(devices, -1, width)
    payload = jnp.concatenate([back.reshape(devices, per_peer, width), extra], axis=1)
    returned = lax.all_to_all(payload, "dev", split_axis=0, concat_axis=0, tiled=True)
    grad = returned[:, :per_peer].transpose(1, 0, 2).reshape(slots, width).astype(f32)
    rows_grad = jnp.sum(returned[:, per_peer:].reshape(devices, -1)[:, :n_rows].astype(f32), axis=0)

    gz = grad.astype(bf)
    dd1 = outer(u1, gz).astype(bf)
    dpre = (slope * backmul(gz, wd1)).astype(bf)
    du1 = outer(a2, dpre).astype(bf)
    dh, dg2 = norm_pull(hat2, root2, g2, backmul(dpre, wu1))
    grad = grad + dh
    gz = grad.astype(bf)
    do1 = outer(o1, gz).astype(bf)
    dblend = backmul(gz, wo1).astype(bf).reshape(slots, HEADS, head)
    dchance = jnp.einsum("qhd,khd->hqk", dblend, values, preferred_element_type=f32)
    dot = jnp.sum(chance * dchance, axis=-1, keepdims=True)
    dscores = (chance * (dchance - dot)).astype(bf)
    dq = jnp.einsum("hqk,khd->qhd", dscores, key_rows, preferred_element_type=f32) * scaling
    dk = jnp.einsum("hqk,qhd->khd", dscores, queries, preferred_element_type=f32) * scaling
    dv = jnp.einsum("hqk,qhd->khd", chance_low, dblend, preferred_element_type=f32)
    djoined = jnp.concatenate([part.reshape(slots, width).astype(bf) for part in (dq, dk, dv)], axis=1)
    dq1 = outer(a1, djoined).astype(bf)
    dh, dg1 = norm_pull(hat1, root1, g1, backmul(djoined, wq1))
    cells_grad = grad + dh

    full = jnp.concatenate([dq1.reshape(-1, width), do1, du1.reshape(-1, width), dd1])
    sets_grad = lax.psum_scatter(full, "dev", scatter_dimension=0, tiled=True).astype(f32).reshape(-1)
    gains = jnp.concatenate([dg1, dg2, dg3, dg4]).reshape(devices, 1, n_gains)
    gains_grad = jnp.sum(lax.all_to_all(gains, "dev", split_axis=0, concat_axis=0, tiled=True), axis=(0, 1))

    set_index = device * sets_grad.shape[0] + jnp.arange(sets_grad.shape[0], dtype=jnp.int32)
    row_index = device * n_rows + jnp.arange(n_rows, dtype=jnp.int32)
    set_rates = block_rates(set_index, width, max(1, 3 * width // slots))
    row_rates = block_rates(row_index, feat, max(1, feat // 8))
    sets_new, sets_first_new, sets_second_new = adam_update(
        sets_weights, sets_grad, sets_first, sets_second, set_rates, decay_rate
    )
    rows_new, rows_first_new, rows_second_new = adam_update(
        rows_weights, rows_grad, rows_first, rows_second, row_rates, decay_rate
    )
    gains_new, gains_first_new, gains_second_new = adam_update(
        norm_gains, gains_grad, gains_first, gains_second, gain_rate, 0.0
    )
    return (
        rows_out, cells_grad, sets_grad, rows_grad, gains_grad, sets_new, rows_new, gains_new,
        sets_first_new, rows_first_new, gains_first_new, sets_second_new, rows_second_new, gains_second_new,
        sets_new.astype(bf), rows_new.astype(bf), gains_new.astype(bf),
    )


def solution(mesh):
    flat = P("dev")
    tall = P("dev", None)
    return jax.shard_map(
        local,
        mesh=mesh,
        in_specs=(tall, P()) + (flat,) * 9 + (tall,),
        out_specs=(tall, tall) + (flat,) * 15,
        check_vma=False,
    )
```

time: 1610 us -> 725 us (0.45)
  waiting for transfers between devices: 752 us -> 356 us
  local copies, waits for them, and re-layouts: 340 us -> 89.1 us
  matrix products: 210 us -> 91 us
  other arithmetic: 150 us -> 55.4 us
  blocking collectives: 126 us -> 74.1 us
  Pallas kernels: 0 us -> 33.8 us
    unnamed x3 -> x2, waiting for transfers between devices: 667 us -> 0.03 us
    reduce_scatter x0 -> x1, waiting for transfers between devices: none -> 222 us  [local(): lax.psum_scatter(full, 'dev', scatter_dimension=0, tiled=True).astype(f32)]
    dot_general x36 -> x18, matrix products: 210 us -> 91 us  [the longest x12 78.3 us: mm(): lax.dot_general(left, right, (dims, ((), ())), preferred_element_type=jnp...]
    unnamed x2 -> x0, blocking collectives: 83.3 us -> none
    convert_element_type x9 -> x2, local copies, waits for them, and re-layouts: 82.6 us -> 0.24 us  [the longest x1 0.14 us: local(): extra = rows_flat.reshape(devices, n_rows).astype(bf)]
    unnamed x185 -> x112, local copies, waits for them, and re-layouts: 61.6 us -> 7.84 us
    slice x17 -> x13, local copies, waits for them, and re-layouts: 71 us -> 17.9 us  [the longest x1 7.57 us: local(): wu1 = flat[4 * width:8 * width].reshape(width, 4 * width)]
    all_gather x1, waiting for transfers between devices: 66.1 us -> 114 us  [local(): lax.all_gather(sets_weights.astype(bf).reshape(-1, width), 'dev', axis=0,...]
  transfers between devices with their start and end apart: 4 -> 4, of which waited for: 3 -> 4; matrix products, arithmetic and copies ran while one was open for 6% -> 4% of each run, Pallas kernels for 0% -> 0%
where the time goes in v1:
time: 725 us; the launch traced here: 720 us
  waiting for transfers between devices  356 us (49%)
  matrix products  91 us (13%)
  local copies, waits for them, and re-layouts  89.1 us (12%)
  blocking collectives  74.1 us (10%)
  other arithmetic  55.4 us (8%)
  Pallas kernels  33.8 us (5%)
  between operations  15.2 us (2%)
    reduce_scatter x1, waiting for transfers between devices, local(): lax.psum_scatter(full, 'dev', scatter_dimension=0, tiled=True).astype(f32)  222 us
    all_gather x1, waiting for transfers between devices, local(): lax.all_gather(sets_weights.astype(bf).reshape(-1, width), 'dev', axis=0,...  114 us
    dot_general x12, matrix products, mm(): lax.dot_general(left, right, (dims, ((), ())), preferred_element_type=jnp...  78.3 us
    all_gather x1, blocking collectives, local(): lax.all_gather(small, 'dev', axis=0, tiled=False).reshape(devices, -1)  44.3 us
    concatenate x1, other arithmetic, local(): jnp.concatenate([dq1.reshape(-1, width), do1, du1.reshape(-1, width), dd1])  35.3 us
    pallas_call x1, Pallas kernels, rows_layer(): pl.pallas_call(rows_kernel, grid=(steps,), in_specs=[pl.BlockSpec((1, 1,...  33.8 us
    all_to_all x1, blocking collectives, local(): lax.all_to_all(payload, 'dev', split_axis=0, concat_axis=0, tiled=True)  29.8 us
    all_to_all x1, waiting for transfers between devices, local(): lax.all_to_all(outgoing, 'dev', split_axis=0, concat_axis=0, tiled=True)  17.6 us
  transfers between devices with their start and end apart: 4, of which 4 were waited for; matrix products, arithmetic and copies ran while one was open for 4% of the time, Pallas kernels for 0%

profile of v1, /device:TPU:0, one launch (start us, length us, event | category | flops | bytes accessed | tf_op | source)
XLA Modules:
  0.0 720.2 jit_solution(5382383329430192540)
XLA Ops:
  7.3 1.6 convert_element_type.126
  8.8 1.2 reshape.280
  10.3 44.3 %all_gather.6 = bf16[32,2,1024]{2,1,0:T(2,128)(2,1)S(1)} all-gather(bf16[1,2,1024]{2,1,0:T(2,128)(2,1)S(1)} %all_gather_reshape.3), channel_id=1, replica_groups=mesh['dev'=32] {'dev'}, dimensions={0}, use_global_device_ids=true | all-gather | bytes 135168 | tf_op jit(solution)/shard_map/all_gather | solution.py:316
  55.6 113.6 %all-gather.2.cloned.1.call-done = bf16[12288,1024]{1,0:T(8,128)(2,1)} async-done(((bf16[384,1024]{1,0:T(8,128)(2,1)}), bf16[12288,1024]{1,0:T(8,128)(2,1)}) %all-gather.2.cloned.1.call-update) | async-done | bytes 25165840 | tf_op jit(solution)/shard_map/all_gather | solution.py:319
  169.3 6.2 slice.100
  175.5 10.5 %reshape.281 = bf16[1024,3072]{1,0:T(8,128)(2,1)} reshape(bf16[3072,1024]{1,0:T(8,128)(2,1)} %slice.100) | data formatting | bytes 12582912 | tf_op jit(solution)/shard_map/reshape | solution.py:320
  186.0 5.8 fusion.22
  192.9 1.4 copy.165
  195.1 1.5 fusion.75
  197.3 1.4 copy-done.9
  198.7 3.0 fusion.76
  202.1 7.6 %slice.106 = bf16[4096,1024]{1,0:T(8,128)(2,1)} slice(bf16[12288,1024]{1,0:T(8,128)(2,1)} %all-gather.2.cloned.1.call-done), slice={[4096:8192], [0:1024]} | slice | bytes 16777216 | tf_op jit(solution)/shard_map/slice | solution.py:322
  209.6 13.9 %reshape.284 = bf16[1024,4096]{1,0:T(8,128)(2,1)} reshape(bf16[4096,1024]{1,0:T(8,128)(2,1)} %slice.106) | data formatting | bytes 16777216 | tf_op jit(solution)/shard_map/reshape | solution.py:322
  223.5 11.4 %multiply_convert_fusion.1 = (bf16[384,4096]{1,0:T(8,128)(2,1)S(1)}, f32[384,4096]{1,0:T(8,128)}) fusion(bf16[1024,4096]{1,0:T(8,128)(2,1)} %reshape.284, f32[384,1024]{1,0:T(8,128)S(1)} %get-tuple-element.63, f32[1024]{0:T(1024)S(1)} %get-tuple-element.58, f32[384]{0:T(512)S(1)} %add_rsqrt_fusion, f32[384]{0:T(512)S(1)} %broadcast_multiply_fusion.4), kind=kOutput, calls=%fused_computation.12 | convolution fusion | flops 3257401344 | bytes 19405824 | tf_op jit(solution)/shard_map/dot_general | solution.py:24
  235.0 7.1 add_convert_fusion
  242.1 1.4 copy.185
  243.5 2.8 all-to-all-start
  252.3 2.1 pad.13.og_ref
  254.9 17.6 %all-to-all-done = bf16[32,12,1024]{2,1,0:T(8,128)(2,1)S(1)} async-done(((bf16[32,12,1024]{2,1,0:T(8,128)(2,1)}), bf16[32,12,1024]{2,1,0:T(8,128)(2,1)S(1)}, u32[]{:S(2)}, u32[]{:S(2)}) %all-to-all-start) | async-done | bytes 786464 | tf_op jit(solution)/shard_map/all_to_all | solution.py:364
  272.5 1.1 reshape.286.arrived_ref
  273.6 33.8 %shard_map.251 = (bf16[384,1024]{1,0:T(8,128)(2,1)}, bf16[384,1024]{1,0:T(8,128)(2,1)}, f32[64,192]{1,0:T(8,128)}, f32[64,64]{1,0:T(8,128)}, f32[64,256]{1,0:T(8...) custom-call(s32[3,1,128]{2,1,0:T(1,128)} %compare_select_fusion.pick_ref, ...), custom_call_target="tpu_custom_call" | custom-call | tf_op jit(solution)/shard_map/pallas_call | solution.py:199
  310.2 0.9 convert.33
  312.5 29.8 %all_to_all.15 = bf16[32,14,1024]{2,1,0:T(8,128)(2,1)S(1)} all-to-all(bf16[32,14,1024]{2,1,0:T(8,128)(2,1)S(1)} %pad_maximum_fusion.2), channel_id=1, replica_groups=mesh['dev'=32] {'dev'}, dimensions={0} | all-to-all | bytes 1835008 | tf_op jit(solution)/shard_map/all_to_all | solution.py:374
  342.4 1.0 copy-done.8
  343.9 11.7 %multiply_convert_fusion = bf16[384,4096]{1,0:T(8,128)(2,1)S(1)} fusion(f32[384,4096]{1,0:T(8,128)} %get-tuple-element.65, bf16[384,1024]{1,0:T(8,128)(2,1)S(1)} %bitcast.103, bf16[12288,1024]{1,0:T(8,128)(2,1)} %all-gather.2.cloned.1.call-done), kind=kOutput, calls=%fused_computation.11 | convolution fusion | flops 3260547072 | bytes 18612224 | tf_op jit(solution)/shard_map/dot_general | solution.py:24
  355.7 3.8 multiply_reduce_fusion.1
  360.6 2.6 convolution_convert_fusion.4
  363.3 3.5 fusion.38
  366.8 2.3 copy.170
  369.1 4.5 convolution_convert_fusion.5
  373.5 3.3 multiply_reduce_fusion
  378.0 1.8 multiply_convert_fusion.3
  379.8 1.6 multiply_convert_fusion.4
  382.0 7.3 %convolution_convert_fusion.1 = bf16[1024,4096]{1,0:T(8,128)(2,1)} fusion(bf16[384,4096]{1,0:T(8,128)(2,1)S(1)} %copy-done.45, f32[384,1024]{1,0:T(8,128)S(1)} %get-tuple-element.63, f32[1024]{0:T(1024)S(1)} %get-tuple-element.58, f32[384]{0:T(512)S(1)} %copy-done.35, f32[384]{0:T(512)S(1)} %broadcast_multiply_fusion.4), kind=kOutput, calls=%fused_computation.5 | convolution fusion | flops 3226992640 | bytes 13114368 | tf_op jit(solution)/shard_map/dot_general | solution.py:24
  389.2 6.8 convolution_convert_fusion
  396.0 14.0 %reshape.300 = bf16[4096,1024]{1,0:T(8,128)(2,1)} reshape(bf16[1024,4096]{1,0:T(8,128)(2,1)} %convolution_convert_fusion.1) | data formatting | bytes 16777216 | tf_op jit(solution)/shard_map/reshape | solution.py:398
  410.1 7.2 convolution_convert_fusion.2
  417.2 10.4 %reshape.299 = bf16[3072,1024]{1,0:T(8,128)(2,1)} reshape(bf16[1024,3072]{1,0:T(8,128)(2,1)} %convolution_convert_fusion.2) | data formatting | bytes 12582912 | tf_op jit(solution)/shard_map/reshape | solution.py:398
  427.6 35.3 %pad_maximum_fusion = bf16[12288,1024]{1,0:T(8,128)(2,1)} fusion(bf16[4096,1024]{1,0:T(8,128)(2,1)} %convolution_convert_fusion, bf16[4096,1024]{1,0:T(8,128)(2,1)} %reshape.300, bf16[1024,1024]{1,0:T(8,128)(2,1)} %convolution_convert_fusion.4, bf16[3072,1024]{1,0:T(8,128)(2,1)} %reshape.299), kind=kLoop, calls=%fused_computation.1 | loop fusion | flops 100663296 | bytes 50331648 | tf_op jit(solution)/shard_map/concatenate | solution.py:398
  463.0 2.0 slice.94
  465.2 1.2 slice.116
  466.5 8.1 %fusion.28 = (f32[1024]{0:T(1024)S(1)}, f32[384]{0:T(512)S(1)}, f32[384]{0:T(512)S(1)}, f32[384,1024]{1,0:T(8,128)}) fusion(bf16[384,1024]{1,0:T(8,128)(2,1)S(1)} %copy-done.1, f32[384]{0:T(512)S(1)} %copy-done.33, f32[384]{0:T(512)S(1)} %broadcast_multiply_fusion.5, f32[1024]{0:T(1024)S(1)} %get-tuple-element.59, bf16[1024,3072]{1,0:T(8,128)(2,1)} %reshape.281, ...), kind=kOutput, calls=%fused_computation.51 | convolution fusion | flops 2426533888 | bytes 11024384 | tf_op jit(solution)/shard_map/dot_general | solution.py:24
  475.4 2.9 all-to-all-start.2
  478.4 3.3 fusion.27
  482.4 3.0 all-to-all-done.2
  486.0 221.6 %reduce-scatter.2.cloned.1.call-done = bf16[384,1024]{1,0:T(8,128)(2,1)} async-done(((bf16[12288,1024]{1,0:T(8,128)(2,1)}), bf16[384,1024]{1,0:T(8,128)(2,1)}) %reduce-scatter.2.cloned.1.call-update) | async-done | bytes 786448 | tf_op jit(solution)/shard_map/reduce_scatter | solution.py:399
  707.6 1.4 convert_bitcast_fusion
  709.4 3.7 fusion.71
  (191 shorter events, 20.8 us)
Async XLA Ops:
  7.2 2.9 copy-start.40
  7.2 2.9 copy-start.25
  7.2 2.9 copy-start.39
  7.2 47.7 %copy-start = (bf16[384,1024]{1,0:T(8,128)(2,1)S(1)}, bf16[384,1024]{1,0:T(8,128)(2,1)}, u32[]{:S(2)}) copy-start(bf16[384,1024]{1,0:T(8,128)(2,1)} %param.12) | copy-start | bytes 2359300
  7.2 162.0 %all-gather.2.cloned.1.call-start = ((), (), s32[]{:S(2)}) async-start(), calls=%async_computation.4 | async-start | bytes 25952256 | tf_op jit(solution)/shard_map/all_gather | solution.py:319
  55.5 130.6 %copy-start.32 = (f32[384]{0:T(512)}, f32[384]{0:T(512)S(1)}, u32[]{:S(2)}) copy-start(f32[384]{0:T(512)S(1)} %add_rsqrt_fusion.1) | copy-start | bytes 4612
  192.9 2.2 copy-start.2
  192.9 2.2 copy-start.4
  196.6 2.1 copy-start.9
  198.7 3.0 copy-start.12
  202.0 21.5 %copy-start.34 = (f32[384]{0:T(512)}, f32[384]{0:T(512)S(1)}, u32[]{:S(2)}) copy-start(f32[384]{0:T(512)S(1)} %add_rsqrt_fusion) | copy-start | bytes 4612
  235.0 7.1 copy-start.46
  243.5 29.0 %all-to-all-start = ((bf16[32,12,1024]{2,1,0:T(8,128)(2,1)}), bf16[32,12,1024]{2,1,0:T(8,128)(2,1)S(1)}, u32[]{:S(2)}, u32[]{:S(2)}) async-start(bf16[32,12,1024]{2,1,0:T(8,128)(2,1)} %bitcast.102), calls=%async_computation | async-start | bytes 2097152 | tf_op jit(solution)/shard_map/all_to_all | solution.py:364
  246.3 461.3 %reduce-scatter.2.cloned.1.call-start = ((), (), s32[]{:S(2)}) async-start(), calls=%async_computation.5 | async-start | bytes 25952256 | tf_op jit(solution)/shard_map/reduce_scatter | solution.py:399
  248.7 24.9 %copy-start.23 = (bf16[64,256]{1,0:T(8,128)(2,1)}, bf16[64,256]{1,0:T(8,128)(2,1)S(1)}, u32[]{:S(2)}) copy-start(bf16[64,256]{1,0:T(8,128)(2,1)S(1)} %slice.111.wu_ref) | copy-start | bytes 98308
  249.4 24.2 %copy-start.21 = (bf16[256,64]{1,0:T(8,128)(2,1)}, bf16[256,64]{1,0:T(8,128)(2,1)S(1)}, u32[]{:S(2)}) copy-start(bf16[256,64]{1,0:T(8,128)(2,1)S(1)} %slice.112.wd_ref) | copy-start | bytes 98308
  250.1 23.5 %copy-start.24 = (bf16[8,8,64]{2,1,0:T(8,128)(2,1)}, bf16[8,8,64]{2,1,0:T(8,128)(2,1)S(1)}, u32[]{:S(2)}) copy-start(bf16[8,8,64]{2,1,0:T(8,128)(2,1)S(1)} %copy.187) | copy-start | bytes 24580
  251.6 22.0 %copy-start.22 = (bf16[64,3,8,8]{0,3,2,1:T(8,128)(2,1)}, bf16[64,3,8,8]{0,3,2,1:T(8,128)(2,1)S(1)}, u32[]{:S(2)}) copy-start(bf16[64,3,8,8]{0,3,2,1:T(8,128)(2,1)S(1)} %copy.135) | copy-start | bytes 73732
  307.4 4.7 copy-start.16
  343.3 12.3 %slice-start = ((s8[8388608]{0:T(1024)(128)(4,1)}), s8[4194304]{0:T(1024)(128)(4,1)S(1)}, s32[]{:S(2)}) async-start(s8[8388608]{0:T(1024)(128)(4,1)} %bitcast.96), calls=%async_computation.6 | async-start | bytes 8388608
  343.9 15.6 %copy-start.10 = (bf16[12,32,1024]{2,1,0:T(8,128)(2,1)}, bf16[12,32,1024]{2,1,0:T(8,128)(2,1)S(1)}, u32[]{:S(2)}) copy-start(bf16[12,32,1024]{2,1,0:T(8,128)(2,1)S(1)} %copy.148) | copy-start | bytes 2359300
  343.9 11.7 %slice-start.1 = ((s8[8388608]{0:T(1024)(128)(4,1)}), s8[4194304]{0:T(1024)(128)(4,1)S(1)}, s32[]{:S(2)}) async-start(s8[8388608]{0:T(1024)(128)(4,1)} %bitcast.96), calls=%async_computation.7 | async-start | bytes 8388608
  343.9 11.7 %copy-start.35 = (f32[384]{0:T(512)S(1)}, f32[384]{0:T(512)}, u32[]{:S(2)}) copy-start(f32[384]{0:T(512)} %copy-done.34) | copy-start | bytes 4612
  355.6 3.8 copy-start.44
  363.3 5.8 copy-start.31
  369.1 4.5 copy-start.18
  369.1 4.5 copy-start.19
  369.1 7.8 %slice-start.2 = ((s8[4718592]{0:T(1024)(128)(4,1)}), s8[4194304]{0:T(1024)(128)(4,1)S(1)}, s32[]{:S(2)}) async-start(s8[4718592]{0:T(1024)(128)(4,1)} %bitcast.100), calls=%async_computation.8 | async-start | bytes 8388608
  373.5 3.3 slice-start.3
  379.8 2.2 copy-start.45
  382.0 7.3 %copy-start.11 = (bf16[12,32,1024]{2,1,0:T(8,128)(2,1)S(1)}, bf16[12,32,1024]{2,1,0:T(8,128)(2,1)}, u32[]{:S(2)}) copy-start(bf16[12,32,1024]{2,1,0:T(8,128)(2,1)} %copy-done.10) | copy-start | bytes 2359300
  382.0 7.3 %copy-start.47 = (bf16[384,4096]{1,0:T(8,128)(2,1)S(1)}, bf16[384,4096]{1,0:T(8,128)(2,1)}, u32[]{:S(2)}) copy-start(bf16[384,4096]{1,0:T(8,128)(2,1)} %copy-done.46) | copy-start | bytes 9437188
  396.0 14.0 %copy-start.1 = (bf16[384,1024]{1,0:T(8,128)(2,1)S(1)}, bf16[384,1024]{1,0:T(8,128)(2,1)}, u32[]{:S(2)}) copy-start(bf16[384,1024]{1,0:T(8,128)(2,1)} %param.12) | copy-start | bytes 2359300
  396.0 14.0 %copy-start.20 = (bf16[8,128,384]{2,1,0:T(8,128)(2,1)S(1)}, bf16[8,128,384]{2,1,0:T(8,128)(2,1)}, u32[]{:S(2)}) copy-start(bf16[8,128,384]{2,1,0:T(8,128)(2,1)} %multiply_convert_fusion.3) | copy-start | bytes 2359300
  396.0 14.0 %copy-start.33 = (f32[384]{0:T(512)S(1)}, f32[384]{0:T(512)}, u32[]{:S(2)}) copy-start(f32[384]{0:T(512)} %copy-done.32) | copy-start | bytes 4612
  462.9 2.2 copy-start.27
  475.4 10.0 %all-to-all-start.2 = ((f32[32,1,68]{2,1,0:T(1,128)}), f32[32,1,68]{2,1,0:T(1,128)S(1)}, u32[]{:S(2)}, u32[]{:S(2)}) async-start(f32[32,1,68]{2,1,0:T(1,128)} %reshape.304), calls=%async_computation.3 | async-start | bytes 32768 | tf_op jit(solution)/shard_map/all_to_all | solution.py:401
  478.3 3.4 copy-start.29
  478.4 3.4 copy-start.26
  478.4 3.4 copy-start.36
  478.4 3.4 copy-start.37
  478.4 7.0 copy-start.41
  478.4 7.0 copy-start.42
  478.4 7.0 copy-start.43
  485.4 223.9 %copy-start.38 = (f32[68]{0:T(128)}, f32[68]{0:T(128)S(1)}, u32[]{:S(2)}) copy-start(f32[68]{0:T(128)S(1)} %reduce_sum.222) | copy-start | bytes 820
  486.0 223.4 %copy-start.6 = (f32[393216]{0:T(1024)S(1)}, f32[393216]{0:T(1024)}, u32[]{:S(2)}) copy-start(f32[393216]{0:T(1024)} %param.14) | copy-start | bytes 4718596
  486.0 223.4 %copy-start.14 = (f32[393216]{0:T(1024)S(1)}, f32[393216]{0:T(1024)}, u32[]{:S(2)}) copy-start(f32[393216]{0:T(1024)} %param.17) | copy-start | bytes 4718596
  709.4 3.7 copy-start.7
  (8 other events, 12.6 us)
Sparse Core Ops, SparseCore 0:
  11.5 157.7 all-gather.1
  463.1 244.4 reduce-scatter.1

commit v2 on v1

--- a/solution.py
+++ b/solution.py
@@ -2,6 +2,7 @@
 
 import jax
 import jax.numpy as jnp
+import numpy as np
 from jax import lax
 from jax.experimental import pallas as pl
 from jax.experimental.pallas import tpu as pltpu
@@ -243,6 +244,91 @@
     return rows_out, back, dwq, dwo, dwu, dwd, jnp.sum(dg3, axis=1), jnp.sum(dg4, axis=1)
 
 
+def flipped(bit):
+    return [(d, d ^ bit) for d in range(32)]
+
+
+def along_z(*moves):
+    return [(src * 8 + i, dst * 8 + i) for src, dst in moves for i in range(8)]
+
+
+CORE, SIDE_X, SIDE_Y = flipped(1), flipped(2), flipped(4)
+CHAINS = (
+    (((3, 2),), ((2, 1),), ((1, 0),)),
+    (((3, 2), (0, 1)), ((2, 1),)),
+    (((0, 1), (3, 2)), ((1, 2),)),
+    (((0, 1),), ((1, 2),), ((2, 3),)),
+)
+
+
+def send(v, pairs):
+    return lax.ppermute(v, "dev", pairs)
+
+
+def plane_sum(group, spot):
+    f32, bf = jnp.float32, jnp.bfloat16
+    half = group.shape[1] // 2
+    block = lambda i: lax.dynamic_index_in_dim(group, i, 0, keepdims=False)
+    far, side, other = block(spot ^ 3), block(spot ^ 1), block(spot ^ 2)
+    from_x = send(far[:half], SIDE_X)
+    from_y = send(far[half:], SIDE_Y)
+    side = jnp.concatenate([side[:half], (side[half:].astype(f32) + from_y.astype(f32)).astype(bf)])
+    other = jnp.concatenate([(other[:half].astype(f32) + from_x.astype(f32)).astype(bf), other[half:]])
+    return block(spot).astype(f32) + send(side, SIDE_X).astype(f32) + send(other, SIDE_Y).astype(f32)
+
+
+def chain_sum(share, plane):
+    for moves in CHAINS[plane]:
+        share = share + send(share.astype(jnp.bfloat16), along_z(*moves)).astype(jnp.float32)
+    return share
+
+
+def chip_rows():
+    table = []
+    for chip in range(16):
+        keys = []
+        for flat in range(chip * 768, chip * 768 + 768):
+            if flat < 3072:
+                keys.append((flat % 3, flat // 3))
+            elif flat < 4096 or flat >= 8192:
+                keys.append((0 if flat < 4096 else 9, flat))
+            else:
+                keys.append((1 + flat % 4, flat // 4))
+        order = sorted(range(768), key=lambda i: keys[i])
+        place = [0] * 768
+        for at, i in enumerate(order):
+            place[i] = at
+        table.append(place)
+    return np.array(table, np.int32)
+
+
+def sum_to_owners(groups, device):
+    core, spot, plane = device % 2, device // 2 % 4, device // 8
+    total = None
+    for z in (3, 2, 1, 0):
+        share = chain_sum(plane_sum(groups[z], spot), z)
+        total = share if total is None else jnp.where(plane == z, share, total)
+    order = lax.dynamic_index_in_dim(jnp.asarray(chip_rows()), device // 2, 0, keepdims=False)
+    total = jnp.take(total, order, axis=0)
+    rows, lanes = total.shape[0] // 2, total.shape[1]
+    mine = lax.dynamic_slice_in_dim(total, core * rows, rows, 0)
+    peer = send(lax.dynamic_slice_in_dim(total, (1 - core) * rows, rows, 0), CORE)
+    return jnp.where(core == 0, jnp.concatenate([mine, peer], axis=1), jnp.concatenate([peer, mine], axis=1))
+
+
+def both(v):
+    return jnp.concatenate([v, send(v, CORE)])
+
+
+def both_half(v, core, parts):
+    width = v.shape[1] // parts
+    half = width // 2
+    pick = lambda c: jnp.concatenate(
+        [lax.dynamic_slice_in_dim(v, j * width + c * half, half, 1) for j in range(parts)], axis=1
+    )
+    return jnp.concatenate([pick(core), send(pick(1 - core), CORE)])
+
+
 def fwd_mul(left, right):
     return mm(left, right, ((1,), (0,)))
 
@@ -309,6 +395,7 @@
     rows_pad = -(-rows_even // LANES) * LANES
     head = width // HEADS
     scaling = head ** (-0.5)
+    grid = devices == 32 and width == 1024 and slots == 384
 
     n_rows, n_gains = rows_weights.shape[0], norm_gains.shape[0]
     small = jnp.concatenate([rows_weights, norm_gains]).astype(bf)
@@ -376,13 +463,26 @@
     rows_grad = jnp.sum(returned[:, per_peer:].reshape(devices, -1)[:, :n_rows].astype(f32), axis=0)
 
     gz = grad.astype(bf)
-    dd1 = outer(u1, gz).astype(bf)
+    if grid:
+        core = device % 2
+        a1_both, a2_both, o1_both, u1_both = both(a1), both(a2), both(o1), both(u1)
+        dd1 = outer(u1_both, both_half(gz, core, 1)).astype(bf)
+    else:
+        dd1 = outer(u1, gz).astype(bf)
     dpre = (slope * backmul(gz, wd1)).astype(bf)
-    du1 = outer(a2, dpre).astype(bf)
+    if grid:
+        dpre_half = both_half(dpre, core, 4)
+        half = width // 2
+        du1 = jnp.stack([outer(a2_both, dpre_half[:, j * half : (j + 1) * half]).astype(bf) for j in range(4)])
+    else:
+        du1 = outer(a2, dpre).astype(bf)
     dh, dg2 = norm_pull(hat2, root2, g2, backmul(dpre, wu1))
     grad = grad + dh
     gz = grad.astype(bf)
-    do1 = outer(o1, gz).astype(bf)
+    if grid:
+        do1 = outer(o1_both, both_half(gz, core, 1)).astype(bf)
+    else:
+        do1 = outer(o1, gz).astype(bf)
     dblend = backmul(gz, wo1).astype(bf).reshape(slots, HEADS, head)
     dchance = jnp.einsum("qhd,khd->hqk", dblend, values, preferred_element_type=f32)
     dot = jnp.sum(chance * dchance, axis=-1, keepdims=True)
@@ -391,12 +491,26 @@
     dk = jnp.einsum("hqk,qhd->khd", dscores, queries, preferred_element_type=f32) * scaling
     dv = jnp.einsum("hqk,qhd->khd", chance_low, dblend, preferred_element_type=f32)
     djoined = jnp.concatenate([part.reshape(slots, width).astype(bf) for part in (dq, dk, dv)], axis=1)
-    dq1 = outer(a1, djoined).astype(bf)
+    if grid:
+        dj_half = both_half(djoined, core, 3)
+        dq1 = [outer(a1_both, dj_half[:, j * half : (j + 1) * half]).astype(bf).reshape(4, width // 4, half) for j in range(3)]
+    else:
+        dq1 = outer(a1, djoined).astype(bf)
     dh, dg1 = norm_pull(hat1, root1, g1, backmul(djoined, wq1))
     cells_grad = grad + dh
 
-    full = jnp.concatenate([dq1.reshape(-1, width), do1, du1.reshape(-1, width), dd1])
-    sets_grad = lax.psum_scatter(full, "dev", scatter_dimension=0, tiled=True).astype(f32).reshape(-1)
+    if grid:
+        tall = lambda lo, hi: du1[:, lo:hi].reshape(4 * (hi - lo), half)
+        groups = (
+            jnp.concatenate(dq1, axis=1),
+            jnp.concatenate([do1, tall(0, 128), tall(128, 320), tall(320, 512)]).reshape(4, -1, half),
+            jnp.concatenate([tall(512, 704), tall(704, 896), tall(896, 1024), dd1[:1024]]).reshape(4, -1, half),
+            dd1[1024:].reshape(4, -1, half),
+        )
+        sets_grad = sum_to_owners(groups, device).reshape(-1)
+    else:
+        full = jnp.concatenate([dq1.reshape(-1, width), do1, du1.reshape(-1, width), dd1])
+        sets_grad = lax.psum_scatter(full, "dev", scatter_dimension=0, tiled=True).astype(f32).reshape(-1)
     gains = jnp.concatenate([dg1, dg2, dg3, dg4]).reshape(devices, 1, n_gains)
     gains_grad = jnp.sum(lax.all_to_all(gains, "dev", split_axis=0, concat_axis=0, tiled=True), axis=(0, 1))
 

time: 725 us -> 578 us (0.80)
  waiting for transfers between devices: 356 us -> 224 us
  starting transfers between devices: 5.73 us -> 47.3 us
  blocking collectives: 74.1 us -> 44.3 us
  matrix products: 91 us -> 70.2 us
  local copies, waits for them, and re-layouts: 89.1 us -> 81.1 us
    reduce_scatter x1 -> x0, waiting for transfers between devices: 222 us -> none  [local(): lax.psum_scatter(full, 'dev', scatter_dimension=0, tiled=True).astype(f32)]
    ppermute x0 -> x35, waiting for transfers between devices: none -> 72.1 us  [send(): return lax.ppermute(v, 'dev', pairs)]
    ppermute x0 -> x35, starting transfers between devices: none -> 34.1 us  [send(): return lax.ppermute(v, 'dev', pairs)]
    all_to_all x1 -> x0, blocking collectives: 29.8 us -> none  [local(): lax.all_to_all(payload, 'dev', split_axis=0, concat_axis=0, tiled=True)]
    reshape x2 -> x0, local copies, waits for them, and re-layouts: 24.4 us -> none  [the longest x1 14 us: local(): du1.reshape(-1, width)]
    concatenate x1 -> x16, other arithmetic: 35.3 us -> 11.9 us  [the longest x2 10 us: both_half(): return jnp.concatenate([pick(core), send(pick(1 - core), CORE)])]
    all_to_all x0 -> x1, waiting for transfers between devices: none -> 20.7 us  [local(): lax.all_to_all(payload, 'dev', split_axis=0, concat_axis=0, tiled=True)]
    dot_general x12 -> x17, matrix products: 78.3 us -> 61 us  [mm(): lax.dot_general(left, right, (dims, ((), ())), preferred_element_type=jnp...]
  transfers between devices with their start and end apart: 4 -> 39, of which waited for: 4 -> 15; matrix products, arithmetic and copies ran while one was open for 4% -> 18% of each run, Pallas kernels for 0% -> 0%
where the time goes in v2:
time: 578 us; the launch traced here: 572 us
  waiting for transfers between devices  224 us (39%)
  local copies, waits for them, and re-layouts  81.1 us (14%)
  matrix products  70.2 us (12%)
  other arithmetic  55.9 us (10%)
  starting transfers between devices  47.3 us (8%)
  blocking collectives  44.3 us (8%)
  Pallas kernels  33.8 us (6%)
  between operations  16.2 us (3%)
    all_gather x1, waiting for transfers between devices, local(): lax.all_gather(sets_weights.astype(bf).reshape(-1, width), 'dev', axis=0,...  113 us
    ppermute x35, waiting for transfers between devices, send(): return lax.ppermute(v, 'dev', pairs)  72.1 us
    dot_general x17, matrix products, mm(): lax.dot_general(left, right, (dims, ((), ())), preferred_element_type=jnp...  61 us
    all_gather x1, blocking collectives, local(): lax.all_gather(small, 'dev', axis=0, tiled=False).reshape(devices, -1)  44.3 us
    ppermute x35, starting transfers between devices, send(): return lax.ppermute(v, 'dev', pairs)  34.1 us
    pallas_call x1, Pallas kernels, rows_layer(): pl.pallas_call(rows_kernel, grid=(steps,), in_specs=[pl.BlockSpec((1, 1,...  33.8 us
    all_to_all x1, waiting for transfers between devices, local(): lax.all_to_all(payload, 'dev', split_axis=0, concat_axis=0, tiled=True)  20.7 us
    all_to_all x1, waiting for transfers between devices, local(): lax.all_to_all(outgoing, 'dev', split_axis=0, concat_axis=0, tiled=True)  17.6 us
  transfers between devices with their start and end apart: 39, of which 15 were waited for; matrix products, arithmetic and copies ran while one was open for 18% of the time, Pallas kernels for 0%

profile of v2, /device:TPU:0, one launch (start us, length us, event | category | flops | bytes accessed | tf_op | source)
XLA Modules:
  0.0 572.5 jit_solution(4681697384285130828)
XLA Ops:
  10.2 44.3 %all_gather.6 = bf16[32,2,1024]{2,1,0:T(2,128)(2,1)S(1)} all-gather(bf16[1,2,1024]{2,1,0:T(2,128)(2,1)S(1)} %all_gather_reshape.3), channel_id=1, replica_groups=mesh['dev'=32] {'dev'}, dimensions={0}, use_global_device_ids=true | all-gather | bytes 135168 | tf_op jit(solution)/shard_map/all_gather | solution.py:403
  55.9 113.4 %all-gather.2.cloned.1.call-done = bf16[12288,1024]{1,0:T(8,128)(2,1)} async-done(((bf16[384,1024]{1,0:T(8,128)(2,1)}), bf16[12288,1024]{1,0:T(8,128)(2,1)}) %all-gather.2.cloned.1.call-update) | async-done | bytes 25165840 | tf_op jit(solution)/shard_map/all_gather | solution.py:406
  169.3 6.1 %slice.330 = bf16[3072,1024]{1,0:T(8,128)(2,1)} slice(bf16[12288,1024]{1,0:T(8,128)(2,1)} %all-gather.2.cloned.1.call-done), slice={[0:3072], [0:1024]} | slice | bytes 12582912 | tf_op jit(solution)/shard_map/slice | solution.py:407
  175.4 10.6 %reshape.392 = bf16[1024,3072]{1,0:T(8,128)(2,1)} reshape(bf16[3072,1024]{1,0:T(8,128)(2,1)} %slice.330) | data formatting | bytes 12582912 | tf_op jit(solution)/shard_map/reshape | solution.py:407
  186.0 5.6 fusion.29
  196.3 2.1 convolution_convert_fusion.9
  198.7 2.9 fusion.132
  201.9 7.6 %slice.336 = bf16[4096,1024]{1,0:T(8,128)(2,1)} slice(bf16[12288,1024]{1,0:T(8,128)(2,1)} %all-gather.2.cloned.1.call-done), slice={[4096:8192], [0:1024]} | slice | bytes 16777216 | tf_op jit(solution)/shard_map/slice | solution.py:409
  209.6 13.9 %reshape.395 = bf16[1024,4096]{1,0:T(8,128)(2,1)} reshape(bf16[4096,1024]{1,0:T(8,128)(2,1)} %slice.336) | data formatting | bytes 16777216 | tf_op jit(solution)/shard_map/reshape | solution.py:409
  223.9 12.0 %multiply_convert_fusion.1 = (bf16[384,4096]{1,0:T(8,128)(2,1)S(1)}, f32[384,4096]{1,0:T(8,128)}) fusion(bf16[384,1024]{1,0:T(8,128)(2,1)S(1)} %multiply_convert_fusion.5, bf16[1024,4096]{1,0:T(8,128)(2,1)} %reshape.395), kind=kOutput, calls=%fused_computation.14 | convolution fusion | flops 3255828480 | bytes 18612224 | tf_op jit(solution)/shard_map/dot_general | solution.py:25
  236.8 3.5 add_convert_fusion
  241.7 3.4 all-to-all-start
  251.0 2.1 pad.13.og_ref
  253.6 17.6 %all-to-all-done = bf16[32,12,1024]{2,1,0:T(8,128)(2,1)} async-done(((bf16[32,12,1024]{2,1,0:T(8,128)(2,1)}), bf16[32,12,1024]{2,1,0:T(8,128)(2,1)}, u32[]{:S(2)}, u32[]{:S(2)}) %all-to-all-start) | async-done | bytes 786464 | tf_op jit(solution)/shard_map/all_to_all | solution.py:451
  271.3 2.1 reshape.397.arrived_ref
  273.4 33.8 %shard_map.260 = (bf16[384,1024]{1,0:T(8,128)(2,1)}, bf16[384,1024]{1,0:T(8,128)(2,1)}, f32[64,192]{1,0:T(8,128)}, f32[64,64]{1,0:T(8,128)}, f32[64,256]{1,0:T(8...) custom-call(s32[3,1,128]{2,1,0:T(1,128)} %compare_select_fusion.2.pick_ref, ...), custom_call_target="tpu_custom_call" | custom-call | tf_op jit(solution)/shard_map/pallas_call | solution.py:200
  311.7 2.1 reshape.402
  313.9 2.5 pad_maximum_fusion.10
  316.3 3.7 all-to-all-start.1
  325.5 20.7 %all-to-all-done.1 = bf16[32,14,1024]{2,1,0:T(8,128)(2,1)} async-done(((bf16[32,14,1024]{2,1,0:T(8,128)(2,1)}), bf16[32,14,1024]{2,1,0:T(8,128)(2,1)}, u32[]{:S(2)}, u32[]{:S(2)}) %all-to-all-start.1) | async-done | bytes 917536 | tf_op jit(solution)/shard_map/all_to_all | solution.py:461
  348.1 11.4 %multiply_convert_fusion = bf16[384,4096]{1,0:T(8,128)(2,1)S(1)} fusion(f32[384,4096]{1,0:T(8,128)} %get-tuple-element.117, bf16[384,1024]{1,0:T(8,128)(2,1)S(1)} %bitcast.250, bf16[12288,1024]{1,0:T(8,128)(2,1)} %all-gather.2.cloned.1.call-done), kind=kOutput, calls=%fused_computation.13 | convolution fusion | flops 3260547072 | bytes 18612224 | tf_op jit(solution)/shard_map/dot_general | solution.py:25
  359.6 3.8 multiply_reduce_fusion.1
  364.4 1.8 fusion.128
  367.0 2.6 fusion.57
  370.8 3.8 multiply_reduce_fusion
  382.2 5.6 fusion.10
  393.0 2.3 fusion.50
  395.4 3.9 collective-permute-done.27
  408.8 9.9 %pad_maximum_fusion.1 = bf16[768,2048]{1,0:T(8,128)(2,1)S(1)} fusion(bf16[384,2048]{1,0:T(8,128)(2,1)S(1)} %collective-permute-done.12, bf16[384,512]{1,0:T(8,128)(2,1)S(1)} %get-tuple-element.84, bf16[384,512]{1,0:T(8,128)(2,1)S(1)} %get-tuple-element.85, bf16[384,512]{1,0:T(8,128)(2,1)S(1)} %get-tuple-element.86, bf16[384,512]{1,0:T(8,128)(2,1)S(1)} %get-tuple-element.79), kind=kLoop, calls=%fused_computation.27 | loop fusion | flops 15728640 | bytes 6291456 | tf_op jit(solution)/shard_map/concatenate | solution.py:329
  422.8 1.7 pad_maximum_fusion.14
  424.9 2.6 collective-permute-start.31
  433.0 7.2 %collective-permute-done.21 = bf16[384,512]{1,0:T(8,128)(2,1)S(1)} collective-permute-done((bf16[384,512]{1,0:T(8,128)(2,1)S(1)}, bf16[384,512]{1,0:T(8,128)(2,1)S(1)}, u32[]{:S(2)}, u32[]{:S(2)}) %collective-permute-start.21) | collective-permute-done | bytes 393248 | tf_op jit(solution)/shard_map/ppermute | solution.py:265
  443.0 5.7 collective-permute-done.13
  451.4 14.1 %collective-permute-done.5 = bf16[768,512]{1,0:T(8,128)(2,1)S(1)} collective-permute-done((bf16[768,512]{1,0:T(8,128)(2,1)S(1)}, bf16[768,512]{1,0:T(8,128)(2,1)S(1)}, u32[]{:S(2)}, u32[]{:S(2)}) %collective-permute-start.5) | collective-permute-done | bytes 786464 | tf_op jit(solution)/shard_map/ppermute | solution.py:265
  469.4 13.0 %collective-permute-done.24 = bf16[768,512]{1,0:T(8,128)(2,1)S(1)} collective-permute-done((bf16[768,512]{1,0:T(8,128)(2,1)S(1)}, bf16[768,512]{1,0:T(8,128)(2,1)S(1)}, u32[]{:S(2)}, u32[]{:S(2)}) %collective-permute-start.24) | collective-permute-done | bytes 786464 | tf_op jit(solution)/shard_map/ppermute | solution.py:265
  483.6 2.4 collective-permute-start.25
  486.0 10.4 %collective-permute-done.16 = bf16[768,512]{1,0:T(8,128)(2,1)S(1)} collective-permute-done((bf16[768,512]{1,0:T(8,128)(2,1)S(1)}, bf16[768,512]{1,0:T(8,128)(2,1)S(1)}, u32[]{:S(2)}, u32[]{:S(2)}) %collective-permute-start.16) | collective-permute-done | bytes 786464 | tf_op jit(solution)/shard_map/ppermute | solution.py:265
  497.6 2.0 collective-permute-start.17
  506.4 11.0 %collective-permute-done.17 = bf16[768,512]{1,0:T(8,128)(2,1)S(1)} collective-permute-done((bf16[768,512]{1,0:T(8,128)(2,1)S(1)}, bf16[768,512]{1,0:T(8,128)(2,1)S(1)}, u32[]{:S(2)}, u32[]{:S(2)}) %collective-permute-start.17) | collective-permute-done | bytes 786464 | tf_op jit(solution)/shard_map/ppermute | solution.py:265
  518.7 1.7 collective-permute-start.18
  523.4 4.1 fusion.35
  529.5 6.1 %all-to-all-start.2 = ((f32[32,1,68]{2,1,0:T(1,128)}), f32[32,1,68]{2,1,0:T(1,128)S(1)}, u32[]{:S(2)}, u32[]{:S(2)}) async-start(f32[32,1,68]{2,1,0:T(1,128)} %reshape.423), calls=%async_computation.2 | async-start | bytes 32768 | tf_op jit(solution)/shard_map/all_to_all | solution.py:515
  536.9 4.3 collective-permute-done.8
  541.1 7.9 %select_select_fusion = f32[768,512]{1,0:T(8,128)S(1)} fusion(bf16[768,512]{1,0:T(8,128)(2,1)} %copy-done.31, bf16[768,512]{1,0:T(8,128)(2,1)} %copy-done.32, bf16[768,512]{1,0:T(8,128)(2,1)} %collective-permute-done.18, bf16[768,512]{1,0:T(8,128)(2,1)} %collective-permute-done.8, bf16[768,512]{1,0:T(8,128)(2,1)} %copy-done.25, ...), kind=kLoop, calls=%fused_computation.83 | loop fusion | flops 16908288 | bytes 18874376 | tf_op jit(solution)/shard_map/jit(_where)/select_n | solution.py:310
  549.1 3.1 gather_fusion
  552.2 1.6 broadcast_select_fusion
  555.7 1.7 fusion.34
  561.7 3.7 fusion.126
  (380 shorter events, 97.1 us)
Async XLA Ops:
  7.2 162.1 %all-gather.2.cloned.1.call-start = ((), (), s32[]{:S(2)}) async-start(), calls=%async_computation.3 | async-start | bytes 25952256 | tf_op jit(solution)/shard_map/all_gather | solution.py:406
  55.0 120.4 %copy-start.49 = (f32[384]{0:T(512)}, f32[384]{0:T(512)S(1)}, u32[]{:S(2)}) copy-start(f32[384]{0:T(512)S(1)} %broadcast_multiply_fusion.5) | copy-start | bytes 4612
  55.4 120.0 %copy-start.56 = (f32[384]{0:T(512)}, f32[384]{0:T(512)S(1)}, u32[]{:S(2)}) copy-start(f32[384]{0:T(512)S(1)} %add_rsqrt_fusion.1) | copy-start | bytes 4612
  55.4 120.0 %copy-start.47 = (f32[1024]{0:T(1024)}, f32[1024]{0:T(1024)S(1)}, u32[]{:S(2)}) copy-start(f32[1024]{0:T(1024)S(1)} %get-tuple-element.111) | copy-start | bytes 12292
  55.9 130.1 %copy-start.33 = (bf16[384,1024]{1,0:T(8,128)(2,1)}, bf16[384,1024]{1,0:T(8,128)(2,1)S(1)}, u32[]{:S(2)}) copy-start(bf16[384,1024]{1,0:T(8,128)(2,1)S(1)} %fusion.30) | copy-start | bytes 2359300
  241.7 29.6 %all-to-all-start = ((bf16[32,12,1024]{2,1,0:T(8,128)(2,1)}), bf16[32,12,1024]{2,1,0:T(8,128)(2,1)}, u32[]{:S(2)}, u32[]{:S(2)}) async-start(bf16[32,12,1024]{2,1,0:T(8,128)(2,1)} %bitcast.258), calls=%async_computation | async-start | bytes 2097152 | tf_op jit(solution)/shard_map/all_to_all | solution.py:451
  316.3 29.9 %all-to-all-start.1 = ((bf16[32,14,1024]{2,1,0:T(8,128)(2,1)}), bf16[32,14,1024]{2,1,0:T(8,128)(2,1)}, u32[]{:S(2)}, u32[]{:S(2)}) async-start(bf16[32,14,1024]{2,1,0:T(8,128)(2,1)} %pad_maximum_fusion.10), calls=%async_computation.1 | async-start | bytes 2097152 | tf_op jit(solution)/shard_map/all_to_all | solution.py:461
  322.8 58.5 %collective-permute-start.19 = (bf16[384,4096]{1,0:T(8,128)(2,1)}, bf16[384,4096]{1,0:T(8,128)(2,1)}, u32[]{:S(2)}, u32[]{:S(2)}) collective-permute-start(bf16[384,4096]{1,0:T(8,128)(2,1)} %copy-done.70), channel_id=1, source_target_pairs={{0,1},{1,0},{2,3},{3,2},{4,5},{5,4},{6,7},{7,6},{8,9},{9,8},{10,11... | collective-permute-start | bytes 9437192 | tf_op jit(solution)/shard_map/ppermute | solution.py:265
  323.0 68.4 %collective-permute-start.9 = (bf16[384,1024]{0,1:T(8,128)(2,1)}, bf16[384,1024]{0,1:T(8,128)(2,1)}, u32[]{:S(2)}, u32[]{:S(2)}) collective-permute-start(bf16[384,1024]{0,1:T(8,128)(2,1)} %bitcast.5), channel_id=1, source_target_pairs={{0,1},{1,0},{2,3},{3,2},{4,5},{5,4},{6,7},{7,6},{8,9},{9,8},{10,11... | collective-permute-start | bytes 2359304 | tf_op jit(solution)/shard_map/ppermute | solution.py:265
  374.6 6.8 %collective-permute-start.20 = (bf16[384,512]{1,0:T(8,128)(2,1)S(1)}, bf16[384,512]{1,0:T(8,128)(2,1)S(1)}, u32[]{:S(2)}, u32[]{:S(2)}) collective-permute-start(bf16[384,512]{1,0:T(8,128)(2,1)S(1)} %copy-done.44), channel_id=1, source_target_pairs={{0,1},{1,0},{2,3},{3,2},{4,5},{5,4},{6,7},{7,6},{8,9},{9,8},{10,11... | collective-permute-start | bytes 1179656 | tf_op jit(solution)/shard_map/ppermute | solution.py:265
  374.6 17.9 %collective-permute-start.10 = (bf16[384,512]{1,0:T(8,128)(2,1)S(1)}, bf16[384,512]{1,0:T(8,128)(2,1)S(1)}, u32[]{:S(2)}, u32[]{:S(2)}) collective-permute-start(bf16[384,512]{1,0:T(8,128)(2,1)S(1)} %copy-done.42), channel_id=1, source_target_pairs={{0,1},{1,0},{2,3},{3,2},{4,5},{5,4},{6,7},{7,6},{8,9},{9,8},{10,11... | collective-permute-start | bytes 1179656 | tf_op jit(solution)/shard_map/ppermute | solution.py:265
  379.6 21.9 %collective-permute-start.1 = (bf16[384,1536]{0,1:T(8,128)(2,1)S(1)}, bf16[384,1536]{0,1:T(8,128)(2,1)S(1)}, u32[]{:S(2)}, u32[]{:S(2)}) collective-permute-start(bf16[384,1536]{0,1:T(8,128)(2,1)S(1)} %pad_maximum_fusion.9), channel_id=1, source_target_pairs={{0,1},{1,0},{2,3},{3,2},{4,5},{5,4},{6,7},{7,6},{8,9},{9,8},{10,11... | collective-permute-start | bytes 3538952 | tf_op jit(solution)/shard_map/ppermute | solution.py:265
  388.0 112.8 %copy-start = (bf16[3072,512]{1,0:T(8,128)(2,1)}, bf16[3072,512]{1,0:T(8,128)(2,1)S(1)}, u32[]{:S(2)}) copy-start(bf16[3072,512]{1,0:T(8,128)(2,1)S(1)} %slice.354) | copy-start | bytes 9437188
  388.1 11.2 %collective-permute-start.27 = (bf16[384,512]{1,0:T(8,128)(2,1)S(1)}, bf16[384,512]{1,0:T(8,128)(2,1)S(1)}, u32[]{:S(2)}, u32[]{:S(2)}) collective-permute-start(bf16[384,512]{1,0:T(8,128)(2,1)S(1)} %get-tuple-element.88), channel_id=1, source_target_pairs={{0,4},{1,5},{2,6},{3,7},{4,0},{5,1},{6,2},{7,3},{8,12},{9,13},{10,... | collective-permute-start | bytes 1179656 | tf_op jit(solution)/shard_map/ppermute | solution.py:265
  389.7 10.8 %collective-permute-start.29 = (bf16[384,512]{1,0:T(8,128)(2,1)S(1)}, bf16[384,512]{1,0:T(8,128)(2,1)S(1)}, u32[]{:S(2)}, u32[]{:S(2)}) collective-permute-start(bf16[384,512]{1,0:T(8,128)(2,1)S(1)} %get-tuple-element.90), channel_id=1, source_target_pairs={{0,2},{1,3},{2,0},{3,1},{4,6},{5,7},{6,4},{7,5},{8,10},{9,11},{10,... | collective-permute-start | bytes 1179656 | tf_op jit(solution)/shard_map/ppermute | solution.py:265
  392.5 10.7 %collective-permute-start = (bf16[384,1024]{1,0:T(8,128)(2,1)S(1)}, bf16[384,1024]{1,0:T(8,128)(2,1)S(1)}, u32[]{:S(2)}, u32[]{:S(2)}) collective-permute-start(bf16[384,1024]{1,0:T(8,128)(2,1)S(1)} %copy-done.34), channel_id=1, source_target_pairs={{0,1},{1,0},{2,3},{3,2},{4,5},{5,4},{6,7},{7,6},{8,9},{9,8},{10,11... | collective-permute-start | bytes 2359304 | tf_op jit(solution)/shard_map/ppermute | solution.py:265
  392.7 25.9 %collective-permute-start.11 = (bf16[384,1024]{1,0:T(8,128)(2,1)S(1)}, bf16[384,1024]{1,0:T(8,128)(2,1)S(1)}, u32[]{:S(2)}, u32[]{:S(2)}) collective-permute-start(bf16[384,1024]{1,0:T(8,128)(2,1)S(1)} %copy-done.38), channel_id=1, source_target_pairs={{0,1},{1,0},{2,3},{3,2},{4,5},{5,4},{6,7},{7,6},{8,9},{9,8},{10,11... | collective-permute-start | bytes 2359304 | tf_op jit(solution)/shard_map/ppermute | solution.py:265
  399.3 8.9 %collective-permute-start.12 = (bf16[384,2048]{1,0:T(8,128)(2,1)S(1)}, bf16[384,2048]{1,0:T(8,128)(2,1)S(1)}, u32[]{:S(2)}, u32[]{:S(2)}) collective-permute-start(bf16[384,2048]{1,0:T(8,128)(2,1)S(1)} %pad_maximum_fusion.8), channel_id=1, source_target_pairs={{0,1},{1,0},{2,3},{3,2},{4,5},{5,4},{6,7},{7,6},{8,9},{9,8},{10,11... | collective-permute-start | bytes 4718600 | tf_op jit(solution)/shard_map/ppermute | solution.py:265
  400.8 23.7 %collective-permute-start.30 = (bf16[768,512]{1,0:T(8,128)(2,1)S(1)}, bf16[768,512]{1,0:T(8,128)(2,1)S(1)}, u32[]{:S(2)}, u32[]{:S(2)}) collective-permute-start(bf16[768,512]{1,0:T(8,128)(2,1)S(1)} %pad_maximum_fusion.22), channel_id=1, source_target_pairs={{0,4},{1,5},{2,6},{3,7},{4,0},{5,1},{6,2},{7,3},{8,12},{9,13},{10,... | collective-permute-start | bytes 2359304 | tf_op jit(solution)/shard_map/ppermute | solution.py:265
  401.5 23.1 %collective-permute-start.28 = (bf16[768,512]{1,0:T(8,128)(2,1)S(1)}, bf16[768,512]{1,0:T(8,128)(2,1)S(1)}, u32[]{:S(2)}, u32[]{:S(2)}) collective-permute-start(bf16[768,512]{1,0:T(8,128)(2,1)S(1)} %pad_maximum_fusion.21), channel_id=1, source_target_pairs={{0,2},{1,3},{2,0},{3,1},{4,6},{5,7},{6,4},{7,5},{8,10},{9,11},{10,... | collective-permute-start | bytes 2359304 | tf_op jit(solution)/shard_map/ppermute | solution.py:265
  406.6 113.9 %copy-start.1 = (bf16[4,768,512]{2,1,0:T(8,128)(2,1)}, bf16[4,768,512]{2,1,0:T(8,128)(2,1)S(1)}, u32[]{:S(2)}) copy-start(bf16[4,768,512]{2,1,0:T(8,128)(2,1)S(1)} %pad_maximum_fusion) | copy-start | bytes 9437188
  406.7 24.2 %collective-permute-start.2 = (bf16[384,512]{1,0:T(8,128)(2,1)S(1)}, bf16[384,512]{1,0:T(8,128)(2,1)S(1)}, u32[]{:S(2)}, u32[]{:S(2)}) collective-permute-start(bf16[384,512]{1,0:T(8,128)(2,1)S(1)} %get-tuple-element.62), channel_id=1, source_target_pairs={{0,4},{1,5},{2,6},{3,7},{4,0},{5,1},{6,2},{7,3},{8,12},{9,13},{10,... | collective-permute-start | bytes 1179656 | tf_op jit(solution)/shard_map/ppermute | solution.py:265
  408.2 23.1 %collective-permute-start.4 = (bf16[384,512]{1,0:T(8,128)(2,1)S(1)}, bf16[384,512]{1,0:T(8,128)(2,1)S(1)}, u32[]{:S(2)}, u32[]{:S(2)}) collective-permute-start(bf16[384,512]{1,0:T(8,128)(2,1)S(1)} %get-tuple-element.64), channel_id=1, source_target_pairs={{0,2},{1,3},{2,0},{3,1},{4,6},{5,7},{6,4},{7,5},{8,10},{9,11},{10,... | collective-permute-start | bytes 1179656 | tf_op jit(solution)/shard_map/ppermute | solution.py:265
  424.6 76.2 %copy-start.6 = (bf16[768,512]{1,0:T(8,128)(2,1)}, bf16[768,512]{1,0:T(8,128)(2,1)S(1)}, u32[]{:S(2)}) copy-start(bf16[768,512]{1,0:T(8,128)(2,1)S(1)} %collective-permute-done.28) | copy-start | bytes 2359300
  424.9 43.3 %collective-permute-start.31 = (bf16[768,512]{1,0:T(8,128)(2,1)S(1)}, bf16[768,512]{1,0:T(8,128)(2,1)S(1)}, u32[]{:S(2)}, u32[]{:S(2)}) collective-permute-start(bf16[768,512]{1,0:T(8,128)(2,1)S(1)} %fusion.120), channel_id=1, source_target_pairs={{0,8},{1,9},{2,10},{3,11},{4,12},{5,13},{6,14},{7,15}} | collective-permute-start | bytes 2359304 | tf_op jit(solution)/shard_map/ppermute | solution.py:265
  427.9 75.4 %copy-start.2 = (bf16[3072,512]{1,0:T(8,128)(2,1)}, bf16[3072,512]{1,0:T(8,128)(2,1)S(1)}, u32[]{:S(2)}) copy-start(bf16[3072,512]{1,0:T(8,128)(2,1)S(1)} %pad_maximum_fusion.3) | copy-start | bytes 9437188
  428.1 12.1 %collective-permute-start.21 = (bf16[384,512]{1,0:T(8,128)(2,1)S(1)}, bf16[384,512]{1,0:T(8,128)(2,1)S(1)}, u32[]{:S(2)}, u32[]{:S(2)}) collective-permute-start(bf16[384,512]{1,0:T(8,128)(2,1)S(1)} %get-tuple-element.74), channel_id=1, source_target_pairs={{0,4},{1,5},{2,6},{3,7},{4,0},{5,1},{6,2},{7,3},{8,12},{9,13},{10,... | collective-permute-start | bytes 1179656 | tf_op jit(solution)/shard_map/ppermute | solution.py:265
  429.0 12.1 %collective-permute-start.23 = (bf16[384,512]{1,0:T(8,128)(2,1)S(1)}, bf16[384,512]{1,0:T(8,128)(2,1)S(1)}, u32[]{:S(2)}, u32[]{:S(2)}) collective-permute-start(bf16[384,512]{1,0:T(8,128)(2,1)S(1)} %get-tuple-element.76), channel_id=1, source_target_pairs={{0,2},{1,3},{2,0},{3,1},{4,6},{5,7},{6,4},{7,5},{8,10},{9,11},{10,... | collective-permute-start | bytes 1179656 | tf_op jit(solution)/shard_map/ppermute | solution.py:265
  430.8 86.6 %copy-start.3 = (bf16[3072,512]{1,0:T(8,128)(2,1)}, bf16[3072,512]{1,0:T(8,128)(2,1)S(1)}, u32[]{:S(2)}) copy-start(bf16[3072,512]{1,0:T(8,128)(2,1)S(1)} %pad_maximum_fusion.2) | copy-start | bytes 9437188
  430.9 17.7 %collective-permute-start.13 = (bf16[384,512]{1,0:T(8,128)(2,1)S(1)}, bf16[384,512]{1,0:T(8,128)(2,1)S(1)}, u32[]{:S(2)}, u32[]{:S(2)}) collective-permute-start(bf16[384,512]{1,0:T(8,128)(2,1)S(1)} %get-tuple-element.68), channel_id=1, source_target_pairs={{0,4},{1,5},{2,6},{3,7},{4,0},{5,1},{6,2},{7,3},{8,12},{9,13},{10,... | collective-permute-start | bytes 1179656 | tf_op jit(solution)/shard_map/ppermute | solution.py:265
  431.4 18.2 %collective-permute-start.15 = (bf16[384,512]{1,0:T(8,128)(2,1)S(1)}, bf16[384,512]{1,0:T(8,128)(2,1)S(1)}, u32[]{:S(2)}, u32[]{:S(2)}) collective-permute-start(bf16[384,512]{1,0:T(8,128)(2,1)S(1)} %get-tuple-element.70), channel_id=1, source_target_pairs={{0,2},{1,3},{2,0},{3,1},{4,6},{5,7},{6,4},{7,5},{8,10},{9,11},{10,... | collective-permute-start | bytes 1179656 | tf_op jit(solution)/shard_map/ppermute | solution.py:265
  440.2 25.3 %collective-permute-start.5 = (bf16[768,512]{1,0:T(8,128)(2,1)S(1)}, bf16[768,512]{1,0:T(8,128)(2,1)S(1)}, u32[]{:S(2)}, u32[]{:S(2)}) collective-permute-start(bf16[768,512]{1,0:T(8,128)(2,1)S(1)} %pad_maximum_fusion.16), channel_id=1, source_target_pairs={{0,4},{1,5},{2,6},{3,7},{4,0},{5,1},{6,2},{7,3},{8,12},{9,13},{10,... | collective-permute-start | bytes 2359304 | tf_op jit(solution)/shard_map/ppermute | solution.py:265
  441.1 25.3 %collective-permute-start.3 = (bf16[768,512]{1,0:T(8,128)(2,1)S(1)}, bf16[768,512]{1,0:T(8,128)(2,1)S(1)}, u32[]{:S(2)}, u32[]{:S(2)}) collective-permute-start(bf16[768,512]{1,0:T(8,128)(2,1)S(1)} %pad_maximum_fusion.15), channel_id=1, source_target_pairs={{0,2},{1,3},{2,0},{3,1},{4,6},{5,7},{6,4},{7,5},{8,10},{9,11},{10,... | collective-permute-start | bytes 2359304 | tf_op jit(solution)/shard_map/ppermute | solution.py:265
  448.6 33.7 %collective-permute-start.24 = (bf16[768,512]{1,0:T(8,128)(2,1)S(1)}, bf16[768,512]{1,0:T(8,128)(2,1)S(1)}, u32[]{:S(2)}, u32[]{:S(2)}) collective-permute-start(bf16[768,512]{1,0:T(8,128)(2,1)S(1)} %pad_maximum_fusion.20), channel_id=1, source_target_pairs={{0,4},{1,5},{2,6},{3,7},{4,0},{5,1},{6,2},{7,3},{8,12},{9,13},{10,... | collective-permute-start | bytes 2359304 | tf_op jit(solution)/shard_map/ppermute | solution.py:265
  449.5 33.7 %collective-permute-start.22 = (bf16[768,512]{1,0:T(8,128)(2,1)S(1)}, bf16[768,512]{1,0:T(8,128)(2,1)S(1)}, u32[]{:S(2)}, u32[]{:S(2)}) collective-permute-start(bf16[768,512]{1,0:T(8,128)(2,1)S(1)} %pad_maximum_fusion.19), channel_id=1, source_target_pairs={{0,2},{1,3},{2,0},{3,1},{4,6},{5,7},{6,4},{7,5},{8,10},{9,11},{10,... | collective-permute-start | bytes 2359304 | tf_op jit(solution)/shard_map/ppermute | solution.py:265
  465.5 30.9 %collective-permute-start.16 = (bf16[768,512]{1,0:T(8,128)(2,1)S(1)}, bf16[768,512]{1,0:T(8,128)(2,1)S(1)}, u32[]{:S(2)}, u32[]{:S(2)}) collective-permute-start(bf16[768,512]{1,0:T(8,128)(2,1)S(1)} %pad_maximum_fusion.18), channel_id=1, source_target_pairs={{0,4},{1,5},{2,6},{3,7},{4,0},{5,1},{6,2},{7,3},{8,12},{9,13},{10,... | collective-permute-start | bytes 2359304 | tf_op jit(solution)/shard_map/ppermute | solution.py:265
  466.4 30.9 %collective-permute-start.14 = (bf16[768,512]{1,0:T(8,128)(2,1)S(1)}, bf16[768,512]{1,0:T(8,128)(2,1)S(1)}, u32[]{:S(2)}, u32[]{:S(2)}) collective-permute-start(bf16[768,512]{1,0:T(8,128)(2,1)S(1)} %pad_maximum_fusion.17), channel_id=1, source_target_pairs={{0,2},{1,3},{2,0},{3,1},{4,6},{5,7},{6,4},{7,5},{8,10},{9,11},{10,... | collective-permute-start | bytes 2359304 | tf_op jit(solution)/shard_map/ppermute | solution.py:265
  468.2 31.4 %collective-permute-start.6 = (bf16[768,512]{1,0:T(8,128)(2,1)S(1)}, bf16[768,512]{1,0:T(8,128)(2,1)S(1)}, u32[]{:S(2)}, u32[]{:S(2)}) collective-permute-start(bf16[768,512]{1,0:T(8,128)(2,1)S(1)} %fusion.119), channel_id=1, source_target_pairs={{24,16},{25,17},{26,18},{27,19},{28,20},{29,21},{30,22},{31,23}} | collective-permute-start | bytes 2359304 | tf_op jit(solution)/shard_map/ppermute | solution.py:265
  482.3 18.4 %collective-permute-start.32 = (bf16[768,512]{1,0:T(8,128)(2,1)S(1)}, bf16[768,512]{1,0:T(8,128)(2,1)S(1)}, u32[]{:S(2)}, u32[]{:S(2)}) collective-permute-start(bf16[768,512]{1,0:T(8,128)(2,1)S(1)} %fusion.69), channel_id=1, source_target_pairs={{8,16},{9,17},{10,18},{11,19},{12,20},{13,21},{14,22},{15,23}} | collective-permute-start | bytes 2359304 | tf_op jit(solution)/shard_map/ppermute | solution.py:265
  483.6 19.8 %collective-permute-start.25 = (bf16[768,512]{1,0:T(8,128)(2,1)S(1)}, bf16[768,512]{1,0:T(8,128)(2,1)S(1)}, u32[]{:S(2)}, u32[]{:S(2)}) collective-permute-start(bf16[768,512]{1,0:T(8,128)(2,1)S(1)} %fusion.98), channel_id=1, source_target_pairs={{0,8},{1,9},{2,10},{3,11},{4,12},{5,13},{6,14},{7,15},{24,16},{25,... | collective-permute-start | bytes 2359304 | tf_op jit(solution)/shard_map/ppermute | solution.py:265
  497.6 19.8 %collective-permute-start.17 = (bf16[768,512]{1,0:T(8,128)(2,1)S(1)}, bf16[768,512]{1,0:T(8,128)(2,1)S(1)}, u32[]{:S(2)}, u32[]{:S(2)}) collective-permute-start(bf16[768,512]{1,0:T(8,128)(2,1)S(1)} %fusion.97), channel_id=1, source_target_pairs={{24,16},{25,17},{26,18},{27,19},{28,20},{29,21},{30,22},{31,23},{0... | collective-permute-start | bytes 2359304 | tf_op jit(solution)/shard_map/ppermute | solution.py:265
  500.0 20.4 %collective-permute-start.7 = (bf16[768,512]{1,0:T(8,128)(2,1)S(1)}, bf16[768,512]{1,0:T(8,128)(2,1)S(1)}, u32[]{:S(2)}, u32[]{:S(2)}) collective-permute-start(bf16[768,512]{1,0:T(8,128)(2,1)S(1)} %fusion.66), channel_id=1, source_target_pairs={{16,8},{17,9},{18,10},{19,11},{20,12},{21,13},{22,14},{23,15}} | collective-permute-start | bytes 2359304 | tf_op jit(solution)/shard_map/ppermute | solution.py:265
  502.2 33.5 %collective-permute-start.33 = (bf16[768,512]{1,0:T(8,128)(2,1)}, bf16[768,512]{1,0:T(8,128)(2,1)S(1)}, u32[]{:S(2)}, u32[]{:S(2)}) collective-permute-start(bf16[768,512]{1,0:T(8,128)(2,1)} %fusion.96), channel_id=1, source_target_pairs={{16,24},{17,25},{18,26},{19,27},{20,28},{21,29},{22,30},{23,31}} | collective-permute-start | bytes 2359304 | tf_op jit(solution)/shard_map/ppermute | solution.py:265
  505.5 30.2 %collective-permute-start.26 = (bf16[768,512]{1,0:T(8,128)(2,1)}, bf16[768,512]{1,0:T(8,128)(2,1)S(1)}, u32[]{:S(2)}, u32[]{:S(2)}) collective-permute-start(bf16[768,512]{1,0:T(8,128)(2,1)} %fusion.68), channel_id=1, source_target_pairs={{8,16},{9,17},{10,18},{11,19},{12,20},{13,21},{14,22},{15,23}} | collective-permute-start | bytes 2359304 | tf_op jit(solution)/shard_map/ppermute | solution.py:265
  518.7 17.0 %collective-permute-start.18 = (bf16[768,512]{1,0:T(8,128)(2,1)}, bf16[768,512]{1,0:T(8,128)(2,1)}, u32[]{:S(2)}, u32[]{:S(2)}) collective-permute-start(bf16[768,512]{1,0:T(8,128)(2,1)} %fusion.67), channel_id=1, source_target_pairs={{16,8},{17,9},{18,10},{19,11},{20,12},{21,13},{22,14},{23,15}} | collective-permute-start | bytes 2359304 | tf_op jit(solution)/shard_map/ppermute | solution.py:265
  521.9 19.3 %collective-permute-start.8 = (bf16[768,512]{1,0:T(8,128)(2,1)}, bf16[768,512]{1,0:T(8,128)(2,1)}, u32[]{:S(2)}, u32[]{:S(2)}) collective-permute-start(bf16[768,512]{1,0:T(8,128)(2,1)} %fusion.95), channel_id=1, source_target_pairs={{8,0},{9,1},{10,2},{11,3},{12,4},{13,5},{14,6},{15,7}} | collective-permute-start | bytes 2359304 | tf_op jit(solution)/shard_map/ppermute | solution.py:265
  529.5 28.6 %all-to-all-start.2 = ((f32[32,1,68]{2,1,0:T(1,128)}), f32[32,1,68]{2,1,0:T(1,128)S(1)}, u32[]{:S(2)}, u32[]{:S(2)}) async-start(f32[32,1,68]{2,1,0:T(1,128)} %reshape.423), calls=%async_computation.2 | async-start | bytes 32768 | tf_op jit(solution)/shard_map/all_to_all | solution.py:515
  554.0 4.7 collective-permute-start.34
  (76 other events, 727.1 us)
Sparse Core Ops, SparseCore 0:
  11.5 157.7 all-gather.1

commit v3 on v1

--- a/solution.py
+++ b/solution.py
@@ -2,6 +2,7 @@
 
 import jax
 import jax.numpy as jnp
+import numpy as np
 from jax import lax
 from jax.experimental import pallas as pl
 from jax.experimental.pallas import tpu as pltpu
@@ -19,6 +20,7 @@
 adam_eps = 1e-08
 decay_rate = 0.1
 gain_rate = 0.5
+
 
 def mm(left, right, dims):
     return lax.dot_general(left, right, (dims, ((), ())), preferred_element_type=jnp.float32)
@@ -243,6 +245,341 @@
     return rows_out, back, dwq, dwo, dwu, dwd, jnp.sum(dg3, axis=1), jnp.sum(dg4, axis=1)
 
 
+def placed(flat):
+    if flat < 3072:
+        return flat % 3 * 1024 + flat // 3
+    if flat < 4096 or flat >= 8192:
+        return flat
+    return 4096 + flat % 4 * 1024 + (flat - 4096) // 4
+
+
+def shard_orders():
+    orders, runs = [], []
+    for d in range(32):
+        places = [placed(384 * d + i) for i in range(384)]
+        order = sorted(range(384), key=lambda i: places[i])
+        orders.append(order)
+        for at, i in enumerate(order):
+            if at and places[i] == runs[-1][1] + runs[-1][2] and places[i] % 1024:
+                runs[-1][2] += 1
+            else:
+                runs.append([384 * d + at, places[i], 1])
+    return np.array(orders, np.int32), sorted((tuple(run) for run in runs), key=lambda run: run[1])
+
+
+def forward_kernel(runs, turn, h0_ref, g1_ref, g2_ref, tall_ref, wide_ref, flat_ref,
+                   big_ref, joined_ref, a1_ref, o1_ref, a2_ref, u1_ref, slope_ref, h1_ref, out_ref,
+                   mats, bias, loaded, stored):
+    f32, bf = jnp.float32, jnp.bfloat16
+    slots, width = h0_ref.shape
+    head = width // HEADS
+    tile = 512
+    groups = {}
+    for n, (src, dst, rows) in enumerate(runs):
+        copy = pltpu.make_async_copy(flat_ref.at[pl.ds(src, rows)], mats.at[pl.ds(dst, rows)], loaded.at[n])
+        copy.start()
+        groups.setdefault(dst // width, []).append(copy)
+    saves = []
+
+    def arrive(i):
+        for copy in groups[i]:
+            copy.wait()
+        saves.append(pltpu.make_async_copy(mats.at[pl.ds(i * width, width)], big_ref.at[pl.ds(i * width, width)], stored.at[i]))
+        saves[-1].start()
+
+    def norm(v, gain):
+        center = v - jnp.mean(v, axis=1, keepdims=True)
+        root = lax.rsqrt(jnp.mean(center * center, axis=1, keepdims=True) + norm_eps)
+        return (center * root * gain).astype(bf)
+
+    bias[...] = jnp.where(tall_ref[...] == wide_ref[...], 0.0, -jnp.inf)
+    a1_ref[...] = norm(h0_ref[...].astype(f32), g1_ref[...])
+    for i in range(3):
+        arrive(i)
+
+        def project(t, carry):
+            cols = pl.ds(pl.multiple_of(t * tile, tile), tile)
+            joined_ref[:, pl.ds(pl.multiple_of(i * width + t * tile, tile), tile)] = mm(
+                a1_ref[...], mats[i * width : (i + 1) * width, cols], ((1,), (0,))
+            ).astype(bf)
+            return carry
+
+        lax.fori_loop(0, width // tile, project, 0)
+
+    def attend(h, carry):
+        part = lambda i: joined_ref[:, pl.ds(pl.multiple_of(i * width + h * head, head), head)]
+        scores = mm(part(0), part(1), ((1,), (1,))) * head ** (-0.5) + bias[...]
+        weights = jnp.exp(scores - jnp.max(scores, axis=1, keepdims=True))
+        chance = weights * (1.0 / jnp.sum(weights, axis=1, keepdims=True))
+        o1_ref[:, pl.ds(pl.multiple_of(h * head, head), head)] = mm(chance.astype(bf), part(2), ((1,), (0,))).astype(bf)
+        return carry
+
+    lax.fori_loop(0, HEADS, attend, 0)
+    arrive(3)
+    for t in range(width // tile):
+        cols = slice(t * tile, (t + 1) * tile)
+        h1_ref[:, cols] = h0_ref[:, cols].astype(f32) + mm(o1_ref[...], mats[3 * width : 4 * width, cols], ((1,), (0,)))
+    a2_ref[...] = norm(h1_ref[...], g2_ref[...])
+    for i in range(4):
+        arrive(4 + i)
+
+        def widen(t, carry):
+            cols = pl.ds(pl.multiple_of(t * tile, tile), tile)
+            active, slope = gelu_pair(mm(a2_ref[...], mats[(4 + i) * width : (5 + i) * width, cols], ((1,), (0,))))
+            cols = pl.ds(pl.multiple_of(i * width + t * tile, tile), tile)
+            u1_ref[:, cols] = active.astype(bf)
+            slope_ref[:, cols] = slope.astype(bf)
+            return carry
+
+        lax.fori_loop(0, width // tile, widen, 0)
+    for i in range(4):
+        arrive(8 + i)
+    to, source = (lax.broadcasted_iota(jnp.int32, (slots, slots), axis) for axis in (0, 1))
+    hot = (source == to % turn * (slots // turn) + to // turn).astype(f32).astype(bf)
+    for t in range(width // tile):
+        cols = slice(t * tile, (t + 1) * tile)
+        h2 = (h1_ref[:, cols] + mm(u1_ref[...], mats[8 * width :, cols], ((1,), (0,)))).astype(bf)
+        out_ref[:, cols] = mm(hot, h2, ((1,), (0,))).astype(bf)
+    for save in saves:
+        save.wait()
+
+
+def forward_layer(runs, turn, h0, g1, g2, labels, flat):
+    f32, bf = jnp.float32, jnp.bfloat16
+    slots, width = h0.shape
+    vmem = pl.BlockSpec(memory_space=pltpu.VMEM)
+    anywhere = pl.BlockSpec(memory_space=pl.ANY)
+    shape = jax.ShapeDtypeStruct
+    return pl.pallas_call(
+        functools.partial(forward_kernel, runs, turn),
+        in_specs=[vmem] * 5 + [anywhere],
+        out_specs=[anywhere] + [vmem] * 8,
+        out_shape=[
+            shape(flat.shape, bf),
+            shape((slots, 3 * width), bf),
+            shape((slots, width), bf),
+            shape((slots, width), bf),
+            shape((slots, width), bf),
+            shape((slots, 4 * width), bf),
+            shape((slots, 4 * width), bf),
+            shape((slots, width), f32),
+            shape((slots, width), bf),
+        ],
+        scratch_shapes=[
+            pltpu.VMEM(flat.shape, bf),
+            pltpu.VMEM((slots, slots), f32),
+            pltpu.SemaphoreType.DMA((len(runs),)),
+            pltpu.SemaphoreType.DMA((12,)),
+        ],
+        compiler_params=pltpu.CompilerParams(vmem_limit_bytes=56 * 2**20),
+        cost_estimate=pl.CostEstimate(flops=10**10, bytes_accessed=64 * 2**20, transcendentals=3 * 10**6),
+    )(h0, g1.reshape(1, -1), g2.reshape(1, -1), labels.reshape(-1, 1), labels.reshape(1, -1), flat)
+
+
+def pull_norm(v, gain, upstream):
+    center = v - jnp.mean(v, axis=1, keepdims=True)
+    root = lax.rsqrt(jnp.mean(center * center, axis=1, keepdims=True) + norm_eps)
+    hat = center * root
+    dhat = upstream * gain
+    inner = jnp.mean(dhat * hat, axis=1, keepdims=True)
+    grad = root * (dhat - jnp.mean(dhat, axis=1, keepdims=True) - hat * inner)
+    return grad, jnp.sum(upstream * hat, axis=0, keepdims=True)
+
+
+def widen_back_kernel(core_ref, gz_ref, slope_ref, h1_ref, g2_ref, big_ref, dpre_ref, dh_ref, gz_out_ref, dg_ref, ups, downs, da, sems):
+    f32, bf = jnp.float32, jnp.bfloat16
+    width = gz_ref.shape[1]
+    half = width // 2
+    core = core_ref[0]
+    copies = []
+    for i in range(4):
+        for n, (first, held) in enumerate(((8, downs), (4, ups))):
+            rows = pl.ds((first + i) * width, width)
+            copies.append(pltpu.make_async_copy(big_ref.at[rows], held.at[pl.ds(i * width, width)], sems.at[2 * i + n]))
+            copies[-1].start()
+    da[...] = jnp.zeros_like(da)
+    for i in range(4):
+        copies[2 * i].wait()
+        copies[2 * i + 1].wait()
+
+        def side(s, carry):
+            hidden = pl.ds(pl.multiple_of(i * width + s * half, half), half)
+            lanes = pl.ds(pl.multiple_of(s * half, half), half)
+            du = mm(gz_ref[...], downs[hidden], ((1,), (1,)))
+            dpre = (slope_ref[:, hidden].astype(f32) * du).astype(bf)
+            dpre_ref[s ^ core, :, i * half : (i + 1) * half] = dpre
+            da[...] += mm(dpre, ups[i * width : (i + 1) * width, lanes], ((1,), (1,)))
+            return carry
+
+        lax.fori_loop(0, 2, side, 0)
+    grad, dg_ref[...] = pull_norm(h1_ref[...], g2_ref[...], da[...])
+    dh_ref[...] = gz_ref[...].astype(f32) + grad
+    for s in range(2):
+        gz_out_ref[s ^ core] = dh_ref[:, s * half : (s + 1) * half].astype(bf)
+
+
+def widen_back(core, gz, slope, h1, g2, big):
+    f32, bf = jnp.float32, jnp.bfloat16
+    slots, width = gz.shape
+    vmem = pl.BlockSpec(memory_space=pltpu.VMEM)
+    shape = jax.ShapeDtypeStruct
+    return pl.pallas_call(
+        widen_back_kernel,
+        in_specs=[pl.BlockSpec(memory_space=pltpu.SMEM)] + [vmem] * 4 + [pl.BlockSpec(memory_space=pl.ANY)],
+        out_specs=[vmem] * 4,
+        out_shape=[
+            shape((2, slots, 2 * width), bf),
+            shape((slots, width), f32),
+            shape((2, slots, width // 2), bf),
+            shape((1, width), f32),
+        ],
+        scratch_shapes=[
+            pltpu.VMEM((4 * width, width), bf),
+            pltpu.VMEM((4 * width, width), bf),
+            pltpu.VMEM((slots, width), f32),
+            pltpu.SemaphoreType.DMA((8,)),
+        ],
+        compiler_params=pltpu.CompilerParams(vmem_limit_bytes=48 * 2**20),
+        cost_estimate=pl.CostEstimate(flops=64 * 10**8, bytes_accessed=32 * 2**20, transcendentals=0),
+    )(core, gz, slope, h1, g2.reshape(1, -1), big)
+
+
+def attend_back_kernel(
+    core_ref, dh_ref, h0_ref, g1_ref, joined_ref, tall_ref, wide_ref, big_ref, dj_ref, out_ref, dg_ref, mats, bias, dblend, dj, sems
+):
+    f32, bf = jnp.float32, jnp.bfloat16
+    slots, width = dh_ref.shape
+    head = width // HEADS
+    half = width // 2
+    tile = 512
+    scaling = head ** (-0.5)
+    core = core_ref[0]
+    copies = []
+    for n, i in enumerate((3, 0, 1, 2)):
+        rows = pl.ds(i * width, width)
+        copies.append(pltpu.make_async_copy(big_ref.at[rows], mats.at[rows], sems.at[n]))
+        copies[-1].start()
+    bias[...] = jnp.where(tall_ref[...] == wide_ref[...], 0.0, -jnp.inf)
+    copies[0].wait()
+    gz = dh_ref[...].astype(bf)
+    for t in range(width // tile):
+        rows = slice(3 * width + t * tile, 3 * width + (t + 1) * tile)
+        dblend[:, t * tile : (t + 1) * tile] = mm(gz, mats[rows], ((1,), (1,))).astype(bf)
+
+    def attend(h, carry):
+        lanes = lambda i: pl.ds(pl.multiple_of(i * width + h * head, head), head)
+        q, k, v = (joined_ref[:, lanes(i)] for i in range(3))
+        do = dblend[:, pl.ds(pl.multiple_of(h * head, head), head)]
+        scores = mm(q, k, ((1,), (1,))) * scaling + bias[...]
+        weights = jnp.exp(scores - jnp.max(scores, axis=1, keepdims=True))
+        chance = weights * (1.0 / jnp.sum(weights, axis=1, keepdims=True))
+        dchance = mm(do, v, ((1,), (1,)))
+        dot = jnp.sum(chance * dchance, axis=1, keepdims=True)
+        ds = (chance * (dchance - dot)).astype(bf)
+        parts = (
+            mm(ds, k, ((1,), (0,))) * scaling,
+            mm(ds, q, ((0,), (0,))) * scaling,
+            mm(chance.astype(bf), do, ((0,), (0,))),
+        )
+        per_side = HEADS // 2
+        for i in range(3):
+            part = parts[i].astype(bf)
+            dj[:, lanes(i)] = part
+            dj_ref[(h // per_side) ^ core, :, pl.ds(pl.multiple_of(i * half + h % per_side * head, head), head)] = part
+        return carry
+
+    lax.fori_loop(0, HEADS, attend, 0)
+    da = None
+    for i in range(3):
+        copies[1 + i].wait()
+        term = mm(dj[:, i * width : (i + 1) * width], mats[i * width : (i + 1) * width], ((1,), (1,)))
+        da = term if da is None else da + term
+    grad, dg_ref[...] = pull_norm(h0_ref[...].astype(f32), g1_ref[...], da)
+    out_ref[...] = dh_ref[...] + grad
+
+
+def attend_back(core, dh, h0, g1, joined, labels, big):
+    f32, bf = jnp.float32, jnp.bfloat16
+    slots, width = dh.shape
+    vmem = pl.BlockSpec(memory_space=pltpu.VMEM)
+    shape = jax.ShapeDtypeStruct
+    return pl.pallas_call(
+        attend_back_kernel,
+        in_specs=[pl.BlockSpec(memory_space=pltpu.SMEM)] + [vmem] * 6 + [pl.BlockSpec(memory_space=pl.ANY)],
+        out_specs=[vmem] * 3,
+        out_shape=[shape((2, slots, 3 * width // 2), bf), shape((slots, width), f32), shape((1, width), f32)],
+        scratch_shapes=[
+            pltpu.VMEM((4 * width, width), bf),
+            pltpu.VMEM((slots, slots), f32),
+            pltpu.VMEM((slots, width), bf),
+            pltpu.VMEM((slots, 3 * width), bf),
+            pltpu.SemaphoreType.DMA((4,)),
+        ],
+        compiler_params=pltpu.CompilerParams(vmem_limit_bytes=48 * 2**20),
+        cost_estimate=pl.CostEstimate(flops=64 * 10**8, bytes_accessed=16 * 2**20, transcendentals=10**6),
+    )(core, dh, h0, g1.reshape(1, -1), joined, labels.reshape(-1, 1), labels.reshape(1, -1), big)
+
+
+CORE = 1
+
+
+def send(v, bit):
+    return lax.ppermute(v, "dev", [(d, d ^ bit) for d in range(32)])
+
+
+def after(*values):
+    return lax.optimization_barrier(values)
+
+
+def chip_rows():
+    table = []
+    for chip in range(16):
+        places = [placed(flat) for flat in range(chip * 768, chip * 768 + 768)]
+        order = sorted(range(768), key=lambda i: places[i])
+        place = [0] * 768
+        for at, i in enumerate(order):
+            place[i] = at
+        table.append(place)
+    return np.array(table, np.int32)
+
+
+def sum_to_owners(blocks, device):
+    f32, bf = jnp.float32, jnp.bfloat16
+    core, chip = device % 2, device // 2
+    half = blocks.shape[1] // 2
+    block = lambda m: lax.dynamic_index_in_dim(blocks, chip ^ (m >> 1), 0, keepdims=False)
+    total = lambda *parts: sum(part.astype(f32) for part in parts)
+    both = lambda one, two: jnp.concatenate([one, two]).astype(bf)
+
+    far = block(30)
+    a, b = after(send(far[:half], 4), send(far[half:], 2))
+    side, other, next_far = block(26), block(28), block(22)
+    side = both(total(side[:half], a), side[half:])
+    other = both(other[:half], total(other[half:], b))
+    a, b, c = after(send(side, 8), send(other, 4), send(next_far, 2))
+
+    far = block(14)
+    over_x, over_y, across = total(block(18), a).astype(bf), total(block(20), c).astype(bf), total(block(24), b).astype(bf)
+    a, b, c, d, e = after(send(far[:half], 4), send(far[half:], 2), send(over_x, 2), send(over_y, 4), send(across, 8))
+    far = block(6)
+    side, other = block(10), block(12)
+    up_x = both(total(side[:half], a), side[half:])
+    up_y = both(other[:half], total(other[half:], b))
+    over = total(block(16), c, d, e).astype(bf)
+    a, b, c, d, e = after(send(far[:half], 4), send(far[half:], 2), send(up_x, 2), send(up_y, 4), send(over, 16))
+    side, other = block(2), block(4)
+    own_x = both(total(side[:half], a), side[half:])
+    own_y = both(other[:half], total(other[half:], b))
+    up = total(block(8), c, d).astype(bf)
+    own = total(block(0), e, send(own_x, 2), send(own_y, 4), send(up, 8))
+
+    order = lax.dynamic_index_in_dim(jnp.asarray(chip_rows()), chip, 0, keepdims=False)
+    own = jnp.take(own, order, axis=0)
+    mine = lax.dynamic_slice_in_dim(own, core * half, half, 0)
+    peer = send(lax.dynamic_slice_in_dim(own, (1 - core) * half, half, 0), CORE)
+    return jnp.where(core == 0, jnp.concatenate([mine, peer], axis=1), jnp.concatenate([peer, mine], axis=1))
+
+
 def fwd_mul(left, right):
     return mm(left, right, ((1,), (0,)))
 
@@ -307,20 +644,28 @@
     per_peer = slots // devices
     rows_even = out_grad.shape[0]
     rows_pad = -(-rows_even // LANES) * LANES
-    head = width // HEADS
-    scaling = head ** (-0.5)
+    grid = devices == 32 and width == 1024 and slots == 384
 
     n_rows, n_gains = rows_weights.shape[0], norm_gains.shape[0]
     small = jnp.concatenate([rows_weights, norm_gains]).astype(bf)
     small = jnp.pad(small, (0, -small.shape[0] % 1024)).reshape(-1, 1024)
-    small = lax.all_gather(small, "dev", axis=0, tiled=False).reshape(devices, -1)
+    small = lax.all_gather(small, "dev", axis=0, tiled=False)
+    shard = sets_weights.astype(bf).reshape(-1, width)
+    if grid:
+        orders, runs = shard_orders()
+        order = lax.dynamic_index_in_dim(jnp.asarray(orders), device, 0, keepdims=False)
+        hot = (order[:, None] == jnp.arange(shard.shape[0], dtype=jnp.int32)[None, :]).astype(bf)
+        flat = lax.all_gather(fwd_mul(hot, shard).astype(bf), "dev", axis=0, tiled=True)
+    else:
+        flat = lax.all_gather(shard, "dev", axis=0, tiled=True)
+        parts = lambda v, n: v.reshape(width, n, width).transpose(1, 0, 2).reshape(n * width, width)
+        flat = jnp.concatenate(
+            [parts(flat[: 3 * width], 3), flat[3 * width : 4 * width], parts(flat[4 * width : 8 * width], 4), flat[8 * width :]]
+        )
+        runs = [(i * width, i * width, width) for i in range(12)]
+    small = small.reshape(devices, -1)
     full_rows = small[:, :n_rows].reshape(-1)
     full_gains = small[:, n_rows : n_rows + n_gains].reshape(-1).astype(f32)
-    flat = lax.all_gather(sets_weights.astype(bf).reshape(-1, width), "dev", axis=0, tiled=True)
-    wq1 = flat[: 3 * width].reshape(width, 3 * width)
-    wo1 = flat[3 * width : 4 * width]
-    wu1 = flat[4 * width : 8 * width].reshape(width, 4 * width)
-    wd1 = flat[8 * width :]
     square = feat * feat
     wq2 = full_rows[: 3 * square].reshape(feat, 3 * feat)
     wo2 = full_rows[3 * square : 4 * square].reshape(feat, feat)
@@ -337,68 +682,57 @@
     ends = running(counts)
     spot = jnp.arange(rows_pad, dtype=jnp.int32)
     past = (ends[None, :] <= spot[:, None]).astype(jnp.int32)
-    source = jnp.sum(past, axis=1)
     start = jnp.sum(past * counts[None, :], axis=1)
-    pick = jnp.where(spot < rows_even, source * per_peer + spot - start, -1)
-
-    h0 = cells_in.astype(f32)
-    hat1, root1 = norm_parts(h0)
-    a1 = (hat1 * g1).astype(bf)
-    joined = fwd_mul(a1, wq1).astype(bf).reshape(slots, 3, HEADS, head)
-    queries, key_rows, values = joined[:, 0], joined[:, 1], joined[:, 2]
-    related = labels[:, None] == labels[None, :]
-    scores = jnp.einsum("qhd,khd->hqk", queries, key_rows, preferred_element_type=f32) * scaling
-    scores = jnp.where(related[None], scores, -jnp.inf)
-    weights = jnp.exp(scores - jnp.max(scores, axis=-1, keepdims=True))
-    chance = weights / jnp.sum(weights, axis=-1, keepdims=True)
-    chance_low = chance.astype(bf)
-    o1 = jnp.einsum("hqk,khd->qhd", chance_low, values, preferred_element_type=f32).astype(bf).reshape(slots, width)
-    h1 = h0 + fwd_mul(o1, wo1)
-    hat2, root2 = norm_parts(h1)
-    a2 = (hat2 * g2).astype(bf)
-    active, slope = gelu_pair(fwd_mul(a2, wu1))
-    u1 = active.astype(bf)
-    h2 = h1 + fwd_mul(u1, wd1)
-
-    outgoing = h2.astype(bf).reshape(per_peer, devices, width).transpose(1, 0, 2)
-    arrived = lax.all_to_all(outgoing, "dev", split_axis=0, concat_axis=0, tiled=True)
+    pick = jnp.where(spot < rows_even, jnp.sum(past, axis=1) * per_peer + spot - start, -1)
+
+    big, joined, a1, o1, a2, u1, slope, h1, leaving = forward_layer(runs, per_peer, cells_in, g1, g2, labels, flat)
+
+    swap = lambda v: lax.all_to_all(v.reshape(devices, -1, width), "dev", split_axis=0, concat_axis=0, tiled=True)
     og = jnp.pad(out_grad, ((0, rows_pad - rows_even), (0, 0)))
     rows_out, back, dq2, do2, du2, dd2, dg3, dg4 = rows_layer(
-        pick, arrived.reshape(slots, width), og, wq2, wo2, wu2, wd2, g3, g4
+        pick, swap(leaving).reshape(slots, width), og, wq2, wo2, wu2, wd2, g3, g4
     )
     rows_out = rows_out[:rows_even]
-    rows_flat = jnp.concatenate([dq2.reshape(-1), do2.reshape(-1), du2.reshape(-1), dd2.reshape(-1)])
-    extra = rows_flat.reshape(devices, n_rows).astype(bf)
-    extra = jnp.pad(extra, ((0, 0), (0, -n_rows % width))).reshape(devices, -1, width)
-    payload = jnp.concatenate([back.reshape(devices, per_peer, width), extra], axis=1)
-    returned = lax.all_to_all(payload, "dev", split_axis=0, concat_axis=0, tiled=True)
-    grad = returned[:, :per_peer].transpose(1, 0, 2).reshape(slots, width).astype(f32)
-    rows_grad = jnp.sum(returned[:, per_peer:].reshape(devices, -1)[:, :n_rows].astype(f32), axis=0)
-
-    gz = grad.astype(bf)
-    dd1 = outer(u1, gz).astype(bf)
-    dpre = (slope * backmul(gz, wd1)).astype(bf)
-    du1 = outer(a2, dpre).astype(bf)
-    dh, dg2 = norm_pull(hat2, root2, g2, backmul(dpre, wu1))
-    grad = grad + dh
-    gz = grad.astype(bf)
-    do1 = outer(o1, gz).astype(bf)
-    dblend = backmul(gz, wo1).astype(bf).reshape(slots, HEADS, head)
-    dchance = jnp.einsum("qhd,khd->hqk", dblend, values, preferred_element_type=f32)
-    dot = jnp.sum(chance * dchance, axis=-1, keepdims=True)
-    dscores = (chance * (dchance - dot)).astype(bf)
-    dq = jnp.einsum("hqk,khd->qhd", dscores, key_rows, preferred_element_type=f32) * scaling
-    dk = jnp.einsum("hqk,qhd->khd", dscores, queries, preferred_element_type=f32) * scaling
-    dv = jnp.einsum("hqk,qhd->khd", chance_low, dblend, preferred_element_type=f32)
-    djoined = jnp.concatenate([part.reshape(slots, width).astype(bf) for part in (dq, dk, dv)], axis=1)
-    dq1 = outer(a1, djoined).astype(bf)
-    dh, dg1 = norm_pull(hat1, root1, g1, backmul(djoined, wq1))
-    cells_grad = grad + dh
-
-    full = jnp.concatenate([dq1.reshape(-1, width), do1, du1.reshape(-1, width), dd1])
-    sets_grad = lax.psum_scatter(full, "dev", scatter_dimension=0, tiled=True).astype(f32).reshape(-1)
-    gains = jnp.concatenate([dg1, dg2, dg3, dg4]).reshape(devices, 1, n_gains)
-    gains_grad = jnp.sum(lax.all_to_all(gains, "dev", split_axis=0, concat_axis=0, tiled=True), axis=(0, 1))
+    gz = swap(back).transpose(1, 0, 2).reshape(slots, width)
+
+    core = device % 2
+    which = core.reshape(1)
+    half = width // 2
+    dpre, dh1, gz_out, dg2 = widen_back(which, gz, slope, h1, g2, big)
+    dj, cells_grad, dg1 = attend_back(which, dh1, cells_in, g1, joined, labels, big)
+    rows_flat = jnp.concatenate([v.reshape(-1) for v in (dq2, do2, du2, dd2)])
+    if grid:
+        gz_sides = [lax.dynamic_slice_in_dim(gz, side * half, half, 1) for side in (core, 1 - core)]
+
+        def chip_outer(left, sides, part):
+            lanes = slice(part * half, (part + 1) * half)
+            return (outer(left[0], sides[0][:, lanes]) + outer(left[1], sides[1][:, lanes])).astype(bf)
+
+        pair = lambda v: (v, send(v, CORE))
+        dd1 = chip_outer(pair(u1), (gz_sides[0], send(gz_sides[1], CORE)), 0)
+        sides, left = (dpre[0], send(dpre[1], CORE)), pair(a2)
+        du1 = jnp.stack([chip_outer(left, sides, j) for j in range(4)])
+        do1 = chip_outer(pair(o1), (gz_out[0], send(gz_out[1], CORE)), 0)
+        sides, left = (dj[0], send(dj[1], CORE)), pair(a1)
+        dq1 = jnp.stack([chip_outer(left, sides, j) for j in range(3)])
+        tall = lambda lo, hi: du1[:, lo:hi].reshape(4 * (hi - lo), half)
+        cuts = (0, 128, 320, 512, 704, 896, 1024)
+        blocks = jnp.concatenate(
+            [dq1.reshape(3, 4, -1, half).transpose(1, 0, 2, 3).reshape(3 * width, half), do1]
+            + [tall(lo, hi) for lo, hi in zip(cuts[:-1], cuts[1:], strict=True)]
+            + [dd1]
+        )
+        sets_grad = sum_to_owners(blocks.reshape(16, -1, half), device).reshape(-1)
+    else:
+        sides = lambda v, n: jnp.where(core == 0, v, v[::-1]).reshape(2, slots, n, half).transpose(1, 2, 0, 3).reshape(slots, -1)
+        dq1, du1 = outer(a1, sides(dj, 3)), outer(a2, sides(dpre, 4))
+        full = jnp.concatenate([dq1.reshape(-1, width), outer(o1, dh1.astype(bf)), du1.reshape(-1, width), outer(u1, gz)])
+        sets_grad = lax.psum_scatter(full.astype(bf), "dev", scatter_dimension=0, tiled=True).astype(f32).reshape(-1)
+
+    gains = jnp.concatenate([dg1[0], dg2[0], dg3, dg4]).reshape(devices, n_gains)
+    extra = jnp.concatenate([rows_flat.reshape(devices, n_rows), gains], axis=1).reshape(devices, 1, -1)
+    extra = jnp.sum(lax.all_to_all(extra, "dev", split_axis=0, concat_axis=0, tiled=True), axis=(0, 1))
+    rows_grad, gains_grad = extra[:n_rows], extra[n_rows:]
 
     set_index = device * sets_grad.shape[0] + jnp.arange(sets_grad.shape[0], dtype=jnp.int32)
     row_index = device * n_rows + jnp.arange(n_rows, dtype=jnp.int32)

time: 725 us -> 555 us (0.77)
  waiting for transfers between devices: 356 us -> 238 us
  Pallas kernels: 33.8 us -> 106 us
  matrix products: 91 us -> 34.3 us
  local copies, waits for them, and re-layouts: 89.1 us -> 42.7 us
  blocking collectives: 74.1 us -> 44.3 us
  starting transfers between devices: 5.73 us -> 30 us
  other arithmetic: 55.4 us -> 33.5 us
    reduce_scatter x1 -> x0, waiting for transfers between devices: 222 us -> none  [local(): lax.psum_scatter(full, 'dev', scatter_dimension=0, tiled=True).astype(f32)]
    ppermute x0 -> x27, waiting for transfers between devices: none -> 83.4 us  [send(): return lax.ppermute(v, 'dev', [(d, d ^ bit) for d in range(32)])]
    pallas_call x0 -> x3, Pallas kernels: none -> 72.7 us  [the longest x1 32 us: forward_layer(): pl.pallas_call(functools.partial(forward_kernel, runs, turn), in_specs=[v...]
    reshape x12 -> x10, local copies, waits for them, and re-layouts: 55.9 us -> 8.72 us  [the longest x2 4.3 us: local(): v.reshape(devices, -1, width)]
    dot_general x12 -> x19, matrix products: 78.3 us -> 34.3 us  [mm(): lax.dot_general(left, right, (dims, ((), ())), preferred_element_type=jnp...]
    concatenate x3 -> x8, other arithmetic: 35.6 us -> 2.98 us  [the longest x6 2.95 us: sum_to_owners(): both = lambda one, two: jnp.concatenate([one, two]).astype(bf)]
    all_to_all x1 -> x0, blocking collectives: 29.8 us -> none  [local(): lax.all_to_all(payload, 'dev', split_axis=0, concat_axis=0, tiled=True)]
    all_to_all x2 -> x3, waiting for transfers between devices: 20.6 us -> 43.8 us  [the longest x2 43.8 us: local(): lax.all_to_all(v.reshape(devices, -1, width), 'dev', split_axis=0, concat...]
  transfers between devices with their start and end apart: 4 -> 31, of which waited for: 4 -> 14; matrix products, arithmetic and copies ran while one was open for 4% -> 13% of each run, Pallas kernels for 0% -> 7%
where the time goes in v3:
time: 555 us; the launch traced here: 545 us
  waiting for transfers between devices  238 us (43%)
  Pallas kernels  106 us (19%)
  blocking collectives  44.3 us (8%)
  local copies, waits for them, and re-layouts  42.7 us (8%)
  matrix products  34.3 us (6%)
  other arithmetic  33.5 us (6%)
  starting transfers between devices  30 us (5%)
  between operations  15.7 us (3%)
    all_gather x1, waiting for transfers between devices, local(): lax.all_gather(fwd_mul(hot, shard).astype(bf), 'dev', axis=0, tiled=True)  111 us
    ppermute x27, waiting for transfers between devices, send(): return lax.ppermute(v, 'dev', [(d, d ^ bit) for d in range(32)])  83.4 us
    all_gather x1, blocking collectives, local(): small = lax.all_gather(small, 'dev', axis=0, tiled=False)  44.3 us
    all_to_all x2, waiting for transfers between devices, local(): lax.all_to_all(v.reshape(devices, -1, width), 'dev', split_axis=0, concat...  43.8 us
    dot_general x19, matrix products, mm(): lax.dot_general(left, right, (dims, ((), ())), preferred_element_type=jnp...  34.3 us
    pallas_call x1, Pallas kernels, rows_layer(): pl.pallas_call(rows_kernel, grid=(steps,), in_specs=[pl.BlockSpec((1, 1,...  33.8 us
    pallas_call x1, Pallas kernels, forward_layer(): pl.pallas_call(functools.partial(forward_kernel, runs, turn), in_specs=[v...  32 us
    pallas_call x1, Pallas kernels, attend_back(): pl.pallas_call(attend_back_kernel, in_specs=[pl.BlockSpec(memory_space=pl...  25.5 us
  transfers between devices with their start and end apart: 31, of which 14 were waited for; matrix products, arithmetic and copies ran while one was open for 13% of the time, Pallas kernels for 7%

profile of v3, /device:TPU:0, one launch (start us, length us, event | category | flops | bytes accessed | tf_op | source)
XLA Modules:
  0.0 545.3 jit_solution(14943064559999519006)
XLA Ops:
  13.1 44.3 %all_gather.6 = bf16[32,2,1024]{2,1,0:T(2,128)(2,1)S(1)} all-gather(bf16[1,2,1024]{2,1,0:T(2,128)(2,1)S(1)} %all_gather_reshape.3), channel_id=1, replica_groups=mesh['dev'=32] {'dev'}, dimensions={0}, use_global_device_ids=true | all-gather | bytes 135168 | tf_op jit(solution)/shard_map/all_gather | solution.py:652
  58.1 111.2 %all-gather.2.cloned.1.call-done.flat_ref = bf16[12288,1024]{1,0:T(8,128)(2,1)} async-done(((bf16[384,1024]{1,0:T(8,128)(2,1)}), bf16[12288,1024]{1,0:T(8,128)(2,1)}) %all-gather.2.cloned.1.call-update) | async-done | bytes 25165840 | tf_op jit(solution)/shard_map/all_gather | solution.py:658
  169.3 32.0 %shard_map.269 = (bf16[12288,1024]{1,0:T(8,128)(2,1)}, bf16[384,3072]{1,0:T(8,128)(2,1)}, bf16[384,1024]{1,0:T(8,128)(2,1)}, bf16[384,1024]{1,0:T(8,128)(2,1)}, ...) custom-call(bf16[384,1024]{1,0:T(8,128)(2,1)} %h0_ref.3, ...), custom_call_target="tpu_custom_call" | custom-call | flops 10000000000 | bytes 67108864 | tf_op jit(solution)/shard_map/pallas_call | solution.py:353
  201.4 2.1 reshape.319
  203.5 3.0 all-to-all-start
  214.0 18.8 %all-to-all-done = bf16[32,12,1024]{2,1,0:T(8,128)(2,1)S(1)} async-done(((bf16[32,12,1024]{2,1,0:T(8,128)(2,1)}), bf16[32,12,1024]{2,1,0:T(8,128)(2,1)S(1)}, u32[]{:S(2)}, u32[]{:S(2)}) %all-to-all-start) | async-done | bytes 786464 | tf_op jit(solution)/shard_map/all_to_all | solution.py:690
  233.8 33.8 %shard_map.270 = (bf16[384,1024]{1,0:T(8,128)(2,1)}, bf16[384,1024]{1,0:T(8,128)(2,1)}, f32[64,192]{1,0:T(8,128)}, f32[64,64]{1,0:T(8,128)}, f32[64,256]{1,0:T(8...) custom-call(s32[3,1,128]{2,1,0:T(1,128)} %compare_select_fusion.2.pick_ref, ...), custom_call_target="tpu_custom_call" | custom-call | tf_op jit(solution)/shard_map/pallas_call | solution.py:201
  267.6 2.2 reshape.326
  269.8 3.8 all-to-all-start.1
  274.7 25.0 %all-to-all-done.1 = bf16[32,12,1024]{2,1,0:T(8,128)(2,1)} async-done(((bf16[32,12,1024]{2,1,0:T(8,128)(2,1)}), bf16[32,12,1024]{2,1,0:T(8,128)(2,1)}, u32[]{:S(2)}, u32[]{:S(2)}) %all-to-all-start.1) | async-done | bytes 786464 | tf_op jit(solution)/shard_map/all_to_all | solution.py:690
  299.8 1.7 copy.84
  301.5 15.2 %shard_map.271 = (bf16[2,384,2048]{2,1,0:T(8,128)(2,1)}, f32[384,1024]{1,0:T(8,128)S(1)}, bf16[2,384,512]{2,1,0:T(8,128)(2,1)S(1)}, f32[1,1024]{1,0:T(1,128)S(1)}) custom-call(s32[1]{0:T(128)} %bitcast.13.core_ref, bf16[384,1024]{1,0:T(8,128)(2,1)S(1)} %bitcast.172, bf16[384,4096]{1,0:T(8,128)(2,1)} %get-tuple-element.59.slope_ref, f32[384,1024]{1,0:T(8,128)S(1)} %copy-done, ...), custom_call_target="tpu_custom_call" | custom-call | flops 6400000000 | bytes 33554432 | tf_op jit(solution)/shard_map/pallas_call | solution.py:426
  316.7 25.5 %shard_map.272 = (bf16[2,384,1536]{2,1,0:T(8,128)(2,1)S(1)}, f32[384,1024]{1,0:T(8,128)}, f32[1,1024]{1,0:T(1,128)S(1)}) custom-call(s32[1]{0:T(128)} %bitcast.13.core_ref, f32[384,1024]{1,0:T(8,128)S(1)} %get-tuple-element.62.dh_ref, bf16[384,1024]{1,0:T(8,128)(2,1)S(1)} %copy-done.2, f32[1,1024]{1,0:T(1,128)S(1)} %bitcast.176, ...), custom_call_target="tpu_custom_call" | custom-call | flops 6400000000 | bytes 16777216 | tf_op jit(solution)/shard_map/pallas_call | solution.py:506
  342.4 1.9 fusion.41
  344.3 1.9 fusion.44
  346.1 2.0 fusion.47
  349.7 2.1 fusion.29
  352.5 2.0 fusion.35
  355.4 3.4 fusion.49
  359.6 2.4 fusion.51
  362.6 1.9 add_convert_fusion.6
  364.5 1.9 add_convert_fusion.7
  366.4 1.9 add_convert_fusion.8
  370.8 1.9 fusion.17
  376.7 1.7 pad_maximum_fusion
  378.8 5.1 fusion
  383.9 1.7 dynamic-slice_bitcast_fusion.3
  385.6 3.4 copy-done.6
  393.8 7.0 %collective-permute-done.12 = bf16[384,512]{1,0:T(8,128)(2,1)} collective-permute-done((bf16[384,512]{1,0:T(8,128)(2,1)}, bf16[384,512]{1,0:T(8,128)(2,1)}, u32[]{:S(2)}, u32[]{:S(2)}) %collective-permute-start.12) | collective-permute-done | bytes 393248 | tf_op jit(solution)/shard_map/ppermute | solution.py:527
  400.8 2.0 collective-permute-done.13
  402.8 1.6 fusion.25
  407.6 11.2 %collective-permute-done.16 = bf16[768,512]{1,0:T(8,128)(2,1)} collective-permute-done((bf16[768,512]{1,0:T(8,128)(2,1)S(1)}, bf16[768,512]{1,0:T(8,128)(2,1)}, u32[]{:S(2)}, u32[]{:S(2)}) %collective-permute-start.16) | collective-permute-done | bytes 786464 | tf_op jit(solution)/shard_map/ppermute | solution.py:527
  418.8 4.7 collective-permute-done.14
  424.6 3.9 fusion.8
  430.3 1.7 collective-permute-start.19
  434.1 21.3 %collective-permute-done.10 = bf16[384,512]{1,0:T(8,128)(2,1)} collective-permute-done((bf16[384,512]{1,0:T(8,128)(2,1)}, bf16[384,512]{1,0:T(8,128)(2,1)}, u32[]{:S(2)}, u32[]{:S(2)}) %collective-permute-start.10) | collective-permute-done | bytes 393248 | tf_op jit(solution)/shard_map/ppermute | solution.py:527
  455.4 2.1 fusion.24
  459.4 2.7 fusion.7
  475.0 7.7 %collective-permute-done.8 = bf16[384,512]{1,0:T(8,128)(2,1)} collective-permute-done((bf16[384,512]{1,0:T(8,128)(2,1)}, bf16[384,512]{1,0:T(8,128)(2,1)}, u32[]{:S(2)}, u32[]{:S(2)}) %collective-permute-start.8) | collective-permute-done | bytes 393248 | tf_op jit(solution)/shard_map/ppermute | solution.py:527
  482.7 13.2 %collective-permute-done.22 = bf16[768,512]{1,0:T(8,128)(2,1)} collective-permute-done((bf16[768,512]{1,0:T(8,128)(2,1)}, bf16[768,512]{1,0:T(8,128)(2,1)}, u32[]{:S(2)}, u32[]{:S(2)}) %collective-permute-start.22) | collective-permute-done | bytes 786464 | tf_op jit(solution)/shard_map/ppermute | solution.py:527
  495.9 2.8 fusion.4
  498.7 1.6 fusion.23
  504.7 3.1 all-to-all-start.2
  507.9 12.6 %collective-permute-done.25 = bf16[768,512]{1,0:T(8,128)(2,1)} collective-permute-done((bf16[768,512]{1,0:T(8,128)(2,1)}, bf16[768,512]{1,0:T(8,128)(2,1)}, u32[]{:S(2)}, u32[]{:S(2)}) %collective-permute-start.25) | collective-permute-done | bytes 786464 | tf_op jit(solution)/shard_map/ppermute | solution.py:527
  520.8 2.2 collective-permute-done.23
  522.9 2.6 fusion.13
  525.5 2.2 gather_fusion
  534.3 3.7 fusion.74
  (246 shorter events, 66.1 us)
Async XLA Ops:
  7.2 162.1 %all-gather.2.cloned.1.call-start = ((), (), s32[]{:S(2)}) async-start(), calls=%async_computation.3 | async-start | bytes 25952256 | tf_op jit(solution)/shard_map/all_gather | solution.py:658
  203.5 29.3 %all-to-all-start = ((bf16[32,12,1024]{2,1,0:T(8,128)(2,1)}), bf16[32,12,1024]{2,1,0:T(8,128)(2,1)S(1)}, u32[]{:S(2)}, u32[]{:S(2)}) async-start(bf16[32,12,1024]{2,1,0:T(8,128)(2,1)} %reshape.319), calls=%async_computation | async-start | bytes 2097152 | tf_op jit(solution)/shard_map/all_to_all | solution.py:690
  208.1 25.7 %copy-start.24 = (bf16[64,3,8,8]{0,3,2,1:T(8,128)(2,1)}, bf16[64,3,8,8]{0,3,2,1:T(8,128)(2,1)S(1)}, u32[]{:S(2)}) copy-start(bf16[64,3,8,8]{0,3,2,1:T(8,128)(2,1)S(1)} %copy.74) | copy-start | bytes 73732
  208.8 24.9 %copy-start.30 = (bf16[8,8,64]{2,1,0:T(8,128)(2,1)}, bf16[8,8,64]{2,1,0:T(8,128)(2,1)S(1)}, u32[]{:S(2)}) copy-start(bf16[8,8,64]{2,1,0:T(8,128)(2,1)S(1)} %copy.98) | copy-start | bytes 24580
  209.5 24.2 %copy-start.26 = (bf16[64,256]{1,0:T(8,128)(2,1)}, bf16[64,256]{1,0:T(8,128)(2,1)S(1)}, u32[]{:S(2)}) copy-start(bf16[64,256]{1,0:T(8,128)(2,1)S(1)} %slice.286.wu_ref) | copy-start | bytes 98308
  210.3 23.5 %copy-start.23 = (bf16[256,64]{1,0:T(8,128)(2,1)}, bf16[256,64]{1,0:T(8,128)(2,1)S(1)}, u32[]{:S(2)}) copy-start(bf16[256,64]{1,0:T(8,128)(2,1)S(1)} %slice.287.wd_ref) | copy-start | bytes 98308
  269.8 31.7 %copy-start = (f32[384,1024]{1,0:T(8,128)S(1)}, f32[384,1024]{1,0:T(8,128)}, u32[]{:S(2)}) copy-start(f32[384,1024]{1,0:T(8,128)} %get-tuple-element.60.h1_ref) | copy-start | bytes 4718596
  269.8 31.7 %copy-start.4 = (f32[1024]{0:T(1024)S(1)}, f32[1024]{0:T(1024)}, u32[]{:S(2)}) copy-start(f32[1024]{0:T(1024)} %get-tuple-element.146) | copy-start | bytes 12292
  269.8 30.0 %all-to-all-start.1 = ((bf16[32,12,1024]{2,1,0:T(8,128)(2,1)}), bf16[32,12,1024]{2,1,0:T(8,128)(2,1)}, u32[]{:S(2)}, u32[]{:S(2)}) async-start(bf16[32,12,1024]{2,1,0:T(8,128)(2,1)} %reshape.326), calls=%async_computation.1 | async-start | bytes 2097152 | tf_op jit(solution)/shard_map/all_to_all | solution.py:690
  273.7 88.3 %collective-permute-start = (bf16[384,1024]{1,0:T(8,128)(2,1)}, bf16[384,1024]{1,0:T(8,128)(2,1)}, u32[]{:S(2)}, u32[]{:S(2)}) collective-permute-start(bf16[384,1024]{1,0:T(8,128)(2,1)} %get-tuple-element.65), channel_id=1, source_target_pairs={{0,1},{1,0},{2,3},{3,2},{4,5},{5,4},{6,7},{7,6},{8,9},{9,8},{10,11... | collective-permute-start | bytes 2359304 | tf_op jit(solution)/shard_map/ppermute | solution.py:527
  273.9 95.4 %collective-permute-start.2 = (bf16[384,1024]{1,0:T(8,128)(2,1)}, bf16[384,1024]{1,0:T(8,128)(2,1)}, u32[]{:S(2)}, u32[]{:S(2)}) collective-permute-start(bf16[384,1024]{1,0:T(8,128)(2,1)} %get-tuple-element.67), channel_id=1, source_target_pairs={{0,1},{1,0},{2,3},{3,2},{4,5},{5,4},{6,7},{7,6},{8,9},{9,8},{10,11... | collective-permute-start | bytes 2359304 | tf_op jit(solution)/shard_map/ppermute | solution.py:527
  274.2 98.5 %collective-permute-start.4 = (bf16[384,1024]{1,0:T(8,128)(2,1)S(1)}, bf16[384,1024]{1,0:T(8,128)(2,1)S(1)}, u32[]{:S(2)}, u32[]{:S(2)}) collective-permute-start(bf16[384,1024]{1,0:T(8,128)(2,1)S(1)} %copy-done.7), channel_id=1, source_target_pairs={{0,1},{1,0},{2,3},{3,2},{4,5},{5,4},{6,7},{7,6},{8,9},{9,8},{10,11... | collective-permute-start | bytes 2359304 | tf_op jit(solution)/shard_map/ppermute | solution.py:527
  274.4 104.3 %collective-permute-start.6 = (bf16[384,4096]{1,0:T(8,128)(2,1)}, bf16[384,4096]{1,0:T(8,128)(2,1)}, u32[]{:S(2)}, u32[]{:S(2)}) collective-permute-start(bf16[384,4096]{1,0:T(8,128)(2,1)} %get-tuple-element.71), channel_id=1, source_target_pairs={{0,1},{1,0},{2,3},{3,2},{4,5},{5,4},{6,7},{7,6},{8,9},{9,8},{10,11... | collective-permute-start | bytes 9437192 | tf_op jit(solution)/shard_map/ppermute | solution.py:527
  301.5 15.2 %copy-start.1 = (s32[384,1]{1,0:T(8,128)S(1)}, s32[384,1]{1,0:T(8,128)}, u32[]{:S(2)}) copy-start(s32[384,1]{1,0:T(8,128)} %reshape.364.tall_ref) | copy-start | bytes 4612
  301.5 15.2 %copy-start.2 = (bf16[384,1024]{1,0:T(8,128)(2,1)S(1)}, bf16[384,1024]{1,0:T(8,128)(2,1)}, u32[]{:S(2)}) copy-start(bf16[384,1024]{1,0:T(8,128)(2,1)} %h0_ref.3) | copy-start | bytes 2359300
  301.5 15.2 %copy-start.3 = (f32[1024]{0:T(1024)S(1)}, f32[1024]{0:T(1024)}, u32[]{:S(2)}) copy-start(f32[1024]{0:T(1024)} %get-tuple-element.147) | copy-start | bytes 12292
  301.5 15.2 %copy-start.5 = (s32[1,384]{1,0:T(1,128)S(1)}, s32[1,384]{1,0:T(1,128)}, u32[]{:S(2)}) copy-start(s32[1,384]{1,0:T(1,128)} %reshape.317.wide_ref) | copy-start | bytes 4612
  355.3 7.2 %collective-permute-start.1 = (bf16[384,1536]{1,0:T(8,128)(2,1)S(1)}, bf16[384,1536]{1,0:T(8,128)(2,1)S(1)}, u32[]{:S(2)}, u32[]{:S(2)}) collective-permute-start(bf16[384,1536]{1,0:T(8,128)(2,1)S(1)} %get-tuple-element.140), channel_id=1, source_target_pairs={{0,1},{1,0},{2,3},{3,2},{4,5},{5,4},{6,7},{7,6},{8,9},{9,8},{10,11... | collective-permute-start | bytes 3538952 | tf_op jit(solution)/shard_map/ppermute | solution.py:527
  362.0 8.5 %collective-permute-start.3 = (bf16[384,512]{1,0:T(8,128)(2,1)S(1)}, bf16[384,512]{1,0:T(8,128)(2,1)S(1)}, u32[]{:S(2)}, u32[]{:S(2)}) collective-permute-start(bf16[384,512]{1,0:T(8,128)(2,1)S(1)} %slice_bitcast_fusion.4), channel_id=1, source_target_pairs={{0,1},{1,0},{2,3},{3,2},{4,5},{5,4},{6,7},{7,6},{8,9},{9,8},{10,11... | collective-permute-start | bytes 1179656 | tf_op jit(solution)/shard_map/ppermute | solution.py:527
  362.5 10.2 %collective-permute-start.5 = (bf16[384,2048]{1,0:T(8,128)(2,1)}, bf16[384,2048]{1,0:T(8,128)(2,1)S(1)}, u32[]{:S(2)}, u32[]{:S(2)}) collective-permute-start(bf16[384,2048]{1,0:T(8,128)(2,1)} %get-tuple-element.138), channel_id=1, source_target_pairs={{0,1},{1,0},{2,3},{3,2},{4,5},{5,4},{6,7},{7,6},{8,9},{9,8},{10,11... | collective-permute-start | bytes 4718600 | tf_op jit(solution)/shard_map/ppermute | solution.py:527
  370.1 8.7 %collective-permute-start.7 = (bf16[384,512]{1,0:T(8,128)(2,1)S(1)}, bf16[384,512]{1,0:T(8,128)(2,1)S(1)}, u32[]{:S(2)}, u32[]{:S(2)}) collective-permute-start(bf16[384,512]{1,0:T(8,128)(2,1)S(1)} %copy-done.25), channel_id=1, source_target_pairs={{0,1},{1,0},{2,3},{3,2},{4,5},{5,4},{6,7},{7,6},{8,9},{9,8},{10,11... | collective-permute-start | bytes 1179656 | tf_op jit(solution)/shard_map/ppermute | solution.py:527
  389.0 11.8 %collective-permute-start.12 = (bf16[384,512]{1,0:T(8,128)(2,1)}, bf16[384,512]{1,0:T(8,128)(2,1)}, u32[]{:S(2)}, u32[]{:S(2)}) collective-permute-start(bf16[384,512]{1,0:T(8,128)(2,1)} %get-tuple-element.117), channel_id=1, source_target_pairs={{0,4},{1,5},{2,6},{3,7},{4,0},{5,1},{6,2},{7,3},{8,12},{9,13},{10,... | collective-permute-start | bytes 1179656 | tf_op jit(solution)/shard_map/ppermute | solution.py:527
  390.5 12.3 %collective-permute-start.13 = (bf16[384,512]{1,0:T(8,128)(2,1)}, bf16[384,512]{1,0:T(8,128)(2,1)}, u32[]{:S(2)}, u32[]{:S(2)}) collective-permute-start(bf16[384,512]{1,0:T(8,128)(2,1)} %get-tuple-element.120), channel_id=1, source_target_pairs={{0,2},{1,3},{2,0},{3,1},{4,6},{5,7},{6,4},{7,5},{8,10},{9,11},{10,... | collective-permute-start | bytes 1179656 | tf_op jit(solution)/shard_map/ppermute | solution.py:527
  393.2 25.7 %collective-permute-start.16 = (bf16[768,512]{1,0:T(8,128)(2,1)S(1)}, bf16[768,512]{1,0:T(8,128)(2,1)}, u32[]{:S(2)}, u32[]{:S(2)}) collective-permute-start(bf16[768,512]{1,0:T(8,128)(2,1)S(1)} %dynamic-slice_bitcast_fusion), channel_id=1, source_target_pairs={{0,2},{1,3},{2,0},{3,1},{4,6},{5,7},{6,4},{7,5},{8,10},{9,11},{10,... | collective-permute-start | bytes 2359304 | tf_op jit(solution)/shard_map/ppermute | solution.py:527
  405.3 18.3 %collective-permute-start.14 = (bf16[768,512]{1,0:T(8,128)(2,1)}, bf16[768,512]{1,0:T(8,128)(2,1)}, u32[]{:S(2)}, u32[]{:S(2)}) collective-permute-start(bf16[768,512]{1,0:T(8,128)(2,1)} %pad_maximum_fusion.4), channel_id=1, source_target_pairs={{0,8},{1,9},{2,10},{3,11},{4,12},{5,13},{6,14},{7,15},{8,0},{9,1},... | collective-permute-start | bytes 2359304 | tf_op jit(solution)/shard_map/ppermute | solution.py:527
  406.7 17.9 %collective-permute-start.15 = (bf16[768,512]{1,0:T(8,128)(2,1)}, bf16[768,512]{1,0:T(8,128)(2,1)S(1)}, u32[]{:S(2)}, u32[]{:S(2)}) collective-permute-start(bf16[768,512]{1,0:T(8,128)(2,1)} %pad_maximum_fusion.5), channel_id=1, source_target_pairs={{0,4},{1,5},{2,6},{3,7},{4,0},{5,1},{6,2},{7,3},{8,12},{9,13},{10,... | collective-permute-start | bytes 2359304 | tf_op jit(solution)/shard_map/ppermute | solution.py:527
  428.5 26.9 %collective-permute-start.17 = (bf16[768,512]{1,0:T(8,128)(2,1)}, bf16[768,512]{1,0:T(8,128)(2,1)S(1)}, u32[]{:S(2)}, u32[]{:S(2)}) collective-permute-start(bf16[768,512]{1,0:T(8,128)(2,1)} %get-tuple-element.129), channel_id=1, source_target_pairs={{0,2},{1,3},{2,0},{3,1},{4,6},{5,7},{6,4},{7,5},{8,10},{9,11},{10,... | collective-permute-start | bytes 2359304 | tf_op jit(solution)/shard_map/ppermute | solution.py:527
  429.7 25.7 %collective-permute-start.18 = (bf16[768,512]{1,0:T(8,128)(2,1)}, bf16[768,512]{1,0:T(8,128)(2,1)S(1)}, u32[]{:S(2)}, u32[]{:S(2)}) collective-permute-start(bf16[768,512]{1,0:T(8,128)(2,1)} %get-tuple-element.128), channel_id=1, source_target_pairs={{0,4},{1,5},{2,6},{3,7},{4,0},{5,1},{6,2},{7,3},{8,12},{9,13},{10,... | collective-permute-start | bytes 2359304 | tf_op jit(solution)/shard_map/ppermute | solution.py:527
  430.3 25.1 %collective-permute-start.19 = (bf16[768,512]{1,0:T(8,128)(2,1)}, bf16[768,512]{1,0:T(8,128)(2,1)}, u32[]{:S(2)}, u32[]{:S(2)}) collective-permute-start(bf16[768,512]{1,0:T(8,128)(2,1)} %get-tuple-element.127), channel_id=1, source_target_pairs={{0,8},{1,9},{2,10},{3,11},{4,12},{5,13},{6,14},{7,15},{8,0},{9,1},... | collective-permute-start | bytes 2359304 | tf_op jit(solution)/shard_map/ppermute | solution.py:527
  432.1 23.3 %collective-permute-start.10 = (bf16[384,512]{1,0:T(8,128)(2,1)}, bf16[384,512]{1,0:T(8,128)(2,1)}, u32[]{:S(2)}, u32[]{:S(2)}) collective-permute-start(bf16[384,512]{1,0:T(8,128)(2,1)} %get-tuple-element.118), channel_id=1, source_target_pairs={{0,4},{1,5},{2,6},{3,7},{4,0},{5,1},{6,2},{7,3},{8,12},{9,13},{10,... | collective-permute-start | bytes 1179656 | tf_op jit(solution)/shard_map/ppermute | solution.py:527
  433.5 21.9 %collective-permute-start.11 = (bf16[384,512]{1,0:T(8,128)(2,1)}, bf16[384,512]{1,0:T(8,128)(2,1)}, u32[]{:S(2)}, u32[]{:S(2)}) collective-permute-start(bf16[384,512]{1,0:T(8,128)(2,1)} %get-tuple-element.122), channel_id=1, source_target_pairs={{0,2},{1,3},{2,0},{3,1},{4,6},{5,7},{6,4},{7,5},{8,10},{9,11},{10,... | collective-permute-start | bytes 1179656 | tf_op jit(solution)/shard_map/ppermute | solution.py:527
  457.6 25.0 %collective-permute-start.20 = (bf16[768,512]{1,0:T(8,128)(2,1)S(1)}, bf16[768,512]{1,0:T(8,128)(2,1)}, u32[]{:S(2)}, u32[]{:S(2)}) collective-permute-start(bf16[768,512]{1,0:T(8,128)(2,1)S(1)} %pad_maximum_fusion.6), channel_id=1, source_target_pairs={{0,2},{1,3},{2,0},{3,1},{4,6},{5,7},{6,4},{7,5},{8,10},{9,11},{10,... | collective-permute-start | bytes 2359304 | tf_op jit(solution)/shard_map/ppermute | solution.py:527
  458.3 10.5 %copy-start.38 = (f32[64,128]{1,0:T(8,128)S(1)}, f32[64,128]{1,0:T(8,128)}, u32[]{:S(2)}) copy-start(f32[64,128]{1,0:T(8,128)} %get-tuple-element.93) | copy-start | bytes 98308
  458.3 11.1 %copy-start.37 = (f32[64,128]{1,0:T(8,128)S(1)}, f32[64,128]{1,0:T(8,128)}, u32[]{:S(2)}) copy-start(f32[64,128]{1,0:T(8,128)} %get-tuple-element.94) | copy-start | bytes 98308
  458.3 11.7 %copy-start.31 = (f32[256,64]{1,0:T(8,128)S(1)}, f32[256,64]{1,0:T(8,128)}, u32[]{:S(2)}) copy-start(f32[256,64]{1,0:T(8,128)} %get-tuple-element.90) | copy-start | bytes 196612
  458.3 12.4 %copy-start.34 = (f32[64,256]{1,0:T(8,128)S(1)}, f32[64,256]{1,0:T(8,128)}, u32[]{:S(2)}) copy-start(f32[64,256]{1,0:T(8,128)} %get-tuple-element.89) | copy-start | bytes 196612
  458.3 13.1 %copy-start.36 = (f32[64,64]{1,0:T(8,128)S(1)}, f32[64,64]{1,0:T(8,128)}, u32[]{:S(2)}) copy-start(f32[64,64]{1,0:T(8,128)} %get-tuple-element.88) | copy-start | bytes 49156
  458.3 13.7 %copy-start.33 = (f32[64,192]{1,0:T(8,128)S(1)}, f32[64,192]{1,0:T(8,128)}, u32[]{:S(2)}) copy-start(f32[64,192]{1,0:T(8,128)} %get-tuple-element.87) | copy-start | bytes 147460
  458.3 24.4 %collective-permute-start.21 = (bf16[768,512]{1,0:T(8,128)(2,1)S(1)}, bf16[768,512]{1,0:T(8,128)(2,1)}, u32[]{:S(2)}, u32[]{:S(2)}) collective-permute-start(bf16[768,512]{1,0:T(8,128)(2,1)S(1)} %pad_maximum_fusion.7), channel_id=1, source_target_pairs={{0,4},{1,5},{2,6},{3,7},{4,0},{5,1},{6,2},{7,3},{8,12},{9,13},{10,... | collective-permute-start | bytes 2359304 | tf_op jit(solution)/shard_map/ppermute | solution.py:527
  462.1 33.8 %collective-permute-start.22 = (bf16[768,512]{1,0:T(8,128)(2,1)}, bf16[768,512]{1,0:T(8,128)(2,1)}, u32[]{:S(2)}, u32[]{:S(2)}) collective-permute-start(bf16[768,512]{1,0:T(8,128)(2,1)} %fusion.7), channel_id=1, source_target_pairs={{0,16},{1,17},{2,18},{3,19},{4,20},{5,21},{6,22},{7,23},{8,24},{9,... | collective-permute-start | bytes 2359304 | tf_op jit(solution)/shard_map/ppermute | solution.py:527
  463.6 19.1 %collective-permute-start.8 = (bf16[384,512]{1,0:T(8,128)(2,1)}, bf16[384,512]{1,0:T(8,128)(2,1)}, u32[]{:S(2)}, u32[]{:S(2)}) collective-permute-start(bf16[384,512]{1,0:T(8,128)(2,1)} %get-tuple-element.119), channel_id=1, source_target_pairs={{0,4},{1,5},{2,6},{3,7},{4,0},{5,1},{6,2},{7,3},{8,12},{9,13},{10,... | collective-permute-start | bytes 1179656 | tf_op jit(solution)/shard_map/ppermute | solution.py:527
  464.6 18.0 %collective-permute-start.9 = (bf16[384,512]{1,0:T(8,128)(2,1)S(1)}, bf16[384,512]{1,0:T(8,128)(2,1)}, u32[]{:S(2)}, u32[]{:S(2)}) collective-permute-start(bf16[384,512]{1,0:T(8,128)(2,1)S(1)} %get-tuple-element.124), channel_id=1, source_target_pairs={{0,2},{1,3},{2,0},{3,1},{4,6},{5,7},{6,4},{7,5},{8,10},{9,11},{10,... | collective-permute-start | bytes 1179656 | tf_op jit(solution)/shard_map/ppermute | solution.py:527
  498.7 21.8 %collective-permute-start.25 = (bf16[768,512]{1,0:T(8,128)(2,1)}, bf16[768,512]{1,0:T(8,128)(2,1)}, u32[]{:S(2)}, u32[]{:S(2)}) collective-permute-start(bf16[768,512]{1,0:T(8,128)(2,1)} %fusion.4), channel_id=1, source_target_pairs={{0,8},{1,9},{2,10},{3,11},{4,12},{5,13},{6,14},{7,15},{8,0},{9,1},... | collective-permute-start | bytes 2359304 | tf_op jit(solution)/shard_map/ppermute | solution.py:527
  500.4 20.4 %collective-permute-start.24 = (bf16[768,512]{1,0:T(8,128)(2,1)S(1)}, bf16[768,512]{1,0:T(8,128)(2,1)}, u32[]{:S(2)}, u32[]{:S(2)}) collective-permute-start(bf16[768,512]{1,0:T(8,128)(2,1)S(1)} %pad_maximum_fusion.9), channel_id=1, source_target_pairs={{0,4},{1,5},{2,6},{3,7},{4,0},{5,1},{6,2},{7,3},{8,12},{9,13},{10,... | collective-permute-start | bytes 2359304 | tf_op jit(solution)/shard_map/ppermute | solution.py:527
  502.1 20.8 %collective-permute-start.23 = (bf16[768,512]{1,0:T(8,128)(2,1)}, bf16[768,512]{1,0:T(8,128)(2,1)}, u32[]{:S(2)}, u32[]{:S(2)}) collective-permute-start(bf16[768,512]{1,0:T(8,128)(2,1)} %pad_maximum_fusion.8), channel_id=1, source_target_pairs={{0,2},{1,3},{2,0},{3,1},{4,6},{5,7},{6,4},{7,5},{8,10},{9,11},{10,... | collective-permute-start | bytes 2359304 | tf_op jit(solution)/shard_map/ppermute | solution.py:527
  504.7 25.2 %all-to-all-start.2 = ((f32[32,1,1604]{2,1,0:T(1,128)}), f32[32,1,1604]{2,1,0:T(1,128)S(1)}, u32[]{:S(2)}, u32[]{:S(2)}) async-start(f32[32,1,1604]{2,1,0:T(1,128)} %reshape.342), calls=%async_computation.2 | async-start | bytes 425984 | tf_op jit(solution)/shard_map/all_to_all | solution.py:734
  507.8 17.7 %copy-start.39 = (s32[1024]{0:T(1024)S(1)}, s32[1024]{0:T(1024)}, u32[]{:S(2)}) copy-start(s32[1024]{0:T(1024)} %pad_clamp_fusion) | copy-start | bytes 12292
  528.1 3.2 collective-permute-start.26
  (33 other events, 95.7 us)
Sparse Core Ops, SparseCore 0:
  11.5 157.7 all-gather.1

commit v4 on v1

--- a/solution.py
+++ b/solution.py
@@ -2,6 +2,7 @@
 
 import jax
 import jax.numpy as jnp
+import numpy as np
 from jax import lax
 from jax.experimental import pallas as pl
 from jax.experimental.pallas import tpu as pltpu
@@ -19,6 +20,7 @@
 adam_eps = 1e-08
 decay_rate = 0.1
 gain_rate = 0.5
+
 
 def mm(left, right, dims):
     return lax.dot_general(left, right, (dims, ((), ())), preferred_element_type=jnp.float32)
@@ -237,10 +239,434 @@
         pick.reshape(steps, 1, LANES), arrived, og,
         wqp, wqp.T, wop, wop.T, wu, wu.T, wd, wd.T, g3.reshape(feat, 1), g4.reshape(feat, 1),
     )
-    rows_out, back, dwqp, dwop, dwu, dwd, dg3, dg4 = outs
+    return outs
+
+
+def rows_order(dwqp, dwop):
+    feat = dwop.shape[0]
     dwq = dwqp.reshape(feat, 3, 8, HEADS).transpose(0, 1, 3, 2).reshape(feat, 3 * feat)
-    dwo = dwop.reshape(8, HEADS, feat).transpose(1, 0, 2).reshape(feat, feat)
-    return rows_out, back, dwq, dwo, dwu, dwd, jnp.sum(dg3, axis=1), jnp.sum(dg4, axis=1)
+    return dwq, dwop.reshape(8, HEADS, feat).transpose(1, 0, 2).reshape(feat, feat)
+
+
+def placed(flat):
+    if flat < 3072:
+        return flat % 3 * 1024 + flat // 3
+    if flat < 4096 or flat >= 8192:
+        return flat
+    return 4096 + flat % 4 * 1024 + (flat - 4096) // 4
+
+
+def sorted_runs(per):
+    orders, runs = [], []
+    for first in range(0, 12288, per):
+        places = [placed(first + i) for i in range(per)]
+        order = sorted(range(per), key=lambda i: places[i])
+        orders.append(order)
+        for at, i in enumerate(order):
+            if at and places[i] == runs[-1][1] + runs[-1][2] and places[i] % 1024:
+                runs[-1][2] += 1
+            else:
+                runs.append([first + at, places[i], 1])
+    return np.array(orders, np.int32), sorted((tuple(run) for run in runs), key=lambda run: run[1])
+
+
+class Copies:
+    def __init__(self, sems):
+        self.sems, self.used = sems, 0
+
+    def start(self, src, dst):
+        copy = pltpu.make_async_copy(src, dst, self.sems.at[self.used])
+        copy.start()
+        self.used += 1
+        return copy
+
+    def rows(self, src, dst, parts=4):
+        count = src.shape[0] // parts
+        cuts = [pl.ds(i * count, count) for i in range(parts)]
+        return [self.start(src.at[cut], dst.at[cut]) for cut in cuts]
+
+
+def wait(copies):
+    for copy in copies:
+        copy.wait()
+
+
+def load_mats(copies, runs, flat_ref, held, first, width):
+    groups = [[] for _ in range(held.shape[0] // width)]
+    for src, dst, rows in runs:
+        i = dst // width - first
+        if 0 <= i < len(groups):
+            groups[i].append(copies.start(flat_ref.at[pl.ds(src, rows)], held.at[pl.ds(dst - first * width, rows)]))
+    return groups
+
+
+def low_norm(v, gain):
+    center = v - jnp.mean(v, axis=1, keepdims=True)
+    root = lax.rsqrt(jnp.mean(center * center, axis=1, keepdims=True) + norm_eps)
+    return (center * root * gain).astype(jnp.bfloat16)
+
+
+def pull_norm(v, gain, upstream):
+    center = v - jnp.mean(v, axis=1, keepdims=True)
+    root = lax.rsqrt(jnp.mean(center * center, axis=1, keepdims=True) + norm_eps)
+    hat = center * root
+    dhat = upstream * gain
+    inner = jnp.mean(dhat * hat, axis=1, keepdims=True)
+    grad = root * (dhat - jnp.mean(dhat, axis=1, keepdims=True) - hat * inner)
+    return grad, jnp.sum(upstream * hat, axis=0, keepdims=True)
+
+
+def forward_kernel(runs, turn, h0_ref, g1_ref, g2_ref, tall_ref, wide_ref, flat_ref,
+                   joined_out, a1_out, o1_out, a2_out, u1_out, slope_out, h1_out, leave_out,
+                   mats, bias, h0, joined, a1, o1, a2, u1, slope, h1, leave, load_sems, store_sems):
+    f32, bf = jnp.float32, jnp.bfloat16
+    slots, width = h0.shape
+    head = width // HEADS
+    tile = 512
+    loads, stores = Copies(load_sems), Copies(store_sems)
+    first = loads.rows(h0_ref, h0)
+    groups = load_mats(loads, runs, flat_ref, mats, 0, width)
+    saves = []
+    bias[...] = jnp.where(tall_ref[...] == wide_ref[...], 0.0, -jnp.inf)
+    wait(first)
+    a1[...] = low_norm(h0[...].astype(f32), g1_ref[...])
+    saves += stores.rows(a1, a1_out)
+    for i in range(3):
+        wait(groups[i])
+        for t in range(width // tile):
+            cols = slice(i * width + t * tile, i * width + (t + 1) * tile)
+            joined[:, cols] = mm(a1[...], mats[i * width : (i + 1) * width, t * tile : (t + 1) * tile], ((1,), (0,))).astype(bf)
+    saves += stores.rows(joined, joined_out)
+
+    def attend(h, carry):
+        part = lambda i: joined[:, pl.ds(pl.multiple_of(i * width + h * head, head), head)]
+        scores = mm(part(0), part(1), ((1,), (1,))) * head ** (-0.5) + bias[...]
+        weights = jnp.exp(scores - jnp.max(scores, axis=1, keepdims=True))
+        chance = weights * (1.0 / jnp.sum(weights, axis=1, keepdims=True))
+        o1[:, pl.ds(pl.multiple_of(h * head, head), head)] = mm(chance.astype(bf), part(2), ((1,), (0,))).astype(bf)
+        return carry
+
+    lax.fori_loop(0, HEADS, attend, 0, unroll=2)
+    saves += stores.rows(o1, o1_out)
+    wait(groups[3])
+    for t in range(width // tile):
+        cols = slice(t * tile, (t + 1) * tile)
+        h1[:, cols] = h0[:, cols].astype(f32) + mm(o1[...], mats[3 * width : 4 * width, cols], ((1,), (0,)))
+    saves += stores.rows(h1, h1_out)
+    a2[...] = low_norm(h1[...], g2_ref[...])
+    saves += stores.rows(a2, a2_out)
+    for i in range(4):
+        wait(groups[4 + i])
+        for t in range(width // tile):
+            cols = slice(t * tile, (t + 1) * tile)
+            active, rise = gelu_pair(mm(a2[...], mats[(4 + i) * width : (5 + i) * width, cols], ((1,), (0,))))
+            cols = slice(i * width + t * tile, i * width + (t + 1) * tile)
+            u1[:, cols] = active.astype(bf)
+            slope[:, cols] = rise.astype(bf)
+            saves.append(stores.start(u1.at[:, cols], u1_out.at[:, cols]))
+            saves.append(stores.start(slope.at[:, cols], slope_out.at[:, cols]))
+    for i in range(4):
+        wait(groups[8 + i])
+    to, source = (lax.broadcasted_iota(jnp.int32, (slots, slots), axis) for axis in (0, 1))
+    hot = (source == to % turn * (slots // turn) + to // turn).astype(f32).astype(bf)
+    for t in range(width // tile):
+        cols = slice(t * tile, (t + 1) * tile)
+        h2 = (h1[:, cols] + mm(u1[...], mats[8 * width :, cols], ((1,), (0,)))).astype(bf)
+        leave[:, cols] = mm(hot, h2, ((1,), (0,))).astype(bf)
+        saves.append(stores.start(leave.at[:, cols], leave_out.at[:, cols]))
+    wait(saves)
+
+
+def own_kernel(kernel, operands, small, outs, scratch, limit, flops):
+    def spec(v):
+        space = pltpu.SMEM if v.ndim == 1 else pltpu.VMEM
+        return pl.BlockSpec(memory_space=space)
+
+    anywhere = pl.BlockSpec(memory_space=pl.ANY)
+    tiny = pl.BlockSpec(memory_space=pltpu.VMEM)
+    return pl.pallas_call(
+        kernel,
+        in_specs=[spec(v) if n in small else anywhere for n, v in enumerate(operands)],
+        out_specs=[tiny if out.shape[0] == 1 else anywhere for out in outs],
+        out_shape=outs,
+        scratch_shapes=scratch,
+        compiler_params=pltpu.CompilerParams(vmem_limit_bytes=limit * 2**20),
+        cost_estimate=pl.CostEstimate(flops=flops, bytes_accessed=40 * 2**20, transcendentals=10**6),
+    )(*operands)
+
+
+def forward_layer(runs, turn, h0, g1, g2, labels, flat):
+    f32, bf = jnp.float32, jnp.bfloat16
+    slots, width = h0.shape
+    shape, vmem = jax.ShapeDtypeStruct, pltpu.VMEM
+    sizes = [(3, bf), (1, bf), (1, bf), (1, bf), (4, bf), (4, bf), (1, f32), (1, bf)]
+    return own_kernel(
+        functools.partial(forward_kernel, runs, turn),
+        (h0, g1.reshape(1, -1), g2.reshape(1, -1), labels.reshape(-1, 1), labels.reshape(1, -1), flat),
+        (1, 2, 3, 4),
+        [shape((slots, n * width), kind) for n, kind in sizes],
+        [vmem(flat.shape, bf), vmem((slots, slots), f32), vmem((slots, width), bf)]
+        + [vmem((slots, n * width), kind) for n, kind in sizes]
+        + [pltpu.SemaphoreType.DMA((len(runs) + 4,)), pltpu.SemaphoreType.DMA((38,))],
+        60,
+        10**10,
+    )
+
+
+def widen_back_kernel(runs, turn, core_ref, g2_ref, raw_ref, slope_ref, h1_ref, flat_ref,
+                      dpre_own, dpre_peer, dh_out, low_own, low_peer, gz_own, gz_peer, dg_ref,
+                      ups, downs, raw, gz, slope, h1, dpre, dh, low, gz_sides, da, load_sems, store_sems):
+    f32, bf = jnp.float32, jnp.bfloat16
+    width = gz.shape[1]
+    half = width // 2
+    core = core_ref[0]
+    loads, stores = Copies(load_sems), Copies(store_sems)
+    raw_copies = loads.rows(raw_ref, raw)
+    down_copies = load_mats(loads, runs, flat_ref, downs, 8, width)
+    slope_copies = [
+        loads.start(slope_ref.at[:, pl.ds(i * width, width)], slope.at[:, pl.ds(i * width, width)]) for i in range(4)
+    ]
+    up_copies = load_mats(loads, runs, flat_ref, ups, 4, width)
+    h1_copies = loads.rows(h1_ref, h1)
+    wait(raw_copies)
+    slots = gz.shape[0]
+    slot, source = (lax.broadcasted_iota(jnp.int32, (slots, slots), axis) for axis in (0, 1))
+    devices = slots // turn
+    hot = (source == slot % devices * turn + slot // devices).astype(f32).astype(bf)
+    gz[...] = mm(hot, raw[...], ((1,), (0,))).astype(bf)
+    saves = []
+    for s in range(2):
+        gz_sides[s ^ core] = gz[:, s * half : (s + 1) * half]
+    saves += [stores.start(gz_sides.at[0], gz_own), stores.start(gz_sides.at[1], gz_peer)]
+    for i in range(4):
+        wait(down_copies[i] + [slope_copies[i]] + up_copies[i])
+        for s in range(2):
+            hidden = slice(i * width + s * half, i * width + (s + 1) * half)
+            du = mm(gz[...], downs[hidden], ((1,), (1,)))
+            piece = (slope[:, hidden].astype(f32) * du).astype(bf)
+            dpre[s ^ core, :, i * half : (i + 1) * half] = piece
+            term = mm(piece, ups[i * width : (i + 1) * width, s * half : (s + 1) * half], ((1,), (1,)))
+            da[...] = term if i == s == 0 else da[...] + term
+        lanes = pl.ds(i * half, half)
+        saves += [stores.start(dpre.at[0, :, lanes], dpre_own.at[:, lanes]), stores.start(dpre.at[1, :, lanes], dpre_peer.at[:, lanes])]
+    wait(h1_copies)
+    grad, dg_ref[...] = pull_norm(h1[...], g2_ref[...], da[...])
+    dh[...] = gz[...].astype(f32) + grad
+    saves += stores.rows(dh, dh_out)
+    for s in range(2):
+        low[s ^ core] = dh[:, s * half : (s + 1) * half].astype(bf)
+    saves += [stores.start(low.at[0], low_own), stores.start(low.at[1], low_peer)]
+    wait(saves)
+
+
+def widen_back(runs, turn, core, raw, slope, h1, g2, flat):
+    f32, bf = jnp.float32, jnp.bfloat16
+    slots, width = raw.shape
+    half = width // 2
+    shape, vmem = jax.ShapeDtypeStruct, pltpu.VMEM
+    side = shape((slots, half), bf)
+    ups = sum(4 <= dst // width < 12 for _, dst, _ in runs)
+    return own_kernel(
+        functools.partial(widen_back_kernel, runs, turn),
+        (core, g2.reshape(1, -1), raw, slope, h1, flat),
+        (0, 1),
+        [shape((slots, 2 * width), bf)] * 2 + [shape((slots, width), f32)] + [side] * 4 + [shape((1, width), f32)],
+        [
+            vmem((4 * width, width), bf), vmem((4 * width, width), bf), vmem((slots, width), bf), vmem((slots, width), bf),
+            vmem((slots, 4 * width), bf),
+            vmem((slots, width), f32), vmem((2, slots, 2 * width), bf), vmem((slots, width), f32), vmem((2, slots, half), bf),
+            vmem((2, slots, half), bf), vmem((slots, width), f32),
+            pltpu.SemaphoreType.DMA((ups + 12,)), pltpu.SemaphoreType.DMA((16,)),
+        ],
+        60,
+        64 * 10**8,
+    )
+
+
+def attend_back_kernel(runs, core_ref, g1_ref, tall_ref, wide_ref, dh_ref, h0_ref, joined_ref, flat_ref,
+                       own_out, peer_out, grad_out, dg_ref,
+                       mats, bias, dh, h0, joined, dblend, dj, sides, load_sems, store_sems):
+    f32, bf = jnp.float32, jnp.bfloat16
+    slots, width = dh.shape
+    head = width // HEADS
+    half = width // 2
+    tile = 512
+    scaling = head ** (-0.5)
+    core = core_ref[0]
+    loads, stores = Copies(load_sems), Copies(store_sems)
+    dh_copies = loads.rows(dh_ref, dh)
+    out_copies = load_mats(loads, runs, flat_ref, mats.at[pl.ds(3 * width, width)], 3, width)
+    joined_copies = loads.rows(joined_ref, joined)
+    mat_copies = load_mats(loads, runs, flat_ref, mats.at[pl.ds(0, 3 * width)], 0, width)
+    h0_copies = loads.rows(h0_ref, h0)
+    bias[...] = jnp.where(tall_ref[...] == wide_ref[...], 0.0, -jnp.inf)
+    wait(dh_copies)
+    gz = dh[...].astype(bf)
+    wait(out_copies[0])
+    for t in range(width // tile):
+        rows = slice(3 * width + t * tile, 3 * width + (t + 1) * tile)
+        dblend[:, t * tile : (t + 1) * tile] = mm(gz, mats[rows], ((1,), (1,))).astype(bf)
+    wait(joined_copies)
+
+    def attend(h, carry):
+        lanes = lambda i: pl.ds(pl.multiple_of(i * width + h * head, head), head)
+        q, k, v = (joined[:, lanes(i)] for i in range(3))
+        do = dblend[:, pl.ds(pl.multiple_of(h * head, head), head)]
+        scores = mm(q, k, ((1,), (1,))) * scaling + bias[...]
+        weights = jnp.exp(scores - jnp.max(scores, axis=1, keepdims=True))
+        chance = weights * (1.0 / jnp.sum(weights, axis=1, keepdims=True))
+        dchance = mm(do, v, ((1,), (1,)))
+        dot = jnp.sum(chance * dchance, axis=1, keepdims=True)
+        ds = (chance * (dchance - dot)).astype(bf)
+        parts = (
+            mm(ds, k, ((1,), (0,))) * scaling,
+            mm(ds, q, ((0,), (0,))) * scaling,
+            mm(chance.astype(bf), do, ((0,), (0,))),
+        )
+        per_side = HEADS // 2
+        for i in range(3):
+            part = parts[i].astype(bf)
+            dj[:, lanes(i)] = part
+            sides[(h // per_side) ^ core, :, pl.ds(pl.multiple_of(i * half + h % per_side * head, head), head)] = part
+        return carry
+
+    lax.fori_loop(0, HEADS, attend, 0, unroll=2)
+    saves = [stores.start(sides.at[1], peer_out), stores.start(sides.at[0], own_out)]
+    da = None
+    for i in range(3):
+        wait(mat_copies[i])
+        term = mm(dj[:, i * width : (i + 1) * width], mats[i * width : (i + 1) * width], ((1,), (1,)))
+        da = term if da is None else da + term
+    wait(h0_copies)
+    grad, dg_ref[...] = pull_norm(h0[...].astype(f32), g1_ref[...], da)
+    dh[...] = dh[...] + grad
+    wait(saves + stores.rows(dh, grad_out))
+
+
+def attend_back(runs, core, dh, h0, g1, joined, labels, flat):
+    f32, bf = jnp.float32, jnp.bfloat16
+    slots, width = dh.shape
+    shape, vmem = jax.ShapeDtypeStruct, pltpu.VMEM
+    mats = sum(dst // width < 4 for _, dst, _ in runs)
+    return own_kernel(
+        functools.partial(attend_back_kernel, runs),
+        (core, g1.reshape(1, -1), labels.reshape(-1, 1), labels.reshape(1, -1), dh, h0, joined, flat),
+        (0, 1, 2, 3),
+        [shape((slots, 3 * width // 2), bf)] * 2 + [shape((slots, width), f32), shape((1, width), f32)],
+        [
+            vmem((4 * width, width), bf), vmem((slots, slots), f32), vmem((slots, width), f32), vmem((slots, width), bf),
+            vmem((slots, 3 * width), bf), vmem((slots, width), bf), vmem((slots, 3 * width), bf),
+            vmem((2, slots, 3 * width // 2), bf),
+            pltpu.SemaphoreType.DMA((mats + 12,)), pltpu.SemaphoreType.DMA((6,)),
+        ],
+        60,
+        64 * 10**8,
+    )
+
+
+def chip_outer_kernel(runs, jobs, shift, *refs):
+    bf = jnp.bfloat16
+    count = 4 * len(jobs)
+    operands, out, held = refs[:count], refs[count], refs[count + 1 : 2 * count + 1]
+    result, load_sems, store_sems = refs[2 * count + 1 :]
+    loads, stores = Copies(load_sems), Copies(store_sems)
+    arrivals = [loads.rows(ref, v, 2) for ref, v in zip(operands, held, strict=True)]
+    width, lanes_out = 1024, result.shape[1]
+    half, tile = width // 2, 512
+    saves, done = [], 0
+    for n, (first, matrices, tall) in enumerate(jobs):
+        left, left_peer, right, right_peer = held[4 * n : 4 * n + 4]
+        for copies in arrivals[4 * n : 4 * n + 4]:
+            wait(copies)
+        for i in range(matrices):
+            from_lane = (0 if tall else i * half) + shift
+            lanes = slice(from_lane, from_lane + lanes_out)
+            for t in range(width // tile):
+                cols = (i if tall else 0) * width + t * tile
+                cols = slice(cols, cols + tile)
+                term = mm(left[:, cols], right[:, lanes], ((0,), (0,))) + mm(left_peer[:, cols], right_peer[:, lanes], ((0,), (0,)))
+                result[done * width + t * tile : done * width + (t + 1) * tile, :] = term.astype(bf)
+            for to, place, rows in runs:
+                if place // width == first + i:
+                    part = result.at[pl.ds(done * width + place % width, rows)]
+                    saves.append(stores.start(part, out.at[pl.ds(to, rows)]))
+            done += 1
+    wait(saves)
+
+
+def chip_outer(runs, jobs, operands, shift, lanes):
+    bf = jnp.bfloat16
+    anywhere = pl.BlockSpec(memory_space=pl.ANY)
+    return pl.pallas_call(
+        functools.partial(chip_outer_kernel, runs, jobs, shift),
+        in_specs=[anywhere] * len(operands),
+        out_specs=anywhere,
+        out_shape=jax.ShapeDtypeStruct((12288, lanes), bf),
+        scratch_shapes=[pltpu.VMEM(v.shape, bf) for v in operands]
+        + [
+            pltpu.VMEM((12288, lanes), bf),
+            pltpu.SemaphoreType.DMA((2 * len(operands),)),
+            pltpu.SemaphoreType.DMA((len(runs),)),
+        ],
+        compiler_params=pltpu.CompilerParams(vmem_limit_bytes=60 * 2**20),
+        cost_estimate=pl.CostEstimate(flops=6 * 10**9, bytes_accessed=24 * 2**20, transcendentals=0),
+    )(*operands)
+
+
+CORE = 1
+
+
+def send(v, bit):
+    return lax.ppermute(v, "dev", [(d, d ^ bit) for d in range(32)])
+
+
+def after(*values):
+    return lax.optimization_barrier(values)
+
+
+def sum_blocks(blocks, chip):
+    f32, bf = jnp.float32, jnp.bfloat16
+    half = blocks.shape[1] // 2
+    block = lambda m: lax.dynamic_index_in_dim(blocks, chip ^ (m >> 1), 0, keepdims=False)
+    total = lambda *parts: sum(part.astype(f32) for part in parts)
+    both = lambda one, two: jnp.concatenate([one.astype(bf), two.astype(bf)])
+
+    across_far, up_far, across = block(30), block(14), block(24)
+    a, b, c, d, e = after(
+        send(across_far[:half], 4), send(across_far[half:], 2), send(across, 8), send(up_far[:half], 4), send(up_far[half:], 2)
+    )
+    side, other = block(26), block(28)
+    across_x, across_y = both(total(side[:half], a), side[half:]), both(other[:half], total(other[half:], b))
+    side, other = block(10), block(12)
+    up_x, up_y = both(total(side[:half], d), side[half:]), both(other[:half], total(other[half:], e))
+    over = total(block(16), c)
+
+    a, b, c = after(send(across_x, 8), send(up_x, 2), send(up_y, 4))
+    over_x, up = total(block(18), a), total(block(8), b, c).astype(bf)
+    over_far, own_far = block(22), block(6)
+    a, b, c, d, e = after(
+        send(across_y, 8), send(over_far[:half], 4), send(over_far[half:], 2), send(own_far[:half], 4), send(own_far[half:], 2)
+    )
+    other = total(block(20), a)
+    over_x, over_y = both(total(over_x[:half], b), over_x[half:]), both(other[:half], total(other[half:], c))
+    side, other = block(2), block(4)
+    own_x, own_y = both(total(side[:half], d), side[half:]), both(other[:half], total(other[half:], e))
+
+    a, b, c = after(send(over_x, 2), send(over_y, 4), send(up, 8))
+    own = total(block(0), c)
+    over = total(over, a, b).astype(bf)
+    return total(own, send(over, 16), send(own_x, 2), send(own_y, 4))
+
+
+def owned_rows(own, device):
+    core, chip = device % 2, device // 2
+    half = own.shape[0] // 2
+    orders, _ = sorted_runs(2 * half)
+    order = lax.dynamic_index_in_dim(jnp.asarray(np.argsort(orders, axis=1).astype(np.int32)), chip, 0, keepdims=False)
+    own = jnp.take(own, order, axis=0)
+    mine = lax.dynamic_slice_in_dim(own, core * half, half, 0)
+    peer = send(lax.dynamic_slice_in_dim(own, (1 - core) * half, half, 0), CORE)
+    return jnp.where(core == 0, jnp.concatenate([mine, peer], axis=1), jnp.concatenate([peer, mine], axis=1))
 
 
 def fwd_mul(left, right):
@@ -249,23 +675,6 @@
 
 def outer(left, right):
     return mm(left, right, ((0,), (0,)))
-
-
-def backmul(upstream, weight):
-    return mm(upstream, weight, ((1,), (1,)))
-
-
-def norm_parts(inputs):
-    center = inputs - jnp.mean(inputs, axis=-1, keepdims=True)
-    root = lax.rsqrt(jnp.mean(center * center, axis=-1, keepdims=True) + norm_eps)
-    return center * root, root
-
-
-def norm_pull(hat, root, gain, upstream):
-    dhat = upstream * gain
-    inner = jnp.mean(dhat * hat, axis=-1, keepdims=True)
-    grad = root * (dhat - jnp.mean(dhat, axis=-1, keepdims=True) - hat * inner)
-    return grad, jnp.sum(upstream * hat, axis=0)
 
 
 def running(values):
@@ -307,20 +716,28 @@
     per_peer = slots // devices
     rows_even = out_grad.shape[0]
     rows_pad = -(-rows_even // LANES) * LANES
-    head = width // HEADS
-    scaling = head ** (-0.5)
+    grid = devices == 32 and width == 1024 and slots == 384
 
     n_rows, n_gains = rows_weights.shape[0], norm_gains.shape[0]
     small = jnp.concatenate([rows_weights, norm_gains]).astype(bf)
     small = jnp.pad(small, (0, -small.shape[0] % 1024)).reshape(-1, 1024)
-    small = lax.all_gather(small, "dev", axis=0, tiled=False).reshape(devices, -1)
+    small = lax.all_gather(small, "dev", axis=0, tiled=False)
+    shard = sets_weights.astype(bf).reshape(-1, width)
+    if grid:
+        orders, runs = sorted_runs(shard.shape[0])
+        order = lax.dynamic_index_in_dim(jnp.asarray(orders), device, 0, keepdims=False)
+        hot = (order[:, None] == jnp.arange(shard.shape[0], dtype=jnp.int32)[None, :]).astype(bf)
+        flat = lax.all_gather(fwd_mul(hot, shard).astype(bf), "dev", axis=0, tiled=True)
+    else:
+        flat = lax.all_gather(shard, "dev", axis=0, tiled=True)
+        parts = lambda v, n: v.reshape(width, n, width).transpose(1, 0, 2).reshape(n * width, width)
+        flat = jnp.concatenate(
+            [parts(flat[: 3 * width], 3), flat[3 * width : 4 * width], parts(flat[4 * width : 8 * width], 4), flat[8 * width :]]
+        )
+        runs = [(i * width, i * width, width) for i in range(12)]
+    small = small.reshape(devices, -1)
     full_rows = small[:, :n_rows].reshape(-1)
     full_gains = small[:, n_rows : n_rows + n_gains].reshape(-1).astype(f32)
-    flat = lax.all_gather(sets_weights.astype(bf).reshape(-1, width), "dev", axis=0, tiled=True)
-    wq1 = flat[: 3 * width].reshape(width, 3 * width)
-    wo1 = flat[3 * width : 4 * width]
-    wu1 = flat[4 * width : 8 * width].reshape(width, 4 * width)
-    wd1 = flat[8 * width :]
     square = feat * feat
     wq2 = full_rows[: 3 * square].reshape(feat, 3 * feat)
     wo2 = full_rows[3 * square : 4 * square].reshape(feat, feat)
@@ -337,68 +754,58 @@
     ends = running(counts)
     spot = jnp.arange(rows_pad, dtype=jnp.int32)
     past = (ends[None, :] <= spot[:, None]).astype(jnp.int32)
-    source = jnp.sum(past, axis=1)
     start = jnp.sum(past * counts[None, :], axis=1)
-    pick = jnp.where(spot < rows_even, source * per_peer + spot - start, -1)
-
-    h0 = cells_in.astype(f32)
-    hat1, root1 = norm_parts(h0)
-    a1 = (hat1 * g1).astype(bf)
-    joined = fwd_mul(a1, wq1).astype(bf).reshape(slots, 3, HEADS, head)
-    queries, key_rows, values = joined[:, 0], joined[:, 1], joined[:, 2]
-    related = labels[:, None] == labels[None, :]
-    scores = jnp.einsum("qhd,khd->hqk", queries, key_rows, preferred_element_type=f32) * scaling
-    scores = jnp.where(related[None], scores, -jnp.inf)
-    weights = jnp.exp(scores - jnp.max(scores, axis=-1, keepdims=True))
-    chance = weights / jnp.sum(weights, axis=-1, keepdims=True)
-    chance_low = chance.astype(bf)
-    o1 = jnp.einsum("hqk,khd->qhd", chance_low, values, preferred_element_type=f32).astype(bf).reshape(slots, width)
-    h1 = h0 + fwd_mul(o1, wo1)
-    hat2, root2 = norm_parts(h1)
-    a2 = (hat2 * g2).astype(bf)
-    active, slope = gelu_pair(fwd_mul(a2, wu1))
-    u1 = active.astype(bf)
-    h2 = h1 + fwd_mul(u1, wd1)
-
-    outgoing = h2.astype(bf).reshape(per_peer, devices, width).transpose(1, 0, 2)
-    arrived = lax.all_to_all(outgoing, "dev", split_axis=0, concat_axis=0, tiled=True)
+    pick = jnp.where(spot < rows_even, jnp.sum(past, axis=1) * per_peer + spot - start, -1)
+
+    joined, a1, o1, a2, u1, slope, h1, leaving = forward_layer(runs, per_peer, cells_in, g1, g2, labels, flat)
+
+    swap = lambda v: lax.all_to_all(
+        v.reshape(devices, -1, LANES), "dev", split_axis=0, concat_axis=0, tiled=True
+    ).reshape(slots, width)
     og = jnp.pad(out_grad, ((0, rows_pad - rows_even), (0, 0)))
     rows_out, back, dq2, do2, du2, dd2, dg3, dg4 = rows_layer(
-        pick, arrived.reshape(slots, width), og, wq2, wo2, wu2, wd2, g3, g4
+        pick, swap(leaving), og, wq2, wo2, wu2, wd2, g3, g4
     )
     rows_out = rows_out[:rows_even]
-    rows_flat = jnp.concatenate([dq2.reshape(-1), do2.reshape(-1), du2.reshape(-1), dd2.reshape(-1)])
-    extra = rows_flat.reshape(devices, n_rows).astype(bf)
-    extra = jnp.pad(extra, ((0, 0), (0, -n_rows % width))).reshape(devices, -1, width)
-    payload = jnp.concatenate([back.reshape(devices, per_peer, width), extra], axis=1)
-    returned = lax.all_to_all(payload, "dev", split_axis=0, concat_axis=0, tiled=True)
-    grad = returned[:, :per_peer].transpose(1, 0, 2).reshape(slots, width).astype(f32)
-    rows_grad = jnp.sum(returned[:, per_peer:].reshape(devices, -1)[:, :n_rows].astype(f32), axis=0)
-
-    gz = grad.astype(bf)
-    dd1 = outer(u1, gz).astype(bf)
-    dpre = (slope * backmul(gz, wd1)).astype(bf)
-    du1 = outer(a2, dpre).astype(bf)
-    dh, dg2 = norm_pull(hat2, root2, g2, backmul(dpre, wu1))
-    grad = grad + dh
-    gz = grad.astype(bf)
-    do1 = outer(o1, gz).astype(bf)
-    dblend = backmul(gz, wo1).astype(bf).reshape(slots, HEADS, head)
-    dchance = jnp.einsum("qhd,khd->hqk", dblend, values, preferred_element_type=f32)
-    dot = jnp.sum(chance * dchance, axis=-1, keepdims=True)
-    dscores = (chance * (dchance - dot)).astype(bf)
-    dq = jnp.einsum("hqk,khd->qhd", dscores, key_rows, preferred_element_type=f32) * scaling
-    dk = jnp.einsum("hqk,qhd->khd", dscores, queries, preferred_element_type=f32) * scaling
-    dv = jnp.einsum("hqk,qhd->khd", chance_low, dblend, preferred_element_type=f32)
-    djoined = jnp.concatenate([part.reshape(slots, width).astype(bf) for part in (dq, dk, dv)], axis=1)
-    dq1 = outer(a1, djoined).astype(bf)
-    dh, dg1 = norm_pull(hat1, root1, g1, backmul(djoined, wq1))
-    cells_grad = grad + dh
-
-    full = jnp.concatenate([dq1.reshape(-1, width), do1, du1.reshape(-1, width), dd1])
-    sets_grad = lax.psum_scatter(full, "dev", scatter_dimension=0, tiled=True).astype(f32).reshape(-1)
-    gains = jnp.concatenate([dg1, dg2, dg3, dg4]).reshape(devices, 1, n_gains)
-    gains_grad = jnp.sum(lax.all_to_all(gains, "dev", split_axis=0, concat_axis=0, tiled=True), axis=(0, 1))
+    raw = swap(back)
+
+    core = device % 2
+    which = core.reshape(1)
+    half = width // 2
+    pair = lambda v: (v, send(v, CORE))
+    if grid:
+        raw, *pairs = after(raw, *pair(u1), *pair(a2), *pair(o1), *pair(a1))
+        u1, a2, o1, a1 = (tuple(pairs[i : i + 2]) for i in (0, 2, 4, 6))
+    *dpre, dh1, low_own, low_peer, gz_own, gz_peer, dg2 = widen_back(runs, per_peer, which, raw, slope, h1, g2, flat)
+    *dj, cells_grad, dg1 = attend_back(runs, which, dh1, cells_in, g1, joined, labels, flat)
+    if grid:
+        chip_runs = sorted_runs(2 * shard.shape[0])[1]
+        swapped = lambda own, peer: (own, send(peer, CORE))
+        operands = u1 + swapped(gz_own, gz_peer) + a2 + swapped(*dpre) + o1 + swapped(low_own, low_peer)
+        operands = operands + a1 + swapped(*dj)
+        jobs = ((8, 4, True), (4, 4, False), (3, 1, True), (0, 3, False))
+        lanes = half // 2
+        blocks = [chip_outer(chip_runs, jobs, operands, shift, lanes).reshape(16, -1, lanes) for shift in (0, lanes)]
+        blocks[0], dq2, do2, du2, dd2, dg3, dg4 = after(blocks[0], dq2, do2, du2, dd2, dg3, dg4)
+        sums = [sum_blocks(part, device // 2) for part in blocks]
+        sets_grad = owned_rows(jnp.concatenate(sums, axis=1), device).reshape(-1)
+    else:
+
+        def sides(own, peer, n):
+            both = jnp.where(core == 0, jnp.stack([own, peer]), jnp.stack([peer, own]))
+            return both.reshape(2, slots, n, half).transpose(1, 2, 0, 3).reshape(slots, -1)
+
+        dq1, du1 = outer(a1, sides(*dj, 3)), outer(a2, sides(*dpre, 4))
+        gz = sides(gz_own, gz_peer, 1)
+        full = jnp.concatenate([dq1.reshape(-1, width), outer(o1, dh1.astype(bf)), du1.reshape(-1, width), outer(u1, gz)])
+        sets_grad = lax.psum_scatter(full.astype(bf), "dev", scatter_dimension=0, tiled=True).astype(f32).reshape(-1)
+
+    rows_flat = jnp.concatenate([v.reshape(-1) for v in (*rows_order(dq2, do2), du2, dd2)])
+    dg3, dg4 = jnp.sum(dg3, axis=1), jnp.sum(dg4, axis=1)
+    gains = jnp.concatenate([dg1[0], dg2[0], dg3, dg4]).reshape(devices, n_gains)
+    extra = jnp.concatenate([rows_flat.reshape(devices, n_rows), gains], axis=1).reshape(devices, 1, -1)
+    extra = jnp.sum(lax.all_to_all(extra, "dev", split_axis=0, concat_axis=0, tiled=True), axis=(0, 1))
+    rows_grad, gains_grad = extra[:n_rows], extra[n_rows:]
 
     set_index = device * sets_grad.shape[0] + jnp.arange(sets_grad.shape[0], dtype=jnp.int32)
     row_index = device * n_rows + jnp.arange(n_rows, dtype=jnp.int32)

time: 725 us -> 494 us (0.68)
  waiting for transfers between devices: 356 us -> 182 us
  matrix products: 91 us -> 1.51 us
  Pallas kernels: 33.8 us -> 120 us
  starting transfers between devices: 5.73 us -> 52.9 us
  local copies, waits for them, and re-layouts: 89.1 us -> 47.3 us
  blocking collectives: 74.1 us -> 44.3 us
  other arithmetic: 55.4 us -> 26.3 us
    reduce_scatter x1 -> x0, waiting for transfers between devices: 222 us -> none  [local(): lax.psum_scatter(full, 'dev', scatter_dimension=0, tiled=True).astype(f32)]
    pallas_call x0 -> x5, Pallas kernels: none -> 85.8 us  [the longest x3 61.8 us: own_kernel(): pl.pallas_call(kernel, in_specs=[spec(v) if n in small else anywhere for...]
    dot_general x12 -> x1, matrix products: 78.3 us -> 1.51 us  [mm(): lax.dot_general(left, right, (dims, ((), ())), preferred_element_type=jnp...]
    ppermute x0 -> x47, waiting for transfers between devices: none -> 46.2 us  [send(): return lax.ppermute(v, 'dev', [(d, d ^ bit) for d in range(32)])]
    reshape x13 -> x12, local copies, waits for them, and re-layouts: 55.9 us -> 11.3 us  [the longest x2 4.3 us: local(): v.reshape(devices, -1, LANES)]
    ppermute x0 -> x47, starting transfers between devices: none -> 42.4 us  [send(): return lax.ppermute(v, 'dev', [(d, d ^ bit) for d in range(32)])]
    concatenate x3 -> x19, other arithmetic: 35.6 us -> 0.65 us  [the longest x16 0.44 us: sum_blocks(): both = lambda one, two: jnp.concatenate([one.astype(bf), two.astype(bf)])]
    all_to_all x1 -> x0, blocking collectives: 29.8 us -> none  [local(): lax.all_to_all(payload, 'dev', split_axis=0, concat_axis=0, tiled=True)]
  transfers between devices with their start and end apart: 4 -> 51, of which waited for: 4 -> 22; matrix products, arithmetic and copies ran while one was open for 4% -> 12% of each run, Pallas kernels for 0% -> 13%
where the time goes in v4:
time: 494 us; the launch traced here: 489 us
  waiting for transfers between devices  182 us (37%)
  Pallas kernels  120 us (24%)
  starting transfers between devices  52.9 us (11%)
  local copies, waits for them, and re-layouts  47.3 us (10%)
  blocking collectives  44.3 us (9%)
  other arithmetic  26.3 us (5%)
  between operations  15.2 us (3%)
    all_gather x1, waiting for transfers between devices, local(): lax.all_gather(fwd_mul(hot, shard).astype(bf), 'dev', axis=0, tiled=True)  111 us
    pallas_call x3, Pallas kernels, own_kernel(): pl.pallas_call(kernel, in_specs=[spec(v) if n in small else anywhere for...  61.8 us
    ppermute x47, waiting for transfers between devices, send(): return lax.ppermute(v, 'dev', [(d, d ^ bit) for d in range(32)])  46.2 us
    all_gather x1, blocking collectives, local(): small = lax.all_gather(small, 'dev', axis=0, tiled=False)  44.3 us
    ppermute x47, starting transfers between devices, send(): return lax.ppermute(v, 'dev', [(d, d ^ bit) for d in range(32)])  42.4 us
    pallas_call x1, Pallas kernels, rows_layer(): pl.pallas_call(rows_kernel, grid=(steps,), in_specs=[pl.BlockSpec((1, 1,...  33.7 us
    all_to_all x2, waiting for transfers between devices, local(): lax.all_to_all(v.reshape(devices, -1, LANES), 'dev', split_axis=0, concat...  24.1 us
    pallas_call x2, Pallas kernels, chip_outer(): pl.pallas_call(functools.partial(chip_outer_kernel, runs, jobs, shift), i...  24 us
  transfers between devices with their start and end apart: 51, of which 22 were waited for; matrix products, arithmetic and copies ran while one was open for 12% of the time, Pallas kernels for 13%

profile of v4, /device:TPU:0, one launch (start us, length us, event | category | flops | bytes accessed | tf_op | source)
XLA Modules:
  0.0 488.5 jit_solution(11972523760284952989)
XLA Ops:
  13.1 44.3 %all_gather.6 = bf16[32,2,1024]{2,1,0:T(2,128)(2,1)S(1)} all-gather(bf16[1,2,1024]{2,1,0:T(2,128)(2,1)S(1)} %all_gather_reshape.3), channel_id=1, replica_groups=mesh['dev'=32] {'dev'}, dimensions={0}, use_global_device_ids=true | all-gather | bytes 135168 | tf_op jit(solution)/shard_map/all_gather | solution.py:724
  58.2 111.2 %all-gather.2.cloned.1.call-done.flat_ref = bf16[12288,1024]{1,0:T(8,128)(2,1)} async-done(((bf16[384,1024]{1,0:T(8,128)(2,1)}), bf16[12288,1024]{1,0:T(8,128)(2,1)}) %all-gather.2.cloned.1.call-update) | async-done | bytes 25165840 | tf_op jit(solution)/shard_map/all_gather | solution.py:730
  169.3 26.7 %shard_map.269 = (bf16[384,3072]{1,0:T(8,128)(2,1)}, bf16[384,1024]{1,0:T(8,128)(2,1)}, bf16[384,1024]{1,0:T(8,128)(2,1)}, bf16[384,1024]{1,0:T(8,128)(2,1)}, bf...) custom-call(bf16[384,1024]{1,0:T(8,128)(2,1)} %h0_ref.3, ...), custom_call_target="tpu_custom_call" | custom-call | flops 10000000000 | bytes 41943040 | tf_op jit(solution)/shard_map/pallas_call | solution.py:387
  196.3 2.1 reshape.324
  198.5 3.6 all-to-all-start
  215.5 2.1 pad.9.og_ref
  218.1 4.4 all-to-all-done
  222.6 2.1 reshape.325.arrived_ref
  224.7 33.7 %shard_map.270 = (bf16[384,1024]{1,0:T(8,128)(2,1)}, bf16[384,1024]{1,0:T(8,128)(2,1)}, f32[64,192]{1,0:T(8,128)}, f32[64,64]{1,0:T(8,128)}, f32[64,256]{1,0:T(8...) custom-call(s32[3,1,128]{2,1,0:T(1,128)} %compare_select_fusion.2.pick_ref, ...), custom_call_target="tpu_custom_call" | custom-call | tf_op jit(solution)/shard_map/pallas_call | solution.py:201
  258.5 2.2 reshape.331
  260.7 4.1 all-to-all-start.1
  265.7 19.7 %all-to-all-done.1 = bf16[32,96,128]{2,1,0:T(8,128)(2,1)} async-done(((bf16[32,96,128]{2,1,0:T(8,128)(2,1)}), bf16[32,96,128]{2,1,0:T(8,128)(2,1)}, u32[]{:S(2)}, u32[]{:S(2)}) %all-to-all-start.1) | async-done | bytes 786464 | tf_op jit(solution)/shard_map/all_to_all | solution.py:762
  285.3 2.1 reshape.332.raw_ref
  287.5 18.2 %shard_map.271 = (bf16[384,2048]{1,0:T(8,128)(2,1)}, bf16[384,2048]{1,0:T(8,128)(2,1)}, f32[384,1024]{1,0:T(8,128)}, bf16[384,512]{1,0:T(8,128)(2,1)}, bf16[384,...) custom-call(s32[1]{0:T(128)} %bitcast.13.core_ref, ...), custom_call_target="tpu_custom_call" | custom-call | flops 6400000000 | bytes 41943040 | tf_op jit(solution)/shard_map/pallas_call | solution.py:387
  305.8 16.9 %shard_map.272 = (bf16[384,1536]{1,0:T(8,128)(2,1)}, bf16[384,1536]{1,0:T(8,128)(2,1)}, f32[384,1024]{1,0:T(8,128)}, f32[1,1024]{1,0:T(1,128)}) custom-call(s32[1]{0:T(128)} %bitcast.13.core_ref, f32[1,1024]{1,0:T(1,128)} %bitcast.228, s32[384,1]{1,0:T(8,128)} %reshape.373.tall_ref, s32[1,384]{1,0:T(1,128)} %reshape.322.wide_ref, ...), custom_call_target="tpu_custom_call" | custom-call | flops 6400000000 | bytes 41943040 | tf_op jit(solution)/shard_map/pallas_call | solution.py:387
  328.8 11.9 %shard_map.274 = bf16[12288,256]{1,0:T(8,128)(2,1)} custom-call(bf16[384,4096]{1,0:T(8,128)(2,1)} %get-tuple-element.106.refs_0_, bf16[384,4096]{1,0:T(8,128)(2,1)} %copy-done, bf16[384,512]{1,0:T(8,128)(2,1)} %get-tuple-element.108.refs_2_, bf16[384,512]{1,0:T(8,128)(2,1)} %copy-done.7, bf16[384,1024]{1,0:T(8,128)(2,1)} %get-tuple-element.110.refs_4_, ...), custom_call_target="tpu_custom_call" | custom-call | flops 6000000000 | bytes 25165824 | tf_op jit(solution)/shard_map/pallas_call | solution.py:600
  340.7 2.9 dynamic-slice_bitcast_fusion.13
  350.2 12.1 %shard_map.273 = bf16[12288,256]{1,0:T(8,128)(2,1)} custom-call(bf16[384,4096]{1,0:T(8,128)(2,1)} %get-tuple-element.106.refs_0_, bf16[384,4096]{1,0:T(8,128)(2,1)} %copy-done, bf16[384,512]{1,0:T(8,128)(2,1)} %get-tuple-element.108.refs_2_, bf16[384,512]{1,0:T(8,128)(2,1)} %copy-done.7, bf16[384,1024]{1,0:T(8,128)(2,1)} %get-tuple-element.110.refs_4_, ...), custom_call_target="tpu_custom_call" | custom-call | flops 6000000000 | bytes 25165824 | tf_op jit(solution)/shard_map/pallas_call | solution.py:600
  362.4 1.8 dynamic-slice_bitcast_fusion.1
  365.2 2.9 dynamic-slice_bitcast_fusion.33
  369.9 1.9 collective-permute-start.10
  378.2 2.1 collective-permute-start.36
  385.7 2.4 collective-permute-start.17
  388.1 1.6 collective-permute-start.18
  389.9 2.4 collective-permute-start.19
  394.0 1.7 fusion.28
  395.8 1.9 collective-permute-start.32
  398.2 2.0 collective-permute-start.34
  400.4 5.2 %collective-permute-done.16 = bf16[768,256]{1,0:T(8,128)(2,1)S(1)} collective-permute-done((bf16[768,256]{1,0:T(8,128)(2,1)S(1)}, bf16[768,256]{1,0:T(8,128)(2,1)S(1)}, u32[]{:S(2)}, u32[]{:S(2)}) %collective-permute-start.16) | collective-permute-done | bytes 393248 | tf_op jit(solution)/shard_map/ppermute | solution.py:620
  405.6 1.7 fusion.34
  408.6 2.6 collective-permute-done.32
  411.2 1.7 fusion.9
  414.0 1.9 collective-permute-start.41
  415.9 2.5 collective-permute-done.13
  418.4 1.7 collective-permute-start.42
  420.1 2.4 collective-permute-done.15
  422.5 1.6 fusion.17
  425.2 3.1 collective-permute-done.40
  428.4 1.6 collective-permute-start.23
  432.7 4.1 collective-permute-done.21
  437.2 2.1 collective-permute-done.22
  445.8 2.8 all-to-all-start.2
  448.6 14.3 %collective-permute-done.43 = bf16[768,256]{1,0:T(8,128)(2,1)} collective-permute-done((bf16[768,256]{1,0:T(8,128)(2,1)S(1)}, bf16[768,256]{1,0:T(8,128)(2,1)}, u32[]{:S(2)}, u32[]{:S(2)}) %collective-permute-start.43) | collective-permute-done | bytes 393248 | tf_op jit(solution)/shard_map/ppermute | solution.py:620
  462.9 1.7 fusion.12
  464.7 2.5 collective-permute-done.24
  467.2 1.6 fusion.20
  468.9 2.2 gather_fusion
  477.7 3.7 fusion.56
  (249 shorter events, 71.3 us)
Async XLA Ops:
  7.2 162.1 %all-gather.2.cloned.1.call-start = ((), (), s32[]{:S(2)}) async-start(), calls=%async_computation.3 | async-start | bytes 25952256 | tf_op jit(solution)/shard_map/all_gather | solution.py:730
  196.0 91.5 %collective-permute-start = (bf16[384,4096]{1,0:T(8,128)(2,1)}, bf16[384,4096]{1,0:T(8,128)(2,1)S(1)}, u32[]{:S(2)}, u32[]{:S(2)}) collective-permute-start(bf16[384,4096]{1,0:T(8,128)(2,1)} %get-tuple-element.106.refs_0_), channel_id=1, source_target_pairs={{0,1},{1,0},{2,3},{3,2},{4,5},{5,4},{6,7},{7,6},{8,9},{9,8},{10,11... | collective-permute-start | bytes 9437192 | tf_op jit(solution)/shard_map/ppermute | solution.py:620
  198.5 24.1 %all-to-all-start = ((bf16[32,96,128]{2,1,0:T(8,128)(2,1)}), bf16[32,96,128]{2,1,0:T(8,128)(2,1)}, u32[]{:S(2)}, u32[]{:S(2)}) async-start(bf16[32,96,128]{2,1,0:T(8,128)(2,1)} %reshape.324), calls=%async_computation | async-start | bytes 1572864 | tf_op jit(solution)/shard_map/all_to_all | solution.py:762
  260.7 24.7 %all-to-all-start.1 = ((bf16[32,96,128]{2,1,0:T(8,128)(2,1)}), bf16[32,96,128]{2,1,0:T(8,128)(2,1)}, u32[]{:S(2)}, u32[]{:S(2)}) async-start(bf16[32,96,128]{2,1,0:T(8,128)(2,1)} %reshape.331), calls=%async_computation.1 | async-start | bytes 1572864 | tf_op jit(solution)/shard_map/all_to_all | solution.py:762
  264.7 22.7 %collective-permute-start.1 = (bf16[384,1024]{1,0:T(8,128)(2,1)}, bf16[384,1024]{1,0:T(8,128)(2,1)}, u32[]{:S(2)}, u32[]{:S(2)}) collective-permute-start(bf16[384,1024]{1,0:T(8,128)(2,1)} %get-tuple-element.110.refs_4_), channel_id=1, source_target_pairs={{0,1},{1,0},{2,3},{3,2},{4,5},{5,4},{6,7},{7,6},{8,9},{9,8},{10,11... | collective-permute-start | bytes 2359304 | tf_op jit(solution)/shard_map/ppermute | solution.py:620
  265.2 22.3 %collective-permute-start.2 = (bf16[384,1024]{1,0:T(8,128)(2,1)}, bf16[384,1024]{1,0:T(8,128)(2,1)}, u32[]{:S(2)}, u32[]{:S(2)}) collective-permute-start(bf16[384,1024]{1,0:T(8,128)(2,1)} %get-tuple-element.114.refs_8_), channel_id=1, source_target_pairs={{0,1},{1,0},{2,3},{3,2},{4,5},{5,4},{6,7},{7,6},{8,9},{9,8},{10,11... | collective-permute-start | bytes 2359304 | tf_op jit(solution)/shard_map/ppermute | solution.py:620
  265.3 22.2 %collective-permute-start.3 = (bf16[384,1024]{1,0:T(8,128)(2,1)}, bf16[384,1024]{1,0:T(8,128)(2,1)}, u32[]{:S(2)}, u32[]{:S(2)}) collective-permute-start(bf16[384,1024]{1,0:T(8,128)(2,1)} %get-tuple-element.118.refs_12_), channel_id=1, source_target_pairs={{0,1},{1,0},{2,3},{3,2},{4,5},{5,4},{6,7},{7,6},{8,9},{9,8},{10,11... | collective-permute-start | bytes 2359304 | tf_op jit(solution)/shard_map/ppermute | solution.py:620
  305.7 21.4 %collective-permute-start.5 = (bf16[384,2048]{1,0:T(8,128)(2,1)}, bf16[384,2048]{1,0:T(8,128)(2,1)S(1)}, u32[]{:S(2)}, u32[]{:S(2)}) collective-permute-start(bf16[384,2048]{1,0:T(8,128)(2,1)} %get-tuple-element.113), channel_id=1, source_target_pairs={{0,1},{1,0},{2,3},{3,2},{4,5},{5,4},{6,7},{7,6},{8,9},{9,8},{10,11... | collective-permute-start | bytes 4718600 | tf_op jit(solution)/shard_map/ppermute | solution.py:620
  322.8 4.4 collective-permute-start.7
  343.6 24.5 %collective-permute-start.27 = (bf16[384,256]{1,0:T(8,128)(2,1)}, bf16[384,256]{1,0:T(8,128)(2,1)}, u32[]{:S(2)}, u32[]{:S(2)}) collective-permute-start(bf16[384,256]{1,0:T(8,128)(2,1)} %get-tuple-element.216), channel_id=1, source_target_pairs={{0,4},{1,5},{2,6},{3,7},{4,0},{5,1},{6,2},{7,3},{8,12},{9,13},{10,... | collective-permute-start | bytes 589832 | tf_op jit(solution)/shard_map/ppermute | solution.py:620
  345.2 24.0 %collective-permute-start.28 = (bf16[384,256]{1,0:T(8,128)(2,1)}, bf16[384,256]{1,0:T(8,128)(2,1)}, u32[]{:S(2)}, u32[]{:S(2)}) collective-permute-start(bf16[384,256]{1,0:T(8,128)(2,1)} %get-tuple-element.222), channel_id=1, source_target_pairs={{0,2},{1,3},{2,0},{3,1},{4,6},{5,7},{6,4},{7,5},{8,10},{9,11},{10,... | collective-permute-start | bytes 589832 | tf_op jit(solution)/shard_map/ppermute | solution.py:620
  347.6 24.8 %collective-permute-start.29 = (bf16[768,256]{1,0:T(8,128)(2,1)S(1)}, bf16[768,256]{1,0:T(8,128)(2,1)S(1)}, u32[]{:S(2)}, u32[]{:S(2)}) collective-permute-start(bf16[768,256]{1,0:T(8,128)(2,1)S(1)} %dynamic-slice_bitcast_fusion), channel_id=1, source_target_pairs={{0,8},{1,9},{2,10},{3,11},{4,12},{5,13},{6,14},{7,15},{8,0},{9,1},... | collective-permute-start | bytes 1179656 | tf_op jit(solution)/shard_map/ppermute | solution.py:620
  347.7 22.2 %collective-permute-start.30 = (bf16[384,256]{1,0:T(8,128)(2,1)}, bf16[384,256]{1,0:T(8,128)(2,1)}, u32[]{:S(2)}, u32[]{:S(2)}) collective-permute-start(bf16[384,256]{1,0:T(8,128)(2,1)} %get-tuple-element.215), channel_id=1, source_target_pairs={{0,4},{1,5},{2,6},{3,7},{4,0},{5,1},{6,2},{7,3},{8,12},{9,13},{10,... | collective-permute-start | bytes 589832 | tf_op jit(solution)/shard_map/ppermute | solution.py:620
  349.1 22.7 %collective-permute-start.31 = (bf16[384,256]{1,0:T(8,128)(2,1)S(1)}, bf16[384,256]{1,0:T(8,128)(2,1)}, u32[]{:S(2)}, u32[]{:S(2)}) collective-permute-start(bf16[384,256]{1,0:T(8,128)(2,1)S(1)} %get-tuple-element.221), channel_id=1, source_target_pairs={{0,2},{1,3},{2,0},{3,1},{4,6},{5,7},{6,4},{7,5},{8,10},{9,11},{10,... | collective-permute-start | bytes 589832 | tf_op jit(solution)/shard_map/ppermute | solution.py:620
  368.1 7.1 %collective-permute-start.8 = (bf16[384,256]{1,0:T(8,128)(2,1)S(1)}, bf16[384,256]{1,0:T(8,128)(2,1)S(1)}, u32[]{:S(2)}, u32[]{:S(2)}) collective-permute-start(bf16[384,256]{1,0:T(8,128)(2,1)S(1)} %get-tuple-element.194), channel_id=1, source_target_pairs={{0,4},{1,5},{2,6},{3,7},{4,0},{5,1},{6,2},{7,3},{8,12},{9,13},{10,... | collective-permute-start | bytes 589832 | tf_op jit(solution)/shard_map/ppermute | solution.py:620
  369.2 9.0 %collective-permute-start.9 = (bf16[384,256]{1,0:T(8,128)(2,1)}, bf16[384,256]{1,0:T(8,128)(2,1)}, u32[]{:S(2)}, u32[]{:S(2)}) collective-permute-start(bf16[384,256]{1,0:T(8,128)(2,1)} %get-tuple-element.200), channel_id=1, source_target_pairs={{0,2},{1,3},{2,0},{3,1},{4,6},{5,7},{6,4},{7,5},{8,10},{9,11},{10,... | collective-permute-start | bytes 589832 | tf_op jit(solution)/shard_map/ppermute | solution.py:620
  369.9 12.4 %collective-permute-start.10 = (bf16[768,256]{1,0:T(8,128)(2,1)}, bf16[768,256]{1,0:T(8,128)(2,1)}, u32[]{:S(2)}, u32[]{:S(2)}) collective-permute-start(bf16[768,256]{1,0:T(8,128)(2,1)} %dynamic-slice_bitcast_fusion.1), channel_id=1, source_target_pairs={{0,8},{1,9},{2,10},{3,11},{4,12},{5,13},{6,14},{7,15},{8,0},{9,1},... | collective-permute-start | bytes 1179656 | tf_op jit(solution)/shard_map/ppermute | solution.py:620
  371.8 8.5 %collective-permute-start.11 = (bf16[384,256]{1,0:T(8,128)(2,1)}, bf16[384,256]{1,0:T(8,128)(2,1)}, u32[]{:S(2)}, u32[]{:S(2)}) collective-permute-start(bf16[384,256]{1,0:T(8,128)(2,1)} %get-tuple-element.193), channel_id=1, source_target_pairs={{0,4},{1,5},{2,6},{3,7},{4,0},{5,1},{6,2},{7,3},{8,12},{9,13},{10,... | collective-permute-start | bytes 589832 | tf_op jit(solution)/shard_map/ppermute | solution.py:620
  372.4 9.3 %collective-permute-start.12 = (bf16[384,256]{1,0:T(8,128)(2,1)}, bf16[384,256]{1,0:T(8,128)(2,1)}, u32[]{:S(2)}, u32[]{:S(2)}) collective-permute-start(bf16[384,256]{1,0:T(8,128)(2,1)} %get-tuple-element.199), channel_id=1, source_target_pairs={{0,2},{1,3},{2,0},{3,1},{4,6},{5,7},{6,4},{7,5},{8,10},{9,11},{10,... | collective-permute-start | bytes 589832 | tf_op jit(solution)/shard_map/ppermute | solution.py:620
  375.2 18.6 %collective-permute-start.35 = (bf16[768,256]{1,0:T(8,128)(2,1)S(1)}, bf16[768,256]{1,0:T(8,128)(2,1)}, u32[]{:S(2)}, u32[]{:S(2)}) collective-permute-start(bf16[768,256]{1,0:T(8,128)(2,1)S(1)} %pad_maximum_fusion.12), channel_id=1, source_target_pairs={{0,8},{1,9},{2,10},{3,11},{4,12},{5,13},{6,14},{7,15},{8,0},{9,1},... | collective-permute-start | bytes 1179656 | tf_op jit(solution)/shard_map/ppermute | solution.py:620
  378.2 7.5 %collective-permute-start.36 = (bf16[384,256]{1,0:T(8,128)(2,1)}, bf16[384,256]{1,0:T(8,128)(2,1)S(1)}, u32[]{:S(2)}, u32[]{:S(2)}) collective-permute-start(bf16[384,256]{1,0:T(8,128)(2,1)} %get-tuple-element.213), channel_id=1, source_target_pairs={{0,4},{1,5},{2,6},{3,7},{4,0},{5,1},{6,2},{7,3},{8,12},{9,13},{10,... | collective-permute-start | bytes 589832 | tf_op jit(solution)/shard_map/ppermute | solution.py:620
  380.3 7.8 %collective-permute-start.37 = (bf16[384,256]{1,0:T(8,128)(2,1)}, bf16[384,256]{1,0:T(8,128)(2,1)S(1)}, u32[]{:S(2)}, u32[]{:S(2)}) collective-permute-start(bf16[384,256]{1,0:T(8,128)(2,1)} %get-tuple-element.219), channel_id=1, source_target_pairs={{0,2},{1,3},{2,0},{3,1},{4,6},{5,7},{6,4},{7,5},{8,10},{9,11},{10,... | collective-permute-start | bytes 589832 | tf_op jit(solution)/shard_map/ppermute | solution.py:620
  381.7 8.2 %collective-permute-start.38 = (bf16[384,256]{1,0:T(8,128)(2,1)}, bf16[384,256]{1,0:T(8,128)(2,1)S(1)}, u32[]{:S(2)}, u32[]{:S(2)}) collective-permute-start(bf16[384,256]{1,0:T(8,128)(2,1)} %get-tuple-element.212), channel_id=1, source_target_pairs={{0,4},{1,5},{2,6},{3,7},{4,0},{5,1},{6,2},{7,3},{8,12},{9,13},{10,... | collective-permute-start | bytes 589832 | tf_op jit(solution)/shard_map/ppermute | solution.py:620
  382.2 10.0 %collective-permute-start.39 = (bf16[384,256]{1,0:T(8,128)(2,1)}, bf16[384,256]{1,0:T(8,128)(2,1)S(1)}, u32[]{:S(2)}, u32[]{:S(2)}) collective-permute-start(bf16[384,256]{1,0:T(8,128)(2,1)} %get-tuple-element.218), channel_id=1, source_target_pairs={{0,2},{1,3},{2,0},{3,1},{4,6},{5,7},{6,4},{7,5},{8,10},{9,11},{10,... | collective-permute-start | bytes 589832 | tf_op jit(solution)/shard_map/ppermute | solution.py:620
  385.7 10.1 %collective-permute-start.17 = (bf16[384,256]{1,0:T(8,128)(2,1)}, bf16[384,256]{1,0:T(8,128)(2,1)S(1)}, u32[]{:S(2)}, u32[]{:S(2)}) collective-permute-start(bf16[384,256]{1,0:T(8,128)(2,1)} %get-tuple-element.191), channel_id=1, source_target_pairs={{0,4},{1,5},{2,6},{3,7},{4,0},{5,1},{6,2},{7,3},{8,12},{9,13},{10,... | collective-permute-start | bytes 589832 | tf_op jit(solution)/shard_map/ppermute | solution.py:620
  388.1 9.6 %collective-permute-start.18 = (bf16[384,256]{1,0:T(8,128)(2,1)}, bf16[384,256]{1,0:T(8,128)(2,1)S(1)}, u32[]{:S(2)}, u32[]{:S(2)}) collective-permute-start(bf16[384,256]{1,0:T(8,128)(2,1)} %get-tuple-element.197), channel_id=1, source_target_pairs={{0,2},{1,3},{2,0},{3,1},{4,6},{5,7},{6,4},{7,5},{8,10},{9,11},{10,... | collective-permute-start | bytes 589832 | tf_op jit(solution)/shard_map/ppermute | solution.py:620
  389.9 8.3 %collective-permute-start.19 = (bf16[384,256]{1,0:T(8,128)(2,1)}, bf16[384,256]{1,0:T(8,128)(2,1)S(1)}, u32[]{:S(2)}, u32[]{:S(2)}) collective-permute-start(bf16[384,256]{1,0:T(8,128)(2,1)} %get-tuple-element.190), channel_id=1, source_target_pairs={{0,4},{1,5},{2,6},{3,7},{4,0},{5,1},{6,2},{7,3},{8,12},{9,13},{10,... | collective-permute-start | bytes 589832 | tf_op jit(solution)/shard_map/ppermute | solution.py:620
  392.3 8.1 %collective-permute-start.20 = (bf16[384,256]{1,0:T(8,128)(2,1)}, bf16[384,256]{1,0:T(8,128)(2,1)S(1)}, u32[]{:S(2)}, u32[]{:S(2)}) collective-permute-start(bf16[384,256]{1,0:T(8,128)(2,1)} %get-tuple-element.196), channel_id=1, source_target_pairs={{0,2},{1,3},{2,0},{3,1},{4,6},{5,7},{6,4},{7,5},{8,10},{9,11},{10,... | collective-permute-start | bytes 589832 | tf_op jit(solution)/shard_map/ppermute | solution.py:620
  393.8 11.8 %collective-permute-start.16 = (bf16[768,256]{1,0:T(8,128)(2,1)S(1)}, bf16[768,256]{1,0:T(8,128)(2,1)S(1)}, u32[]{:S(2)}, u32[]{:S(2)}) collective-permute-start(bf16[768,256]{1,0:T(8,128)(2,1)S(1)} %pad_maximum_fusion.4), channel_id=1, source_target_pairs={{0,8},{1,9},{2,10},{3,11},{4,12},{5,13},{6,14},{7,15},{8,0},{9,1},... | collective-permute-start | bytes 1179656 | tf_op jit(solution)/shard_map/ppermute | solution.py:620
  395.8 15.4 %collective-permute-start.32 = (bf16[768,256]{1,0:T(8,128)(2,1)S(1)}, bf16[768,256]{1,0:T(8,128)(2,1)S(1)}, u32[]{:S(2)}, u32[]{:S(2)}) collective-permute-start(bf16[768,256]{1,0:T(8,128)(2,1)S(1)} %pad_maximum_fusion.9), channel_id=1, source_target_pairs={{0,8},{1,9},{2,10},{3,11},{4,12},{5,13},{6,14},{7,15},{8,0},{9,1},... | collective-permute-start | bytes 1179656 | tf_op jit(solution)/shard_map/ppermute | solution.py:620
  397.7 13.5 %collective-permute-start.33 = (bf16[768,256]{1,0:T(8,128)(2,1)S(1)}, bf16[768,256]{1,0:T(8,128)(2,1)S(1)}, u32[]{:S(2)}, u32[]{:S(2)}) collective-permute-start(bf16[768,256]{1,0:T(8,128)(2,1)S(1)} %pad_maximum_fusion.10), channel_id=1, source_target_pairs={{0,2},{1,3},{2,0},{3,1},{4,6},{5,7},{6,4},{7,5},{8,10},{9,11},{10,... | collective-permute-start | bytes 1179656 | tf_op jit(solution)/shard_map/ppermute | solution.py:620
  398.2 12.9 %collective-permute-start.34 = (bf16[768,256]{1,0:T(8,128)(2,1)S(1)}, bf16[768,256]{1,0:T(8,128)(2,1)S(1)}, u32[]{:S(2)}, u32[]{:S(2)}) collective-permute-start(bf16[768,256]{1,0:T(8,128)(2,1)S(1)} %pad_maximum_fusion.11), channel_id=1, source_target_pairs={{0,4},{1,5},{2,6},{3,7},{4,0},{5,1},{6,2},{7,3},{8,12},{9,13},{10,... | collective-permute-start | bytes 1179656 | tf_op jit(solution)/shard_map/ppermute | solution.py:620
  407.3 11.1 %collective-permute-start.13 = (bf16[768,256]{1,0:T(8,128)(2,1)S(1)}, bf16[768,256]{1,0:T(8,128)(2,1)S(1)}, u32[]{:S(2)}, u32[]{:S(2)}) collective-permute-start(bf16[768,256]{1,0:T(8,128)(2,1)S(1)} %pad_maximum_fusion.1), channel_id=1, source_target_pairs={{0,8},{1,9},{2,10},{3,11},{4,12},{5,13},{6,14},{7,15},{8,0},{9,1},... | collective-permute-start | bytes 1179656 | tf_op jit(solution)/shard_map/ppermute | solution.py:620
  407.8 12.3 %collective-permute-start.14 = (bf16[768,256]{1,0:T(8,128)(2,1)S(1)}, bf16[768,256]{1,0:T(8,128)(2,1)S(1)}, u32[]{:S(2)}, u32[]{:S(2)}) collective-permute-start(bf16[768,256]{1,0:T(8,128)(2,1)S(1)} %pad_maximum_fusion.2), channel_id=1, source_target_pairs={{0,2},{1,3},{2,0},{3,1},{4,6},{5,7},{6,4},{7,5},{8,10},{9,11},{10,... | collective-permute-start | bytes 1179656 | tf_op jit(solution)/shard_map/ppermute | solution.py:620
  411.2 11.3 %collective-permute-start.15 = (bf16[768,256]{1,0:T(8,128)(2,1)S(1)}, bf16[768,256]{1,0:T(8,128)(2,1)S(1)}, u32[]{:S(2)}, u32[]{:S(2)}) collective-permute-start(bf16[768,256]{1,0:T(8,128)(2,1)S(1)} %pad_maximum_fusion.3), channel_id=1, source_target_pairs={{0,4},{1,5},{2,6},{3,7},{4,0},{5,1},{6,2},{7,3},{8,12},{9,13},{10,... | collective-permute-start | bytes 1179656 | tf_op jit(solution)/shard_map/ppermute | solution.py:620
  413.0 15.4 %collective-permute-start.40 = (bf16[768,256]{1,0:T(8,128)(2,1)S(1)}, bf16[768,256]{1,0:T(8,128)(2,1)S(1)}, u32[]{:S(2)}, u32[]{:S(2)}) collective-permute-start(bf16[768,256]{1,0:T(8,128)(2,1)S(1)} %pad_maximum_fusion.13), channel_id=1, source_target_pairs={{0,2},{1,3},{2,0},{3,1},{4,6},{5,7},{6,4},{7,5},{8,10},{9,11},{10,... | collective-permute-start | bytes 1179656 | tf_op jit(solution)/shard_map/ppermute | solution.py:620
  414.0 16.9 %collective-permute-start.41 = (bf16[768,256]{1,0:T(8,128)(2,1)S(1)}, bf16[768,256]{1,0:T(8,128)(2,1)S(1)}, u32[]{:S(2)}, u32[]{:S(2)}) collective-permute-start(bf16[768,256]{1,0:T(8,128)(2,1)S(1)} %pad_maximum_fusion.14), channel_id=1, source_target_pairs={{0,4},{1,5},{2,6},{3,7},{4,0},{5,1},{6,2},{7,3},{8,12},{9,13},{10,... | collective-permute-start | bytes 1179656 | tf_op jit(solution)/shard_map/ppermute | solution.py:620
  418.4 12.5 %collective-permute-start.42 = (bf16[768,256]{1,0:T(8,128)(2,1)S(1)}, bf16[768,256]{1,0:T(8,128)(2,1)S(1)}, u32[]{:S(2)}, u32[]{:S(2)}) collective-permute-start(bf16[768,256]{1,0:T(8,128)(2,1)S(1)} %get-tuple-element.207), channel_id=1, source_target_pairs={{0,8},{1,9},{2,10},{3,11},{4,12},{5,13},{6,14},{7,15},{8,0},{9,1},... | collective-permute-start | bytes 1179656 | tf_op jit(solution)/shard_map/ppermute | solution.py:620
  424.2 12.6 %collective-permute-start.21 = (bf16[768,256]{1,0:T(8,128)(2,1)S(1)}, bf16[768,256]{1,0:T(8,128)(2,1)S(1)}, u32[]{:S(2)}, u32[]{:S(2)}) collective-permute-start(bf16[768,256]{1,0:T(8,128)(2,1)S(1)} %pad_maximum_fusion.5), channel_id=1, source_target_pairs={{0,2},{1,3},{2,0},{3,1},{4,6},{5,7},{6,4},{7,5},{8,10},{9,11},{10,... | collective-permute-start | bytes 1179656 | tf_op jit(solution)/shard_map/ppermute | solution.py:620
  424.7 14.7 %collective-permute-start.22 = (bf16[768,256]{1,0:T(8,128)(2,1)S(1)}, bf16[768,256]{1,0:T(8,128)(2,1)S(1)}, u32[]{:S(2)}, u32[]{:S(2)}) collective-permute-start(bf16[768,256]{1,0:T(8,128)(2,1)S(1)} %pad_maximum_fusion.6), channel_id=1, source_target_pairs={{0,4},{1,5},{2,6},{3,7},{4,0},{5,1},{6,2},{7,3},{8,12},{9,13},{10,... | collective-permute-start | bytes 1179656 | tf_op jit(solution)/shard_map/ppermute | solution.py:620
  428.4 11.5 %collective-permute-start.23 = (bf16[768,256]{1,0:T(8,128)(2,1)S(1)}, bf16[768,256]{1,0:T(8,128)(2,1)S(1)}, u32[]{:S(2)}, u32[]{:S(2)}) collective-permute-start(bf16[768,256]{1,0:T(8,128)(2,1)S(1)} %get-tuple-element.185), channel_id=1, source_target_pairs={{0,8},{1,9},{2,10},{3,11},{4,12},{5,13},{6,14},{7,15},{8,0},{9,1},... | collective-permute-start | bytes 1179656 | tf_op jit(solution)/shard_map/ppermute | solution.py:620
  430.9 13.3 %collective-permute-start.45 = (bf16[768,256]{1,0:T(8,128)(2,1)S(1)}, bf16[768,256]{1,0:T(8,128)(2,1)S(1)}, u32[]{:S(2)}, u32[]{:S(2)}) collective-permute-start(bf16[768,256]{1,0:T(8,128)(2,1)S(1)} %pad_maximum_fusion.16), channel_id=1, source_target_pairs={{0,4},{1,5},{2,6},{3,7},{4,0},{5,1},{6,2},{7,3},{8,12},{9,13},{10,... | collective-permute-start | bytes 1179656 | tf_op jit(solution)/shard_map/ppermute | solution.py:620
  430.9 17.7 %collective-permute-start.44 = (bf16[768,256]{1,0:T(8,128)(2,1)S(1)}, bf16[768,256]{1,0:T(8,128)(2,1)}, u32[]{:S(2)}, u32[]{:S(2)}) collective-permute-start(bf16[768,256]{1,0:T(8,128)(2,1)S(1)} %pad_maximum_fusion.15), channel_id=1, source_target_pairs={{0,2},{1,3},{2,0},{3,1},{4,6},{5,7},{6,4},{7,5},{8,10},{9,11},{10,... | collective-permute-start | bytes 1179656 | tf_op jit(solution)/shard_map/ppermute | solution.py:620
  436.8 27.9 %collective-permute-start.26 = (bf16[768,256]{1,0:T(8,128)(2,1)S(1)}, bf16[768,256]{1,0:T(8,128)(2,1)}, u32[]{:S(2)}, u32[]{:S(2)}) collective-permute-start(bf16[768,256]{1,0:T(8,128)(2,1)S(1)} %pad_maximum_fusion.8), channel_id=1, source_target_pairs={{0,4},{1,5},{2,6},{3,7},{4,0},{5,1},{6,2},{7,3},{8,12},{9,13},{10,... | collective-permute-start | bytes 1179656 | tf_op jit(solution)/shard_map/ppermute | solution.py:620
  439.3 25.3 %collective-permute-start.25 = (bf16[768,256]{1,0:T(8,128)(2,1)S(1)}, bf16[768,256]{1,0:T(8,128)(2,1)}, u32[]{:S(2)}, u32[]{:S(2)}) collective-permute-start(bf16[768,256]{1,0:T(8,128)(2,1)S(1)} %pad_maximum_fusion.7), channel_id=1, source_target_pairs={{0,2},{1,3},{2,0},{3,1},{4,6},{5,7},{6,4},{7,5},{8,10},{9,11},{10,... | collective-permute-start | bytes 1179656 | tf_op jit(solution)/shard_map/ppermute | solution.py:620
  439.8 23.1 %collective-permute-start.43 = (bf16[768,256]{1,0:T(8,128)(2,1)S(1)}, bf16[768,256]{1,0:T(8,128)(2,1)}, u32[]{:S(2)}, u32[]{:S(2)}) collective-permute-start(bf16[768,256]{1,0:T(8,128)(2,1)S(1)} %fusion.7), channel_id=1, source_target_pairs={{0,16},{1,17},{2,18},{3,19},{4,20},{5,21},{6,22},{7,23},{8,24},{9,... | collective-permute-start | bytes 1179656 | tf_op jit(solution)/shard_map/ppermute | solution.py:620
  444.2 22.9 %collective-permute-start.24 = (bf16[768,256]{1,0:T(8,128)(2,1)S(1)}, bf16[768,256]{1,0:T(8,128)(2,1)}, u32[]{:S(2)}, u32[]{:S(2)}) collective-permute-start(bf16[768,256]{1,0:T(8,128)(2,1)S(1)} %fusion.15), channel_id=1, source_target_pairs={{0,16},{1,17},{2,18},{3,19},{4,20},{5,21},{6,22},{7,23},{8,24},{9,... | collective-permute-start | bytes 1179656 | tf_op jit(solution)/shard_map/ppermute | solution.py:620
  445.8 27.5 %all-to-all-start.2 = ((f32[32,1,1604]{2,1,0:T(1,128)}), f32[32,1,1604]{2,1,0:T(1,128)S(1)}, u32[]{:S(2)}, u32[]{:S(2)}) async-start(f32[32,1,1604]{2,1,0:T(1,128)} %reshape.341), calls=%async_computation.2 | async-start | bytes 425984 | tf_op jit(solution)/shard_map/all_to_all | solution.py:807
  (38 other events, 248.5 us)
Sparse Core Ops, SparseCore 0:
  11.5 157.7 all-gather.1
